TPU v7x, 128 devices: a whole 4x4x4 slice. The times are simulated.
128 devices in a mesh: layer: 16 (over y, z), latent: 8 (over x, core).
Axes of the slice: x: 4, y: 4, z: 4, core: 2. Of those that a mesh axis runs over, the one named last changes fastest.
Arguments:
- acts: bfloat16 [1280, 16, 4096], P(None, 'layer'), may hold values from -16 to 16
- active: int32 [1280, 1024], P(None, 'latent'), may hold values 0 or 1
- w_enc: bfloat16 [16, 4096, 1024], P('layer', None, 'latent'), may hold values from -6 to 6
- m_enc: bfloat16 [16, 4096, 1024], P('layer', None, 'latent'), may hold values from -4 to 4
- v_enc: bfloat16 [16, 4096, 1024], P('layer', None, 'latent'), may hold values from 0.0099487305 to 1
- w_dec: bfloat16 [1024, 16, 4096], P('latent', 'layer'), may hold values from -4 to 4
- m_dec: bfloat16 [1024, 16, 4096], P('latent', 'layer'), may hold values from -0.4375 to 0.4375
- v_dec: bfloat16 [1024, 16, 4096], P('latent', 'layer'), may hold values from 9.9658966e-05 to 0.0099487305
Outputs:
- w_enc_new: bfloat16 [16, 4096, 1024], P('layer', None, 'latent')
- m_enc_new: bfloat16 [16, 4096, 1024], P('layer', None, 'latent')
- v_enc_new: bfloat16 [16, 4096, 1024], P('layer', None, 'latent')
- w_dec_new: bfloat16 [1024, 16, 4096], P('latent', 'layer')
- m_dec_new: bfloat16 [1024, 16, 4096], P('latent', 'layer')
- v_dec_new: bfloat16 [1024, 16, 4096], P('latent', 'layer')
All inputs are finite; a program needn't handle non-finite values. No bound on the sum of `active` on one device may be relied on, other than what follows from the above.
Results may differ from a plain program's by a relative error of at most 0.02.
Values may be sent and summed in bfloat16 or wider, within the bound.
No kernel may reach another device: no remote copies, remote signals or barrier semaphores. Data moves between devices by JAX's collectives and lax.ppermute only.
A program may use at most 128 MiB of HBM per device.

v0:
```python
import jax
import jax.numpy as jnp
from jax import lax
from jax.sharding import PartitionSpec as P

D = 4096
LAT = 1024


def adam_step(weights, gradient, moment_one, moment_two):
    grad_value = gradient.astype(jnp.float32)
    one_new = 0.9 * moment_one.astype(jnp.float32) + 0.1 * grad_value
    two_new = 0.999 * moment_two.astype(jnp.float32) + 0.001 * grad_value * grad_value
    stepped = weights.astype(jnp.float32) - 0.05 * one_new / (jnp.sqrt(two_new) + 1e-08)
    return (stepped, one_new, two_new)


def local(acts, active, w_enc, m_enc, v_enc, w_dec, m_dec, v_dec):
    layers = lax.axis_size("layer") * w_enc.shape[0]
    enc_scale = (layers * D) ** (-0.5)
    dec_scale = LAT ** (-0.5)
    local_acts = acts[:, 0, :]
    preact = jnp.dot(local_acts, w_enc[0], preferred_element_type=jnp.float32) * enc_scale
    preact = lax.psum(preact, "layer")
    alive_mask = active.astype(jnp.float32)
    latent_codes = (alive_mask * jax.nn.softplus(preact)).astype(jnp.bfloat16)
    decoder_cols = lax.all_to_all(w_dec, "latent", split_axis=2, concat_axis=0, tiled=True)[:, 0, :]
    all_codes = lax.all_gather(latent_codes, "latent", axis=1, tiled=True)
    slice_width = decoder_cols.shape[1]
    own_acts = lax.dynamic_slice_in_dim(
        local_acts, lax.axis_index("latent") * slice_width, slice_width, 1
    )
    rebuilt = jnp.dot(all_codes, decoder_cols, preferred_element_type=jnp.float32) * dec_scale
    residue = (rebuilt - own_acts.astype(jnp.float32)).astype(jnp.bfloat16)
    grad_cols = (
        lax.dot_general(
            all_codes, residue, (((0,), (0,)), ((), ())), preferred_element_type=jnp.float32
        )
        * dec_scale
    ).astype(jnp.bfloat16)
    grad_dec = lax.all_to_all(
        grad_cols[:, None, :], "latent", split_axis=0, concat_axis=2, tiled=True
    )
    grad_codes = lax.psum_scatter(
        (
            lax.dot_general(
                decoder_cols, residue, (((1,), (1,)), ((), ())), preferred_element_type=jnp.float32
            )
            * dec_scale
        ).astype(jnp.bfloat16),
        "latent",
        scatter_dimension=0,
        tiled=True,
    ).astype(jnp.float32)
    grad_codes = lax.psum(grad_codes.astype(jnp.bfloat16), "layer").astype(jnp.float32)
    grad_pre = (grad_codes.T * alive_mask * jax.nn.sigmoid(preact)).astype(jnp.bfloat16)
    grad_enc = (
        lax.dot_general(
            local_acts, grad_pre, (((0,), (0,)), ((), ())), preferred_element_type=jnp.float32
        )
        * enc_scale
    ).astype(jnp.bfloat16)
    stepped_enc, one_enc, two_enc = adam_step(w_enc[0], grad_enc, m_enc[0], v_enc[0])
    stepped_dec, one_dec, two_dec = adam_step(w_dec, grad_dec, m_dec, v_dec)
    layer_rms = jnp.sqrt(jnp.mean(stepped_dec * stepped_dec, axis=2) + 1e-06)[:, 0]
    latent_scale = lax.psum(layer_rms, "layer") / layers
    w_dec_new = (stepped_dec / latent_scale[:, None, None]).astype(jnp.bfloat16)
    m_dec_new = one_dec.astype(jnp.bfloat16)
    v_dec_new = two_dec.astype(jnp.bfloat16)
    w_enc_new = (stepped_enc * latent_scale[None, :]).astype(jnp.bfloat16)[None]
    return (
        w_enc_new,
        one_enc.astype(jnp.bfloat16)[None],
        two_enc.astype(jnp.bfloat16)[None],
        w_dec_new,
        m_dec_new,
        v_dec_new,
    )


def solution(mesh):
    return jax.shard_map(
        local,
        mesh=mesh,
        in_specs=(
            P(None, "layer", None),
            P(None, "latent"),
            P("layer", None, "latent"),
            P("layer", None, "latent"),
            P("layer", None, "latent"),
            P("latent", "layer", None),
            P("latent", "layer", None),
            P("latent", "layer", None),
        ),
        out_specs=(
            P("layer", None, "latent"),
            P("layer", None, "latent"),
            P("layer", None, "latent"),
            P("latent", "layer", None),
            P("latent", "layer", None),
            P("latent", "layer", None),
        ),
        check_vma=False,
    )
```

profile of v0, /device:TPU:0, one launch (start us, length us, event | category | flops | bytes accessed | tf_op | source)
XLA Modules:
  0.0 360.0 jit_solution(17131364635191658213)
XLA Ops:
  7.2 0.0 copy-start.5
  7.2 0.0 all-reduce.3.cloned.1.call-start
  7.2 8.0 %fusion.19 = f32[1280,128]{1,0:T(8,128)} fusion(bf16[1280,1,4096]{2,0,1:T(8,128)(2,1)} %param.8, bf16[1,4096,128]{2,1,0:T(8,128)(2,1)} %param.10), kind=kOutput, calls=%fused_computation.15 | convolution fusion | flops 1342341120 | bytes 12189696 | tf_op jit(solution)/shard_map/dot_general | solution.py:23
  15.3 0.0 all-reduce.3.cloned.1.call-update
  15.3 0.0 all-gather.2.cloned.1.call-start
  15.3 87.9 %all-reduce.3.cloned.1.call-done = f32[1280,128]{1,0:T(8,128)} async-done(((f32[1280,128]{1,0:T(8,128)}), f32[1280,128]{1,0:T(8,128)}) %all-reduce.3.cloned.1.call-update) | async-done | bytes 655376 | tf_op jit(solution)/shard_map/psum | solution.py:24
  103.3 2.2 fusion.34
  105.5 0.0 all-gather.2.cloned.1.call-update
  105.5 2.8 copy.39
  108.3 0.5 broadcast.45
  108.9 23.4 %reduce.1 = bf16[4096,128]{1,0:T(8,128)(2,1)} reduce(bf16[4096,1,128]{2,1,0:T(2,128)(2,1)S(1)} %bitcast.84, bf16[]{:T(256)} %broadcast.45), dimensions={1}, to_apply=%bitcast.71.reduce_sub_computation | reduce | bytes 2097154
  132.2 2.2 reshape.70
  134.4 4.2 %all-to-all-start = ((bf16[8,2,32768]{2,1,0:T(2,128)(2,1)}), bf16[8,2,32768]{2,1,0:T(2,128)(2,1)}, u32[]{:S(2)}, u32[]{:S(2)}) async-start(bf16[8,2,32768]{2,1,0:T(2,128)(2,1)} %reshape.70), calls=%async_computation | async-start | bytes 2097152 | tf_op jit(solution)/shard_map/all_to_all | solution.py:27
  138.6 0.2 reduce-scatter.4.cloned.1.call-start
  138.9 15.8 %all-to-all-done = bf16[8,2,32768]{2,1,0:T(2,128)(2,1)} async-done(((bf16[8,2,32768]{2,1,0:T(2,128)(2,1)}), bf16[8,2,32768]{2,1,0:T(2,128)(2,1)}, u32[]{:S(2)}, u32[]{:S(2)}) %all-to-all-start) | async-done | bytes 1048608 | tf_op jit(solution)/shard_map/all_to_all | solution.py:27
  154.7 4.3 %reshape.71 = bf16[4096,1,128]{2,1,0:T(2,128)(2,1)S(1)} reshape(bf16[8,2,32768]{2,1,0:T(2,128)(2,1)} %all-to-all-done) | data formatting | bytes 2097152
  159.0 1.1 copy.49
  160.1 1.5 copy.40
  161.6 0.0 all-gather.2.cloned.1.call-done
  161.6 3.7 %fusion.18 = bf16[1280,512]{1,0:T(8,128)(2,1)S(1)} fusion(bf16[1280,1024]{1,0:T(8,128)(2,1)} %all-gather.2.cloned.1.call-done, bf16[1024,512]{1,0:T(8,128)(2,1)S(1)} %bitcast.88, bf16[1280,1,4096]{2,0,1:T(8,128)(2,1)} %param.8, s32[]{:T(128)S(6)} %select_n.8), kind=kOutput, calls=%fused_computation.14 | convolution fusion | flops 1344798720 | bytes 6291460 | tf_op jit(solution)/shard_map/dot_general | solution.py:33
  165.3 1.2 copy-done.6
  166.5 3.1 fusion.17
  169.5 4.4 %copy.47 = bf16[1024,1280]{1,0:T(8,128)(2,1)} copy(bf16[1024,1280]{0,1:T(8,128)(2,1)} %fusion.17) | data formatting | bytes 5242880
  173.9 0.0 reduce-scatter.4.cloned.1.call-update
  173.9 3.7 %fusion.24 = bf16[1024,1,512]{2,0,1:T(8,128)(2,1)S(1)} fusion(bf16[1280,1024]{1,0:T(8,128)(2,1)} %all-gather.2.cloned.1.call-done, bf16[1280,512]{1,0:T(8,128)(2,1)} %copy-done.6), kind=kOutput, calls=%fused_computation.27 | convolution fusion | flops 1343225856 | bytes 4980736 | tf_op jit(solution)/shard_map/dot_general | solution.py:36
  177.6 1.5 reduce.2
  179.1 1.6 reshape.72
  180.6 4.4 %all-to-all-start.1 = ((bf16[8,2,32768]{2,1,0:T(2,128)(2,1)}), bf16[8,2,32768]{2,1,0:T(2,128)(2,1)}, u32[]{:S(2)}, u32[]{:S(2)}) async-start(bf16[8,2,32768]{2,1,0:T(2,128)(2,1)} %reshape.72), calls=%async_computation.1 | async-start | bytes 2097152 | tf_op jit(solution)/shard_map/all_to_all | solution.py:41
  185.0 0.3 all-reduce.5.cloned.1.call-start
  185.3 1.3 copy.37
  186.6 1.3 copy.38
  187.9 1.3 copy.41
  189.2 17.6 %all-to-all-done.1 = bf16[8,2,32768]{2,1,0:T(2,128)(2,1)} async-done(((bf16[8,2,32768]{2,1,0:T(2,128)(2,1)}), bf16[8,2,32768]{2,1,0:T(2,128)(2,1)}, u32[]{:S(2)}, u32[]{:S(2)}) %all-to-all-start.1) | async-done | bytes 1048608 | tf_op jit(solution)/shard_map/all_to_all | solution.py:41
  206.8 4.3 %reshape.73 = bf16[1024,1,512]{2,1,0:T(2,128)(2,1)S(1)} reshape(bf16[8,2,32768]{2,1,0:T(2,128)(2,1)} %all-to-all-done.1) | data formatting | bytes 2097152
  211.1 2.2 convert_bitcast_fusion
  213.3 1.2 copy.43
  214.5 1.5 reshape.66
  216.1 5.2 %multiply_reduce_fusion = (f32[128]{0:T(128)S(1)}, f32[128,1,4096]{2,0,1:T(8,128)S(1)}, bf16[128,1,4096]{2,0,1:T(8,128)(2,1)}, bf16[128,1,4096]{2,0,1:T(8,128)(2,1)}) fusion(f32[128,1,4096]{2,0,1:T(8,128)} %reshape.66, bf16[128,1,4096]{2,0,1:T(8,128)(2,1)} %param.15, bf16[128,1,4096]{2,0,1:T(8,128)(2,1)} %param.14, bf16[128,1,4096]{2,0,1:T(8,128)(2,1)S(1)} %copy-done), kind=kLoop, calls=%fused_computation.22 | loop fusion | flops 9437056 | bytes 9437696 | tf_op jit(solution)/shard_map/reduce_sum | solution.py:65
  221.2 38.3 %psum.23 = f32[128]{0:T(128)S(1)} all-reduce(f32[128]{0:T(128)S(1)} %add_sqrt_fusion), channel_id=1, replica_groups=mesh['layer'=16,'latent'=8] {'layer'}, use_global_device_ids=true, to_apply=%region_4.5 | all-reduce | flops 128 | bytes 1024 | tf_op jit(solution)/shard_map/psum | solution.py:66
  259.6 0.0 reduce-scatter.4.cloned.1.call-done
  259.6 1.9 copy.48
  261.5 0.0 all-reduce.5.cloned.1.call-update
  261.5 1.2 divide_convert_fusion
  262.7 76.7 %all-reduce.5.cloned.1.call-done = bf16[1280,128]{1,0:T(8,128)(2,1)} async-done(((bf16[1280,128]{1,0:T(8,128)(2,1)}), bf16[1280,128]{1,0:T(8,128)(2,1)}) %all-reduce.5.cloned.1.call-update) | async-done | bytes 327696 | tf_op jit(solution)/shard_map/psum | solution.py:55
  339.4 9.2 %fusion.29 = (bf16[1,4096,128]{1,2,0:T(8,128)(2,1)S(1)}, bf16[1,4096,128]{1,2,0:T(8,128)(2,1)}, bf16[1,4096,128]{1,2,0:T(8,128)(2,1)S(1)}) fusion(bf16[1,4096,128]{1,2,0:T(8,128)(2,1)} %copy.41, f32[128]{0:T(128)S(1)} %broadcast_multiply_fusion, bf16[1,4096,128]{1,2,0:T(8,128)(2,1)} %copy.38, bf16[1,4096,128]{1,2,0:T(8,128)(2,1)S(1)} %copy-done.4, ...), kind=kOutput, calls=%fused_computation.32 | convolution fusion | flops 1354498048 | bytes 18416128 | tf_op jit(solution)/shard_map/dot_general | solution.py:58
  348.6 2.3 copy.44
  350.9 1.3 copy.45
  352.2 1.3 copy.46
  (14 shorter events, 0.0 us)
Async XLA Ops:
  7.2 96.1 %copy-start.5 = (s32[1280,128]{1,0:T(8,128)S(1)}, s32[1280,128]{1,0:T(8,128)}, u32[]{:S(2)}) copy-start(s32[1280,128]{1,0:T(8,128)} %param.9) | copy-start | bytes 1966084
  7.2 96.1 %all-reduce.3.cloned.1.call-start = ((), (), s32[]{:S(2)}) async-start(), calls=%async_computation.3 | async-start | bytes 1310720 | tf_op jit(solution)/shard_map/psum | solution.py:24
  15.3 90.2 %copy-start = (bf16[128,1,4096]{2,0,1:T(8,128)(2,1)S(1)}, bf16[128,1,4096]{2,0,1:T(8,128)(2,1)}, u32[]{:S(2)}) copy-start(bf16[128,1,4096]{2,0,1:T(8,128)(2,1)} %param.13) | copy-start | bytes 3145732
  15.3 146.3 %all-gather.2.cloned.1.call-start = ((), (), s32[]{:S(2)}) async-start(), calls=%async_computation.4 | async-start | bytes 2949120 | tf_op jit(solution)/shard_map/all_gather | solution.py:28
  134.4 20.3 %all-to-all-start = ((bf16[8,2,32768]{2,1,0:T(2,128)(2,1)}), bf16[8,2,32768]{2,1,0:T(2,128)(2,1)}, u32[]{:S(2)}, u32[]{:S(2)}) async-start(bf16[8,2,32768]{2,1,0:T(2,128)(2,1)} %reshape.70), calls=%async_computation | async-start | bytes 2097152 | tf_op jit(solution)/shard_map/all_to_all | solution.py:27
  138.6 120.9 %reduce-scatter.4.cloned.1.call-start = ((), (), s32[]{:S(2)}) async-start(), calls=%async_computation.6 | async-start | bytes 2949120
  165.3 1.2 copy-start.6
  179.1 6.3 %copy-start.1 = (bf16[1,4096,128]{2,1,0:T(8,128)(2,1)S(1)}, bf16[1,4096,128]{2,1,0:T(8,128)(2,1)}, u32[]{:S(2)}) copy-start(bf16[1,4096,128]{2,1,0:T(8,128)(2,1)} %param.10) | copy-start | bytes 3145732
  180.6 6.0 %copy-start.2 = (bf16[1,4096,128]{2,1,0:T(8,128)(2,1)S(1)}, bf16[1,4096,128]{2,1,0:T(8,128)(2,1)}, u32[]{:S(2)}) copy-start(bf16[1,4096,128]{2,1,0:T(8,128)(2,1)} %param.11) | copy-start | bytes 3145732
  180.6 26.2 %all-to-all-start.1 = ((bf16[8,2,32768]{2,1,0:T(2,128)(2,1)}), bf16[8,2,32768]{2,1,0:T(2,128)(2,1)}, u32[]{:S(2)}, u32[]{:S(2)}) async-start(bf16[8,2,32768]{2,1,0:T(2,128)(2,1)} %reshape.72), calls=%async_computation.1 | async-start | bytes 2097152 | tf_op jit(solution)/shard_map/all_to_all | solution.py:41
  185.0 154.4 %all-reduce.5.cloned.1.call-start = ((), (), s32[]{:S(2)}) async-start(), calls=%async_computation.5 | async-start | bytes 655360 | tf_op jit(solution)/shard_map/psum | solution.py:55
  186.6 1.3 copy-start.3
  221.2 118.2 %copy-start.4 = (bf16[1,4096,128]{1,2,0:T(8,128)(2,1)S(1)}, bf16[1,4096,128]{1,2,0:T(8,128)(2,1)}, u32[]{:S(2)}) copy-start(bf16[1,4096,128]{1,2,0:T(8,128)(2,1)} %copy.37) | copy-start | bytes 3145732
Sparse Core Ops, SparseCore 0:
  15.4 87.7 all-reduce.2
  105.6 28.5 all-gather.1
  174.1 38.0 reduce-scatter.3
  261.6 77.7 all-reduce.4
where the time goes:
time: 361 us; the launch traced here: 360 us
  waiting for transfers between devices  198 us (55%)
  blocking collectives  38.3 us (11%)
  local copies, waits for them, and re-layouts  37.3 us (10%)
  other arithmetic  35.6 us (10%)
  matrix products  27.6 us (8%)
  between operations  13.9 us (4%)
  starting transfers between devices  9.2 us (3%)
    psum x1, waiting for transfers between devices, local(): preact = lax.psum(preact, 'layer')  87.9 us
    psum x1, waiting for transfers between devices, local(): lax.psum(grad_codes.astype(jnp.bfloat16), 'layer').astype(jnp.float32)  76.7 us
    psum x1, blocking collectives, local(): latent_scale = lax.psum(layer_rms, 'layer') / layers  38.3 us
    unnamed x29, local copies, waits for them, and re-layouts  33 us
    unnamed x1, other arithmetic  23.4 us
    all_to_all x1, waiting for transfers between devices, local(): lax.all_to_all(grad_cols[:, None, :], 'latent', split_axis=0, concat_axis...  17.6 us
    all_to_all x1, waiting for transfers between devices, local(): lax.all_to_all(w_dec, 'latent', split_axis=2, concat_axis=0, tiled=True)  15.8 us
    dot_general x1, matrix products, local(): lax.dot_general(local_acts, grad_pre, (((0,), (0,)), ((), ())), preferred...  9.2 us
  transfers between devices with their start and end apart: 6, of which 4 were waited for; matrix products, arithmetic and copies ran while one was open for 17% of the time, Pallas kernels for 0%

commit v1 on v0

v1 whole, which is shorter than its diff:
```python
import functools

import jax
import jax.numpy as jnp
from jax import lax
from jax.experimental import pallas as pl
from jax.experimental.pallas import tpu as pltpu
from jax.sharding import Mesh
from jax.sharding import PartitionSpec as P

D = 4096
LAT = 1024
TOKENS = 1280
LAYERS = 16
NX = 4
HALF = TOKENS // 2
SHARD = HALF // LAYERS
OWN = 128
WIDE = D // NX
ENC_SCALE = (LAYERS * D) ** (-0.5)
DEC_SCALE = LAT ** (-0.5)
MESSAGE = 48

bf16 = jnp.bfloat16
f32 = jnp.float32


def params(mib=48):
    return pltpu.CompilerParams(vmem_limit_bytes=mib * 1024 * 1024)


def cost(flops, nbytes):
    return pl.CostEstimate(flops=flops, bytes_accessed=nbytes, transcendentals=0)


def adam_step(weights, gradient, moment_one, moment_two):
    one_new = 0.9 * moment_one + 0.1 * gradient
    two_new = 0.999 * moment_two + 0.001 * gradient * gradient
    stepped = weights - 0.05 * one_new / (jnp.sqrt(two_new) + 1e-08)
    return (stepped, one_new, two_new)


def preact_kernel(acts_ref, w_ref, out_ref):
    share = jnp.dot(acts_ref[...], w_ref[...], preferred_element_type=f32)
    out_ref[...] = (share * ENC_SCALE).astype(out_ref.dtype)


def preact_share(acts, w_enc):
    rows = 256
    return pl.pallas_call(
        preact_kernel,
        grid=(TOKENS // rows,),
        in_specs=[
            pl.BlockSpec((rows, D), lambda i: (i, 0)),
            pl.BlockSpec((D, OWN), lambda i: (0, 0)),
        ],
        out_specs=pl.BlockSpec((rows, OWN), lambda i: (i, 0)),
        out_shape=jax.ShapeDtypeStruct((TOKENS, OWN), bf16),
        compiler_params=params(),
        cost_estimate=cost(2 * TOKENS * D * OWN, 2 * TOKENS * D),
        name="preact_share",
    )(acts, w_enc)


def codes_kernel(core_ref, got_ref, alive_ref, codes_ref, slope_ref):
    core = core_ref[0]
    for rel in range(2):
        src = core if rel == 0 else 1 - core
        preact = jnp.sum(got_ref[src].astype(f32), axis=0)
        alive = alive_ref[rel].astype(f32)
        code = (alive * jax.nn.softplus(preact)).astype(bf16)
        codes_ref[:, rel] = jnp.broadcast_to(code[None], (NX * LAYERS, SHARD, OWN))
        slope_ref[rel] = alive * jax.nn.sigmoid(preact)


def make_codes(core, got, alive):
    return pl.pallas_call(
        codes_kernel,
        in_specs=[
            pl.BlockSpec(memory_space=pltpu.SMEM),
            pl.BlockSpec(memory_space=pltpu.VMEM),
            pl.BlockSpec(memory_space=pltpu.VMEM),
        ],
        out_specs=[pl.BlockSpec(memory_space=pltpu.VMEM)] * 2,
        out_shape=[
            jax.ShapeDtypeStruct((NX * LAYERS, 2, SHARD, OWN), bf16),
            jax.ShapeDtypeStruct((2, SHARD, OWN), f32),
        ],
        compiler_params=params(16),
        cost_estimate=cost(1000000, 2000000),
        name="make_codes",
    )(core, got, alive)


def residue_kernel(place_ref, codes_ref, own_ref, other_ref, acts_ref, share_ref, keep_ref, send_ref, flat, cols, wide):
    del place_ref
    weights = (own_ref, other_ref)
    for x in range(NX):
        for rel in range(2):
            part = codes_ref[x * LAYERS:(x + 1) * LAYERS, rel].astype(f32)
            flat[:, (2 * x + rel) * OWN:(2 * x + rel + 1) * OWN] = part.reshape(HALF, OWN).astype(bf16)
            cols[(2 * x + rel) * OWN:(2 * x + rel + 1) * OWN, :] = weights[rel][x]
    rows = 160
    for r in range(HALF // rows):
        rebuilt = jnp.dot(flat[r * rows:(r + 1) * rows, :], cols[...], preferred_element_type=f32) * DEC_SCALE
        wide[r * rows:(r + 1) * rows, :] = (rebuilt - acts_ref[r * rows:(r + 1) * rows, :].astype(f32)).astype(bf16)
    for x in range(NX):
        grad = lax.dot_general(
            wide[...], cols[2 * x * OWN:(2 * x + 2) * OWN, :], (((1,), (1,)), ((), ())), preferred_element_type=f32
        ) * DEC_SCALE
        for rel in range(2):
            share_ref[x * LAYERS:(x + 1) * LAYERS, rel] = (
                grad[:, rel * OWN:(rel + 1) * OWN].reshape(LAYERS, SHARD, OWN).astype(bf16)
            )
    for x in range(NX):
        grad = lax.dot_general(
            flat[:, 2 * x * OWN:(2 * x + 2) * OWN], wide[...], (((0,), (0,)), ((), ())), preferred_element_type=f32
        ) * DEC_SCALE
        keep_ref[x] = grad[:OWN]
        send_ref[x] = grad[OWN:].astype(bf16)


def residue_part(place, codes, own, other, acts):
    whole = lambda *dims: pl.BlockSpec(dims, lambda i, p: (0,) * len(dims))
    return pl.pallas_call(
        residue_kernel,
        grid_spec=pltpu.PrefetchScalarGridSpec(
            num_scalar_prefetch=1,
            grid=(1,),
            in_specs=[
                whole(NX * LAYERS, 2, SHARD, OWN),
                whole(NX, OWN, WIDE),
                whole(NX, OWN, WIDE),
                pl.BlockSpec((HALF, WIDE), lambda i, p: (p[0], p[1])),
            ],
            out_specs=[whole(NX * LAYERS, 2, SHARD, OWN), whole(NX, OWN, WIDE), whole(NX, OWN, WIDE)],
            scratch_shapes=[
                pltpu.VMEM((HALF, LAT), bf16),
                pltpu.VMEM((LAT, WIDE), bf16),
                pltpu.VMEM((HALF, WIDE), bf16),
            ],
        ),
        out_shape=[
            jax.ShapeDtypeStruct((NX * LAYERS, 2, SHARD, OWN), bf16),
            jax.ShapeDtypeStruct((NX, OWN, WIDE), f32),
            jax.ShapeDtypeStruct((NX, OWN, WIDE), bf16),
        ],
        compiler_params=params(),
        cost_estimate=cost(6 * HALF * LAT * WIDE, 10000000),
        name="residue_part",
    )(place, codes, own, other, acts)


def join_kernel(keep_ref, got_ref, out_ref):
    out_ref[...] = (keep_ref[...] + got_ref[...].astype(f32)).astype(bf16)


def join_halves(keep, got):
    block = pl.BlockSpec((1, OWN, WIDE), lambda i: (i, 0, 0))
    return pl.pallas_call(
        join_kernel,
        grid=(NX,),
        in_specs=[block, block],
        out_specs=block,
        out_shape=jax.ShapeDtypeStruct((NX, OWN, WIDE), bf16),
        compiler_params=params(16),
        cost_estimate=cost(1000000, 4000000),
        name="join_halves",
    )(keep, got)


def decoder_kernel(grad_ref, w_ref, m_ref, v_ref, m_out, v_out, stepped_out, rms_out, total):
    step = pl.program_id(0)

    @pl.when(step == 0)
    def _():
        total[...] = jnp.zeros_like(total)

    stepped, one, two = adam_step(
        w_ref[...].astype(f32), grad_ref[0].astype(f32), m_ref[...].astype(f32), v_ref[...].astype(f32)
    )
    m_out[...] = one.astype(bf16)
    v_out[...] = two.astype(bf16)
    stepped_out[...] = stepped
    total[...] += jnp.sum(stepped * stepped, axis=1, keepdims=True)

    @pl.when(step == NX - 1)
    def _():
        rms = jnp.sqrt(total[...] * (1.0 / D) + 1e-06)
        rms_out[...] = jnp.broadcast_to(rms, (OWN, OWN)).T[:8]


def decoder_adam(grad, w, m, v):
    block = pl.BlockSpec((OWN, WIDE), lambda i: (0, i))
    return pl.pallas_call(
        decoder_kernel,
        grid=(NX,),
        in_specs=[pl.BlockSpec((1, OWN, WIDE), lambda i: (i, 0, 0)), block, block, block],
        out_specs=[block, block, block, pl.BlockSpec((8, OWN), lambda i: (0, 0))],
        out_shape=[
            jax.ShapeDtypeStruct((OWN, D), bf16),
            jax.ShapeDtypeStruct((OWN, D), bf16),
            jax.ShapeDtypeStruct((OWN, D), f32),
            jax.ShapeDtypeStruct((8, OWN), f32),
        ],
        scratch_shapes=[pltpu.VMEM((OWN, 1), f32)],
        compiler_params=params(16),
        cost_estimate=cost(20 * OWN * D, 8000000),
        name="decoder_adam",
    )(grad, w, m, v)


def grad_pre_kernel(core_ref, got_ref, slope_ref, rms_ref, out_ref):
    core = core_ref[0]
    rms = rms_ref[...]
    high = rms.astype(bf16).astype(f32)
    mid = (rms - high).astype(bf16).astype(f32)
    low = rms - high - mid
    row = lax.broadcasted_iota(jnp.int32, (8, OWN), 0)
    tail = jnp.where(row == 0, high, jnp.where(row == 1, mid, jnp.where(row == 2, low, 0.0)))
    for rel in range(2):
        grad = jnp.sum(got_ref[:, rel].astype(f32), axis=0) * slope_ref[rel]
        message = jnp.concatenate([grad, tail], axis=0).astype(bf16)
        dest = core if rel == 0 else 1 - core
        out_ref[dest] = jnp.broadcast_to(message[None], (LAYERS, MESSAGE, OWN))


def make_grad_pre(core, got, slope, rms):
    return pl.pallas_call(
        grad_pre_kernel,
        in_specs=[pl.BlockSpec(memory_space=pltpu.SMEM)] + [pl.BlockSpec(memory_space=pltpu.VMEM)] * 3,
        out_specs=pl.BlockSpec(memory_space=pltpu.VMEM),
        out_shape=jax.ShapeDtypeStruct((2, LAYERS, MESSAGE, OWN), bf16),
        compiler_params=params(16),
        cost_estimate=cost(1000000, 2000000),
        name="make_grad_pre",
    )(core, got, slope, rms)


def encoder_kernel(core_ref, got_ref, acts_ref, w_ref, m_ref, v_ref, dec_ref, w_out, m_out, v_out, dec_out, turned, scale):
    @pl.when(pl.program_id(0) == 0)
    def _():
        got = got_ref[...].astype(f32)
        grad_pre = got[:, :, :SHARD].reshape(TOKENS, OWN)
        turned[...] = grad_pre.T.astype(bf16)
        mine = got_ref[core_ref[0]].astype(f32)[:, SHARD:]
        rms = jnp.sum(mine, axis=0)
        scale[...] = jnp.sum(rms[:3], axis=0, keepdims=True) * (1.0 / LAYERS)

    grad = jnp.dot(turned[...], acts_ref[...], preferred_element_type=f32) * ENC_SCALE
    grad = grad.astype(bf16).astype(f32).T
    stepped, one, two = adam_step(w_ref[...].astype(f32), grad, m_ref[...].astype(f32), v_ref[...].astype(f32))
    latent_scale = scale[...]
    w_out[...] = (stepped * latent_scale).astype(bf16)
    m_out[...] = one.astype(bf16)
    v_out[...] = two.astype(bf16)
    column = jnp.broadcast_to(latent_scale, (OWN, OWN)).T[:, :1]
    dec_out[...] = (dec_ref[...] / column).astype(bf16)


def encoder_adam(core, got, acts, w, m, v, stepped_dec):
    width = 512
    block = pl.BlockSpec((width, OWN), lambda i: (i, 0))
    across = pl.BlockSpec((OWN, width), lambda i: (0, i))
    return pl.pallas_call(
        encoder_kernel,
        grid=(D // width,),
        in_specs=[
            pl.BlockSpec(memory_space=pltpu.SMEM),
            pl.BlockSpec((2, LAYERS, MESSAGE, OWN), lambda i: (0, 0, 0, 0)),
            pl.BlockSpec((TOKENS, width), lambda i: (0, i)),
            block,
            block,
            block,
            across,
        ],
        out_specs=[block, block, block, across],
        out_shape=[jax.ShapeDtypeStruct((D, OWN), bf16)] * 3 + [jax.ShapeDtypeStruct((OWN, D), bf16)],
        scratch_shapes=[pltpu.VMEM((OWN, TOKENS), bf16), pltpu.VMEM((1, OWN), f32)],
        compiler_params=params(),
        cost_estimate=cost(2 * TOKENS * D * OWN, 20000000),
        name="encoder_adam",
    )(core, got, acts, w, m, v, stepped_dec)


SWAP = [(0, 1), (1, 0)]
ACROSS = ("x", "y", "z")
TOKEN_AXES = ("core", "y", "z")


def exchange(array, axes):
    flat = array.reshape(-1, array.shape[-1])
    return lax.all_to_all(flat, axes, split_axis=0, concat_axis=0, tiled=True).reshape(array.shape)


def local(acts, active, w_enc, m_enc, v_enc, w_dec, m_dec, v_dec):
    core = lax.axis_index("core")
    layer = lax.axis_index(("y", "z"))
    core_array = core.astype(jnp.int32)[None]
    place = jnp.stack([core, lax.axis_index("x")]).astype(jnp.int32)
    acts = acts[:, 0, :]

    own_cols = exchange(w_dec[:, 0, :].reshape(OWN, NX, WIDE).transpose(1, 0, 2), "x")
    other_cols = lax.ppermute(own_cols, "core", SWAP)

    alive = active.astype(bf16).reshape(2, LAYERS, SHARD, OWN)
    alive = lax.dynamic_index_in_dim(alive, layer, 1, keepdims=False)
    alive_own = lax.dynamic_index_in_dim(alive, core, 0, keepdims=False)
    alive_other = lax.ppermute(lax.dynamic_index_in_dim(alive, 1 - core, 0, keepdims=False), "core", SWAP)
    alive = jnp.stack([alive_own, alive_other])

    share = preact_share(acts, w_enc[0])
    share = exchange(share.reshape(2 * LAYERS, SHARD, OWN), TOKEN_AXES)
    codes, slope = make_codes(core_array, share.reshape(2, LAYERS, SHARD, OWN), alive)
    codes = exchange(codes, ACROSS)
    grad_share, keep, send = residue_part(place, codes, own_cols, other_cols, acts)
    grad_share = exchange(grad_share, ACROSS)

    grad_dec = join_halves(keep, lax.ppermute(send, "core", SWAP))
    grad_dec = exchange(grad_dec, "x")
    m_dec_new, v_dec_new, stepped_dec, rms = decoder_adam(grad_dec, w_dec[:, 0, :], m_dec[:, 0, :], v_dec[:, 0, :])

    messages = exchange(make_grad_pre(core_array, grad_share, slope, rms), TOKEN_AXES)
    w_enc_new, m_enc_new, v_enc_new, w_dec_new = encoder_adam(
        core_array, messages, acts, w_enc[0], m_enc[0], v_enc[0], stepped_dec
    )
    return (
        w_enc_new[None],
        m_enc_new[None],
        v_enc_new[None],
        w_dec_new[:, None, :],
        m_dec_new[:, None, :],
        v_dec_new[:, None, :],
    )


def solution(mesh):
    fine = Mesh(mesh.devices.reshape(4, 4, NX, 2), ("y", "z", "x", "core"))
    layer = ("y", "z")
    latent = ("x", "core")
    return jax.shard_map(
        local,
        mesh=fine,
        in_specs=(
            P(None, layer, None),
            P(None, latent),
            P(layer, None, latent),
            P(layer, None, latent),
            P(layer, None, latent),
            P(latent, layer, None),
            P(latent, layer, None),
            P(latent, layer, None),
        ),
        out_specs=(
            P(layer, None, latent),
            P(layer, None, latent),
            P(layer, None, latent),
            P(latent, layer, None),
            P(latent, layer, None),
            P(latent, layer, None),
        ),
        check_vma=False,
    )
```

time: 361 us -> 157 us (0.43)
  waiting for transfers between devices: 198 us -> 58.6 us
  other arithmetic: 35.6 us -> 0.12 us
  Pallas kernels: 0 us -> 30 us
  matrix products: 27.6 us -> 0 us
  local copies, waits for them, and re-layouts: 37.3 us -> 12.5 us
  starting transfers between devices: 9.2 us -> 22.5 us
  between operations: 13.9 us -> 0.77 us
  blocking collectives: 38.3 us -> 31.7 us
    psum x2 -> x0, waiting for transfers between devices: 165 us -> none  [the longest x1 87.9 us: local(): preact = lax.psum(preact, 'layer')]
    psum x1 -> x0, blocking collectives: 38.3 us -> none  [local(): latent_scale = lax.psum(layer_rms, 'layer') / layers]
    all_to_all x0 -> x2, blocking collectives: none -> 31.7 us  [exchange(): lax.all_to_all(flat, axes, split_axis=0, concat_axis=0, tiled=True)]
    pallas_call x0 -> x7, Pallas kernels: none -> 30 us  [the longest x1 10.1 us: encoder_adam(): pl.pallas_call(encoder_kernel, grid=(D // width,), in_specs=[pl.BlockSpec...]
    dot_general x5 -> x0, matrix products: 27.6 us -> none  [the longest x1 9.2 us: local(): lax.dot_general(local_acts, grad_pre, (((0,), (0,)), ((), ())), preferred...]
    unnamed x1 -> x0, other arithmetic: 23.4 us -> none
    unnamed x29 -> x27, local copies, waits for them, and re-layouts: 33 us -> 11.2 us
    all_to_all x2 -> x4, waiting for transfers between devices: 33.4 us -> 54.8 us  [exchange(): lax.all_to_all(flat, axes, split_axis=0, concat_axis=0, tiled=True)]
  transfers between devices with their start and end apart: 6 -> 7, of which waited for: 4 -> 6; matrix products, arithmetic and copies ran while one was open for 17% -> 1% of each run, Pallas kernels for 0% -> 2%
where the time goes in v1:
time: 157 us; the launch traced here: 156 us
  waiting for transfers between devices  58.6 us (37%)
  blocking collectives  31.7 us (20%)
  Pallas kernels  30 us (19%)
  starting transfers between devices  22.5 us (14%)
  local copies, waits for them, and re-layouts  12.5 us (8%)
    all_to_all x4, waiting for transfers between devices, exchange(): lax.all_to_all(flat, axes, split_axis=0, concat_axis=0, tiled=True)  54.8 us
    all_to_all x2, blocking collectives, exchange(): lax.all_to_all(flat, axes, split_axis=0, concat_axis=0, tiled=True)  31.7 us
    all_to_all x4, starting transfers between devices, exchange(): lax.all_to_all(flat, axes, split_axis=0, concat_axis=0, tiled=True)  22.3 us
    unnamed x27, local copies, waits for them, and re-layouts  11.2 us
    pallas_call x1, Pallas kernels, encoder_adam(): pl.pallas_call(encoder_kernel, grid=(D // width,), in_specs=[pl.BlockSpec...  10.1 us
    pallas_call x1, Pallas kernels, residue_part(): pl.pallas_call(residue_kernel, grid_spec=pltpu.PrefetchScalarGridSpec(num...  8.06 us
    pallas_call x1, Pallas kernels, preact_share(): pl.pallas_call(preact_kernel, grid=(TOKENS // rows,), in_specs=[pl.BlockS...  7.69 us
    pallas_call x1, Pallas kernels, decoder_adam(): pl.pallas_call(decoder_kernel, grid=(NX,), in_specs=[pl.BlockSpec((1, OWN...  3.53 us
  transfers between devices with their start and end apart: 7, of which 6 were waited for; matrix products, arithmetic and copies ran while one was open for 1% of the time, Pallas kernels for 2%

profile of v1, /device:TPU:0, one launch (start us, length us, event | category | flops | bytes accessed | tf_op | source)
XLA Modules:
  0.0 156.2 jit_solution(6787098176139479600)
XLA Ops:
  0.6 0.0 copy-start
  0.6 1.2 copy-done
  1.9 7.7 %preact_share.1 = bf16[1280,128]{1,0:T(8,128)(2,1)} custom-call(bf16[1280,4096]{1,0:T(8,128)(2,1)} %bitcast.45, bf16[4096,128]{1,0:T(8,128)(2,1)S(1)} %bitcast.32), custom_call_target="tpu_custom_call" | custom-call | flops 1342177280 | bytes 10485760 | tf_op jit(solution)/shard_map/preact_share/pallas_call | solution.py:50
  9.6 8.4 %all-to-all-start = ((bf16[32,40,128]{2,1,0:T(8,128)(2,1)}), bf16[32,40,128]{2,1,0:T(8,128)(2,1)S(1)}, u32[]{:S(2)}, u32[]{:S(2)}) async-start(bf16[32,40,128]{2,1,0:T(8,128)(2,1)} %bitcast.4), calls=%async_computation | async-start | bytes 655360 | tf_op jit(solution)/shard_map/all_to_all | solution.py:293
  18.0 0.0 copy-done.2
  18.0 0.7 copy.14
  18.6 1.3 copy.15
  20.0 0.0 copy-start.12
  20.0 7.9 %all-to-all-done = bf16[32,40,128]{2,1,0:T(8,128)(2,1)S(1)} async-done(((bf16[32,40,128]{2,1,0:T(8,128)(2,1)}), bf16[32,40,128]{2,1,0:T(8,128)(2,1)S(1)}, u32[]{:S(2)}, u32[]{:S(2)}) %all-to-all-start) | async-done | bytes 327712 | tf_op jit(solution)/shard_map/all_to_all | solution.py:293
  27.9 4.3 %all-to-all-start.2 = ((bf16[4,128,1024]{2,1,0:T(8,128)(2,1)}), bf16[4,128,1024]{2,1,0:T(8,128)(2,1)S(1)}, u32[]{:S(2)}, u32[]{:S(2)}) async-start(bf16[4,128,1024]{2,1,0:T(8,128)(2,1)} %bitcast.48), calls=%async_computation.2 | async-start | bytes 2097152 | tf_op jit(solution)/shard_map/all_to_all | solution.py:293
  32.2 0.0 copy-done.12
  32.3 0.1 collective-permute-start
  32.4 1.2 collective-permute-done
  33.5 0.1 make_codes.1
  33.7 0.0 copy-start.7
  33.7 1.1 copy-done.7
  34.8 12.5 %all-to-all-done.2.own_ref = bf16[4,128,1024]{2,1,0:T(8,128)(2,1)S(1)} async-done(((bf16[4,128,1024]{2,1,0:T(8,128)(2,1)}), bf16[4,128,1024]{2,1,0:T(8,128)(2,1)S(1)}, u32[]{:S(2)}, u32[]{:S(2)}) %all-to-all-start.2) | async-done | bytes 1048608 | tf_op jit(solution)/shard_map/all_to_all | solution.py:293
  47.2 5.0 %all-to-all-start.1 = ((bf16[64,80,128]{2,1,0:T(8,128)(2,1)}), bf16[64,80,128]{2,1,0:T(8,128)(2,1)S(1)}, u32[]{:S(2)}, u32[]{:S(2)}) async-start(bf16[64,80,128]{2,1,0:T(8,128)(2,1)} %bitcast.39), calls=%async_computation.1 | async-start | bytes 2621440 | tf_op jit(solution)/shard_map/all_to_all | solution.py:293
  52.2 0.1 collective-permute-start.1
  52.3 0.1 pad_add_fusion.place_ref
  52.4 20.5 %all-to-all-done.1 = bf16[64,80,128]{2,1,0:T(8,128)(2,1)S(1)} async-done(((bf16[64,80,128]{2,1,0:T(8,128)(2,1)}), bf16[64,80,128]{2,1,0:T(8,128)(2,1)S(1)}, u32[]{:S(2)}, u32[]{:S(2)}) %all-to-all-start.1) | async-done | bytes 1310752 | tf_op jit(solution)/shard_map/all_to_all | solution.py:293
  72.8 0.0 collective-permute-done.1.other_ref
  72.8 8.1 %residue_part.1 = (bf16[64,2,40,128]{3,2,1,0:T(8,128)(2,1)S(1)}, f32[4,128,1024]{2,1,0:T(8,128)}, bf16[4,128,1024]{2,1,0:T(8,128)(2,1)S(1)}) custom-call(s32[2]{0:T(128)S(1)} %pad_add_fusion.place_ref, bf16[64,2,40,128]{3,2,1,0:T(8,128)(2,1)S(1)} %bitcast.37, bf16[4,128,1024]{2,1,0:T(8,128)(2,1)S(1)} %all-to-all-done.2.own_ref, ...), custom_call_target="tpu_custom_call" | custom-call | flops 4026531840 | bytes 10000000 | tf_op jit(solution)/shard_map/residue_part/pallas_call | solution.py:125
  80.9 0.0 copy-start.6
  80.9 0.0 collective-permute-start.2
  80.9 2.7 %collective-permute-done.2.got_ref = bf16[4,128,1024]{2,1,0:T(8,128)(2,1)S(1)} collective-permute-done((bf16[4,128,1024]{2,1,0:T(8,128)(2,1)S(1)}, bf16[4,128,1024]{2,1,0:T(8,128)(2,1)S(1)}, u32[]{:S(2)}, u32[]{:S(2)}) %collective-permute-start.2) | collective-permute-done | bytes 1048608 | tf_op jit(solution)/shard_map/ppermute | solution.py:319
  83.6 0.0 copy-start.5
  83.6 1.6 %copy-done.5 = f32[4,128,1024]{2,1,0:T(8,128)S(1)} copy-done((f32[4,128,1024]{2,1,0:T(8,128)S(1)}, f32[4,128,1024]{2,1,0:T(8,128)}, u32[]{:S(2)}) %copy-start.5) | copy-done | bytes 2097176
  85.2 0.2 join_halves.1
  85.4 0.0 copy-done.6
  85.4 18.1 %all_to_all.48.grad_ref = bf16[4,128,1024]{2,1,0:T(8,128)(2,1)S(1)} all-to-all(bf16[4,128,1024]{2,1,0:T(8,128)(2,1)S(1)} %join_halves.1), channel_id=1, replica_groups=mesh['y'=4,'z'=4,'x'=4,'core'=2] {'x'}, dimensions={0} | all-to-all | bytes 2097152 | tf_op jit(solution)/shard_map/all_to_all | solution.py:293
  103.5 4.7 %all-to-all-start.3 = ((bf16[64,80,128]{2,1,0:T(8,128)(2,1)}), bf16[64,80,128]{2,1,0:T(8,128)(2,1)S(1)}, u32[]{:S(2)}, u32[]{:S(2)}) async-start(bf16[64,80,128]{2,1,0:T(8,128)(2,1)} %bitcast.38), calls=%async_computation.3 | async-start | bytes 2621440 | tf_op jit(solution)/shard_map/all_to_all | solution.py:293
  108.2 0.0 copy-start.10
  108.2 1.2 copy-done.10
  109.4 0.0 copy-start.11
  109.4 1.2 copy-done.11
  110.6 3.5 %decoder_adam.1 = (bf16[128,4096]{1,0:T(8,128)(2,1)}, bf16[128,4096]{1,0:T(8,128)(2,1)}, f32[128,4096]{1,0:T(8,128)S(1)}, f32[8,128]{1,0:T(8,128)S(1)}) custom-call(bf16[4,128,1024]{2,1,0:T(8,128)(2,1)S(1)} %all_to_all.48.grad_ref, bf16[128,4096]{1,0:T(8,128)(2,1)S(1)} %bitcast.34, bf16[128,4096]{1,0:T(8,128)(2,1)S(1)} %bitcast.43, ...), custom_call_target="tpu_custom_call" | custom-call | flops 10485760 | bytes 8000000 | tf_op jit(solution)/shard_map/decoder_adam/pallas_call | solution.py:195
  114.2 0.0 copy-start.3
  114.2 1.3 copy-done.3
  115.5 0.0 copy-start.1
  115.5 13.9 %all-to-all-done.3 = bf16[64,80,128]{2,1,0:T(8,128)(2,1)S(1)} async-done(((bf16[64,80,128]{2,1,0:T(8,128)(2,1)}), bf16[64,80,128]{2,1,0:T(8,128)(2,1)S(1)}, u32[]{:S(2)}, u32[]{:S(2)}) %all-to-all-start.3) | async-done | bytes 1310752 | tf_op jit(solution)/shard_map/all_to_all | solution.py:293
  129.4 0.2 make_grad_pre.1
  129.6 13.6 %all_to_all.49 = bf16[32,48,128]{2,1,0:T(8,128)(2,1)S(1)} all-to-all(bf16[32,48,128]{2,1,0:T(8,128)(2,1)S(1)} %bitcast.35), channel_id=1, replica_groups=mesh['y'=4,'z'=4,'x'=4,'core'=2] {'core','y','z'}, dimensions={0} | all-to-all | bytes 786432 | tf_op jit(solution)/shard_map/all_to_all | solution.py:293
  143.2 0.0 copy-done.1
  143.2 0.0 copy-done.8
  143.2 1.6 %copy-done.4 = f32[128,4096]{1,0:T(8,128)S(1)} copy-done((f32[128,4096]{1,0:T(8,128)S(1)}, f32[128,4096]{1,0:T(8,128)}, u32[]{:S(2)}) %copy-start.4) | copy-done | bytes 2097176
  144.8 1.2 copy-done.9
  146.0 10.1 %encoder_adam.1 = (bf16[4096,128]{1,0:T(8,128)(2,1)}, bf16[4096,128]{1,0:T(8,128)(2,1)}, bf16[4096,128]{1,0:T(8,128)(2,1)}, bf16[128,4096]{1,0:T(8,128)(2,1)}) custom-call(s32[1]{0:T(128)} %bitcast.core_ref, bf16[2,16,48,128]{3,2,1,0:T(8,128)(2,1)S(1)} %bitcast.36, bf16[1280,4096]{1,0:T(8,128)(2,1)} %bitcast.47, bf16[4096,128]{1,0:T(8,128)(2,1)S(1)} %bitcast.33, ...), custom_call_target="tpu_custom_call" | custom-call | flops 1342177280 | bytes 20000000 | tf_op jit(solution)/shard_map/encoder_adam/pallas_call | solution.py:265
  (7 shorter events, 0.1 us)
Async XLA Ops:
  0.6 1.2 copy-start
  1.9 16.1 %copy-start.2 = (bf16[128,1,4096]{2,0,1:T(8,128)(2,1)S(1)}, bf16[128,1,4096]{2,0,1:T(8,128)(2,1)}, u32[]{:S(2)}) copy-start(bf16[128,1,4096]{2,0,1:T(8,128)(2,1)} %param.13) | copy-start | bytes 3145732
  9.6 18.3 %all-to-all-start = ((bf16[32,40,128]{2,1,0:T(8,128)(2,1)}), bf16[32,40,128]{2,1,0:T(8,128)(2,1)S(1)}, u32[]{:S(2)}, u32[]{:S(2)}) async-start(bf16[32,40,128]{2,1,0:T(8,128)(2,1)} %bitcast.4), calls=%async_computation | async-start | bytes 655360 | tf_op jit(solution)/shard_map/all_to_all | solution.py:293
  20.0 12.2 %copy-start.12 = (s32[1280,128]{1,0:T(8,128)S(1)}, s32[1280,128]{1,0:T(8,128)}, u32[]{:S(2)}) copy-start(s32[1280,128]{1,0:T(8,128)} %param.9) | copy-start | bytes 1966084
  27.9 19.3 %all-to-all-start.2 = ((bf16[4,128,1024]{2,1,0:T(8,128)(2,1)}), bf16[4,128,1024]{2,1,0:T(8,128)(2,1)S(1)}, u32[]{:S(2)}, u32[]{:S(2)}) async-start(bf16[4,128,1024]{2,1,0:T(8,128)(2,1)} %bitcast.48), calls=%async_computation.2 | async-start | bytes 2097152 | tf_op jit(solution)/shard_map/all_to_all | solution.py:293
  32.3 1.3 collective-permute-start
  33.7 1.1 copy-start.7
  47.2 25.6 %all-to-all-start.1 = ((bf16[64,80,128]{2,1,0:T(8,128)(2,1)}), bf16[64,80,128]{2,1,0:T(8,128)(2,1)S(1)}, u32[]{:S(2)}, u32[]{:S(2)}) async-start(bf16[64,80,128]{2,1,0:T(8,128)(2,1)} %bitcast.39), calls=%async_computation.1 | async-start | bytes 2621440 | tf_op jit(solution)/shard_map/all_to_all | solution.py:293
  52.2 20.6 %collective-permute-start.1 = (bf16[4,128,1024]{2,1,0:T(8,128)(2,1)S(1)}, bf16[4,128,1024]{2,1,0:T(8,128)(2,1)}, u32[]{:S(2)}, u32[]{:S(2)}) collective-permute-start(bf16[4,128,1024]{2,1,0:T(8,128)(2,1)S(1)} %all-to-all-done.2.own_ref), channel_id=1, source_target_pairs={{0,1},{1,0},{2,3},{3,2},{4,5},{5,4},{6,7},{7,6},{8,9},{9,8},{10,11... | collective-permute-start | bytes 3145736 | tf_op jit(solution)/shard_map/ppermute | solution.py:304
  80.9 4.5 %copy-start.6 = (bf16[64,2,40,128]{3,2,1,0:T(8,128)(2,1)}, bf16[64,2,40,128]{3,2,1,0:T(8,128)(2,1)S(1)}, u32[]{:S(2)}) copy-start(bf16[64,2,40,128]{3,2,1,0:T(8,128)(2,1)S(1)} %get-tuple-element.20) | copy-start | bytes 3932164
  80.9 2.7 %collective-permute-start.2 = (bf16[4,128,1024]{2,1,0:T(8,128)(2,1)S(1)}, bf16[4,128,1024]{2,1,0:T(8,128)(2,1)S(1)}, u32[]{:S(2)}, u32[]{:S(2)}) collective-permute-start(bf16[4,128,1024]{2,1,0:T(8,128)(2,1)S(1)} %get-tuple-element.23), channel_id=1, source_target_pairs={{0,1},{1,0},{2,3},{3,2},{4,5},{5,4},{6,7},{7,6},{8,9},{9,8},{10,11... | collective-permute-start | bytes 3145736 | tf_op jit(solution)/shard_map/ppermute | solution.py:319
  83.6 1.6 %copy-start.5 = (f32[4,128,1024]{2,1,0:T(8,128)S(1)}, f32[4,128,1024]{2,1,0:T(8,128)}, u32[]{:S(2)}) copy-start(f32[4,128,1024]{2,1,0:T(8,128)} %get-tuple-element.22.keep_ref) | copy-start | bytes 6291460
  103.5 25.9 %all-to-all-start.3 = ((bf16[64,80,128]{2,1,0:T(8,128)(2,1)}), bf16[64,80,128]{2,1,0:T(8,128)(2,1)S(1)}, u32[]{:S(2)}, u32[]{:S(2)}) async-start(bf16[64,80,128]{2,1,0:T(8,128)(2,1)} %bitcast.38), calls=%async_computation.3 | async-start | bytes 2621440 | tf_op jit(solution)/shard_map/all_to_all | solution.py:293
  108.2 1.2 copy-start.10
  109.4 1.2 copy-start.11
  114.2 1.3 copy-start.3
  115.5 27.7 %copy-start.1 = (bf16[1,4096,128]{2,1,0:T(8,128)(2,1)S(1)}, bf16[1,4096,128]{2,1,0:T(8,128)(2,1)}, u32[]{:S(2)}) copy-start(bf16[1,4096,128]{2,1,0:T(8,128)(2,1)} %param.10) | copy-start | bytes 3145732
  115.5 27.7 %copy-start.8 = (bf16[1,4096,128]{2,1,0:T(8,128)(2,1)S(1)}, bf16[1,4096,128]{2,1,0:T(8,128)(2,1)}, u32[]{:S(2)}) copy-start(bf16[1,4096,128]{2,1,0:T(8,128)(2,1)} %param.11) | copy-start | bytes 3145732
  143.2 1.6 %copy-start.4 = (f32[128,4096]{1,0:T(8,128)S(1)}, f32[128,4096]{1,0:T(8,128)}, u32[]{:S(2)}) copy-start(f32[128,4096]{1,0:T(8,128)} %copy-done.3) | copy-start | bytes 6291460
  144.8 1.2 copy-start.9

commit v2 on v1

v2 whole, which is shorter than its diff:
```python
import jax
import jax.numpy as jnp
from jax import lax
from jax.experimental import pallas as pl
from jax.experimental.pallas import tpu as pltpu
from jax.sharding import Mesh
from jax.sharding import PartitionSpec as P

D = 4096
LAT = 1024
TOKENS = 1280
LAYERS = 16
NX = 4
HALF = TOKENS // 2
SHARD = HALF // LAYERS
OWN = 128
WIDE = D // NX
ENC_SCALE = (LAYERS * D) ** (-0.5)
DEC_SCALE = LAT ** (-0.5)
MESSAGE = 48

bf16 = jnp.bfloat16
f32 = jnp.float32


def params(mib=48):
    return pltpu.CompilerParams(vmem_limit_bytes=mib * 1024 * 1024)


def cost(flops, nbytes):
    return pl.CostEstimate(flops=flops, bytes_accessed=nbytes, transcendentals=0)


def adam_step(weights, gradient, moment_one, moment_two):
    one_new = 0.9 * moment_one + 0.1 * gradient
    two_new = 0.999 * moment_two + 0.001 * gradient * gradient
    stepped = weights - 0.05 * one_new / (jnp.sqrt(two_new) + 1e-08)
    return (stepped, one_new, two_new)


CHUNKS = 8
CHUNK = TOKENS // CHUNKS


def preact_kernel(acts_ref, w_ref, dec_ref, out_ref, *rest):
    pieces, (rows, weights, dec, row_sems, weight_sem, cut_sems) = rest[:NX], rest[NX:]
    here = lax.axis_index("x")
    fetch = pltpu.make_async_copy(w_ref, weights, weight_sem)
    fetch.start()

    def block(c):
        source = acts_ref.at[pl.ds(pl.multiple_of(c * CHUNK, CHUNK), CHUNK)]
        return pltpu.make_async_copy(source, rows.at[c], row_sems.at[c])

    block(0).start()
    block(1).start()
    cuts = []
    for r in range(NX):
        start = pl.multiple_of(lax.rem(here + r, NX) * WIDE, WIDE)
        cuts.append((
            pltpu.make_async_copy(dec_ref.at[:, pl.ds(start, WIDE)], dec.at[r], cut_sems.at[0, r]),
            pltpu.make_async_copy(dec.at[r], pieces[r], cut_sems.at[1, r]),
        ))
        cuts[r][0].start()

    @pl.loop(2, CHUNKS)
    def _(c):
        block(c).start()

    def multiply(c):
        block(c).wait()
        share = jnp.dot(rows[c], weights[...], preferred_element_type=f32)
        out_ref[pl.ds(pl.multiple_of(c * CHUNK, CHUNK), CHUNK), :] = (share * ENC_SCALE).astype(out_ref.dtype)

    fetch.wait()

    @pl.loop(0, CHUNKS // 2)
    def _(c):
        multiply(c)

    for take, give in cuts:
        take.wait()
        give.start()

    @pl.loop(CHUNKS // 2, CHUNKS)
    def _(c):
        multiply(c)

    for _, give in cuts:
        give.wait()


def preact_share(acts, w_enc, w_dec):
    anywhere = pl.BlockSpec(memory_space=pl.ANY)
    return pl.pallas_call(
        preact_kernel,
        in_specs=[anywhere] * 3,
        out_specs=[pl.BlockSpec(memory_space=pltpu.VMEM)] + [anywhere] * NX,
        out_shape=[jax.ShapeDtypeStruct((TOKENS, OWN), bf16)] + [jax.ShapeDtypeStruct((OWN, WIDE), bf16)] * NX,
        scratch_shapes=[
            pltpu.VMEM((CHUNKS, CHUNK, D), bf16),
            pltpu.VMEM((D, OWN), bf16),
            pltpu.VMEM((NX, OWN, WIDE), bf16),
            pltpu.SemaphoreType.DMA((CHUNKS,)),
            pltpu.SemaphoreType.DMA,
            pltpu.SemaphoreType.DMA((2, NX)),
        ],
        compiler_params=params(60),
        cost_estimate=cost(2 * TOKENS * D * OWN, 2 * TOKENS * D),
        name="preact_share",
    )(acts, w_enc, w_dec)


def codes_kernel(place_ref, got_ref, alive_ref, codes_ref, slope_ref):
    core = place_ref[0]
    codes = []
    for rel in range(2):
        src = core if rel == 0 else 1 - core
        preact = jnp.sum(got_ref[src].astype(f32), axis=0)
        alive = alive_ref[rel].astype(f32)
        codes.append(alive * jax.nn.softplus(preact))
        slope_ref[rel] = alive * jax.nn.sigmoid(preact)
    codes_ref[...] = jnp.concatenate(codes, axis=0).astype(bf16)


def make_codes(place, got, alive):
    held = pl.BlockSpec(memory_space=pltpu.VMEM)
    return pl.pallas_call(
        codes_kernel,
        in_specs=[pl.BlockSpec(memory_space=pltpu.SMEM), held, held],
        out_specs=[held] * 2,
        out_shape=[
            jax.ShapeDtypeStruct((2 * SHARD, OWN), bf16),
            jax.ShapeDtypeStruct((2, SHARD, OWN), f32),
        ],
        compiler_params=params(16),
        cost_estimate=cost(1000000, 2000000),
        name="make_codes",
    )(place, got, alive)


def spread_kernel(*refs):
    out_ref = refs[NX]
    for r in range(NX):
        out_ref[:, r] = jnp.broadcast_to(refs[r][...][None], (LAYERS, 2 * SHARD, OWN))


def spread_codes(parts):
    held = pl.BlockSpec(memory_space=pltpu.VMEM)
    return pl.pallas_call(
        spread_kernel,
        in_specs=[held] * NX,
        out_specs=held,
        out_shape=jax.ShapeDtypeStruct((LAYERS, NX, 2 * SHARD, OWN), bf16),
        compiler_params=params(16),
        cost_estimate=cost(1000000, 2000000),
        name="spread_codes",
    )(*parts)


ROWS = 160


def residue_kernel(place_ref, codes_ref, acts_ref, *rest):
    pieces, rest = rest[:2 * NX], rest[2 * NX:]
    share_ref, wide_ref, own_ref, other_ref, got, own_acts, flat, cols, wide, share, in_sems, out_sems = rest
    here = place_ref[1]
    fetch_codes, fetch_cols = [], []
    for r in range(NX):
        fetch_codes.append(pltpu.make_async_copy(codes_ref.at[:, r], got.at[r], in_sems.at[r]))
        for rel in range(2):
            fetch_cols.append(
                pltpu.make_async_copy(
                    pieces[NX * rel + r], cols.at[rel, pl.ds(r * OWN, OWN)], in_sems.at[NX + 2 * r + rel]
                )
            )
    tokens = pl.ds(pl.multiple_of(place_ref[0] * HALF, HALF), HALF)
    width = pl.ds(pl.multiple_of(here * WIDE, WIDE), WIDE)
    fetch_acts = pltpu.make_async_copy(acts_ref.at[tokens, width], own_acts, in_sems.at[3 * NX])
    for copy in fetch_codes + fetch_cols + [fetch_acts]:
        copy.start()
    for r in range(NX):
        fetch_codes[r].wait()
        part = got[r].astype(f32)
        for rel in range(2):
            half = part[:, rel * SHARD:(rel + 1) * SHARD].reshape(HALF, OWN).astype(bf16)
            flat[rel, :, r * OWN:(r + 1) * OWN] = half
    stores = [
        pltpu.make_async_copy(flat.at[0], own_ref, out_sems.at[0]),
        pltpu.make_async_copy(flat.at[1], other_ref, out_sems.at[1]),
        pltpu.make_async_copy(wide, wide_ref, out_sems.at[2]),
        pltpu.make_async_copy(share, share_ref, out_sems.at[3]),
    ]
    stores[0].start()
    stores[1].start()
    for copy in fetch_cols + [fetch_acts]:
        copy.wait()
    for c in range(HALF // ROWS):
        rows = slice(c * ROWS, (c + 1) * ROWS)
        rebuilt = jnp.dot(flat[0, rows, :], cols[0], preferred_element_type=f32)
        rebuilt += jnp.dot(flat[1, rows, :], cols[1], preferred_element_type=f32)
        wide[rows, :] = (rebuilt * DEC_SCALE - own_acts[rows, :].astype(f32)).astype(bf16)
    stores[2].start()
    for pair in range(NX // 2):
        span = slice(2 * pair * OWN, 2 * (pair + 1) * OWN)
        grads = [
            lax.dot_general(
                wide[...], cols[rel, span, :], (((1,), (1,)), ((), ())), preferred_element_type=f32
            ) * DEC_SCALE
            for rel in range(2)
        ]
        for i in range(2):
            parts = [grads[rel][:, i * OWN:(i + 1) * OWN].reshape(LAYERS, SHARD, OWN) for rel in range(2)]
            share[:, 2 * pair + i] = jnp.concatenate(parts, axis=1).astype(bf16)
    stores[3].start()
    for copy in stores:
        copy.wait()


def residue_part(place, codes, acts, pieces):
    anywhere = pl.BlockSpec(memory_space=pl.ANY)
    return pl.pallas_call(
        residue_kernel,
        in_specs=[pl.BlockSpec(memory_space=pltpu.SMEM)] + [anywhere] * (2 + 2 * NX),
        out_specs=[anywhere] * 4,
        scratch_shapes=[
            pltpu.VMEM((NX, LAYERS, 2 * SHARD, OWN), bf16),
            pltpu.VMEM((HALF, WIDE), bf16),
            pltpu.VMEM((2, HALF, NX * OWN), bf16),
            pltpu.VMEM((2, NX * OWN, WIDE), bf16),
            pltpu.VMEM((HALF, WIDE), bf16),
            pltpu.VMEM((LAYERS, NX, 2 * SHARD, OWN), bf16),
            pltpu.SemaphoreType.DMA((3 * NX + 1,)),
            pltpu.SemaphoreType.DMA((4,)),
        ],
        out_shape=[
            jax.ShapeDtypeStruct((LAYERS, NX, 2 * SHARD, OWN), bf16),
            jax.ShapeDtypeStruct((HALF, WIDE), bf16),
            jax.ShapeDtypeStruct((HALF, NX * OWN), bf16),
            jax.ShapeDtypeStruct((HALF, NX * OWN), bf16),
        ],
        compiler_params=params(60),
        cost_estimate=cost(4 * HALF * LAT * WIDE, 10000000),
        name="residue_part",
    )(place, codes, acts, *pieces)


def gradient_kernel(own_ref, wide_ref, own_got_ref, wide_got_ref, *rest):
    outs, (codes, wide, grads, in_sems, out_sems) = rest[:NX], rest[NX:]
    fetches = []
    for i, (left, right) in enumerate(((own_ref, wide_ref), (own_got_ref, wide_got_ref))):
        rows = pl.ds(i * HALF, HALF)
        fetches.append(pltpu.make_async_copy(left, codes.at[rows], in_sems.at[2 * i]))
        fetches.append(pltpu.make_async_copy(right, wide.at[rows], in_sems.at[2 * i + 1]))
    for copy in fetches:
        copy.start()
    for copy in fetches:
        copy.wait()
    stores = []
    for pair in range(NX // 2):
        span = slice(2 * pair * OWN, 2 * (pair + 1) * OWN)
        grad = lax.dot_general(
            codes[:, span], wide[...], (((0,), (0,)), ((), ())), preferred_element_type=f32
        ) * DEC_SCALE
        for i in range(2):
            r = 2 * pair + i
            grads[r] = grad[i * OWN:(i + 1) * OWN].astype(bf16)
            stores.append(pltpu.make_async_copy(grads.at[r], outs[r], out_sems.at[r]))
            stores[r].start()
    for copy in stores:
        copy.wait()


def decoder_gradient(own, wide, own_got, wide_got):
    anywhere = pl.BlockSpec(memory_space=pl.ANY)
    return pl.pallas_call(
        gradient_kernel,
        in_specs=[anywhere] * 4,
        out_specs=[anywhere] * NX,
        out_shape=[jax.ShapeDtypeStruct((OWN, WIDE), bf16)] * NX,
        scratch_shapes=[
            pltpu.VMEM((TOKENS, NX * OWN), bf16),
            pltpu.VMEM((TOKENS, WIDE), bf16),
            pltpu.VMEM((NX, OWN, WIDE), bf16),
            pltpu.SemaphoreType.DMA((4,)),
            pltpu.SemaphoreType.DMA((NX,)),
        ],
        compiler_params=params(60),
        cost_estimate=cost(2 * HALF * LAT * WIDE, 5000000),
        name="decoder_gradient",
    )(own, wide, own_got, wide_got)


def decoder_kernel(place_ref, *refs):
    grads, refs = refs[:NX], refs[NX:]
    w_ref, m_ref, v_ref, m_out, v_out, stepped_out, rms_out, taken, moved, held, in_sems, out_sems = refs
    fetches, stores = [], []
    for r in range(NX):
        span = pl.ds(pl.multiple_of(lax.rem(place_ref[1] + r, NX) * WIDE, WIDE), WIDE)
        sources = (grads[r], w_ref.at[:, span], m_ref.at[:, span], v_ref.at[:, span])
        fetches.append([
            pltpu.make_async_copy(source, taken.at[r, i], in_sems.at[r, i]) for i, source in enumerate(sources)
        ])
        stores.append([
            pltpu.make_async_copy(moved.at[r, 0], m_out.at[:, span], out_sems.at[r, 0]),
            pltpu.make_async_copy(moved.at[r, 1], v_out.at[:, span], out_sems.at[r, 1]),
            pltpu.make_async_copy(held.at[r], stepped_out.at[:, span], out_sems.at[r, 2]),
        ])
    for copies in fetches:
        for copy in copies:
            copy.start()
    total = jnp.zeros((OWN, 1), f32)
    for r in range(NX):
        for copy in fetches[r]:
            copy.wait()
        grad, w, m, v = (taken[r, i].astype(f32) for i in range(4))
        stepped, one, two = adam_step(w, grad, m, v)
        moved[r, 0] = one.astype(bf16)
        moved[r, 1] = two.astype(bf16)
        held[r] = stepped
        for copy in stores[r]:
            copy.start()
        total += jnp.sum(stepped * stepped, axis=1, keepdims=True)
    rms = jnp.sqrt(total * (1.0 / D) + 1e-06)
    rms_out[...] = jnp.broadcast_to(rms, (OWN, OWN)).T[:8]
    for copies in stores:
        for copy in copies:
            copy.wait()


def decoder_adam(place, grads, w, m, v):
    anywhere = pl.BlockSpec(memory_space=pl.ANY)
    return pl.pallas_call(
        decoder_kernel,
        in_specs=[pl.BlockSpec(memory_space=pltpu.SMEM)] + [anywhere] * (NX + 3),
        out_specs=[anywhere] * 3 + [pl.BlockSpec(memory_space=pltpu.VMEM)],
        out_shape=[
            jax.ShapeDtypeStruct((OWN, D), bf16),
            jax.ShapeDtypeStruct((OWN, D), bf16),
            jax.ShapeDtypeStruct((OWN, D), f32),
            jax.ShapeDtypeStruct((8, OWN), f32),
        ],
        scratch_shapes=[
            pltpu.VMEM((NX, 4, OWN, WIDE), bf16),
            pltpu.VMEM((NX, 2, OWN, WIDE), bf16),
            pltpu.VMEM((NX, OWN, WIDE), f32),
            pltpu.SemaphoreType.DMA((NX, 4)),
            pltpu.SemaphoreType.DMA((NX, 3)),
        ],
        compiler_params=params(60),
        cost_estimate=cost(20 * OWN * D, 8000000),
        name="decoder_adam",
    )(place, *grads, w, m, v)


def sum_kernel(got_ref, keep_ref, *outs):
    for r in range(NX):
        both = jnp.sum(got_ref[:, r].astype(f32), axis=0)
        for rel in range(2):
            total = both[rel * SHARD:(rel + 1) * SHARD]
            if r == 0:
                keep_ref[rel] = total
            else:
                outs[r - 1][rel] = total.astype(bf16)


def sum_layers(got):
    return pl.pallas_call(
        sum_kernel,
        in_specs=[pl.BlockSpec(memory_space=pltpu.VMEM)],
        out_specs=[pl.BlockSpec(memory_space=pltpu.VMEM)] * NX,
        out_shape=[jax.ShapeDtypeStruct((2, SHARD, OWN), f32)]
        + [jax.ShapeDtypeStruct((2, SHARD, OWN), bf16)] * (NX - 1),
        compiler_params=params(16),
        cost_estimate=cost(1000000, 2000000),
        name="sum_layers",
    )(got)


def grad_pre_kernel(core_ref, keep_ref, one_ref, two_ref, three_ref, slope_ref, rms_ref, out_ref):
    core = core_ref[0]
    rms = rms_ref[...]
    high = rms.astype(bf16).astype(f32)
    mid = (rms - high).astype(bf16).astype(f32)
    low = rms - high - mid
    row = lax.broadcasted_iota(jnp.int32, (8, OWN), 0)
    tail = jnp.where(row == 0, high, jnp.where(row == 1, mid, jnp.where(row == 2, low, 0.0)))
    for rel in range(2):
        grad = keep_ref[rel] + one_ref[rel].astype(f32) + two_ref[rel].astype(f32) + three_ref[rel].astype(f32)
        message = jnp.concatenate([grad * slope_ref[rel], tail], axis=0).astype(bf16)
        dest = core if rel == 0 else 1 - core
        out_ref[dest] = jnp.broadcast_to(message[None], (LAYERS, MESSAGE, OWN))


def make_grad_pre(core, parts, slope, rms):
    return pl.pallas_call(
        grad_pre_kernel,
        in_specs=[pl.BlockSpec(memory_space=pltpu.SMEM)] + [pl.BlockSpec(memory_space=pltpu.VMEM)] * 6,
        out_specs=pl.BlockSpec(memory_space=pltpu.VMEM),
        out_shape=jax.ShapeDtypeStruct((2, LAYERS, MESSAGE, OWN), bf16),
        compiler_params=params(16),
        cost_estimate=cost(1000000, 2000000),
        name="make_grad_pre",
    )(core, *parts, slope, rms)


PART = 1024
PARTS = D // PART


def encoder_kernel(core_ref, got_ref, w_ref, m_ref, v_ref, acts_ref, dec_ref, *rest):
    w_out, m_out, v_out, dec_out, acts, dec, w_new, m_new, v_new, dec_new, turned, in_sems, out_sems = rest

    def span(c):
        return pl.ds(pl.multiple_of(c * PART, PART), PART)

    def fetches(c):
        return (
            pltpu.make_async_copy(acts_ref.at[:, span(c)], acts.at[c], in_sems.at[c, 0]),
            pltpu.make_async_copy(dec_ref.at[:, span(c)], dec.at[c], in_sems.at[c, 1]),
        )

    def stores(c):
        return (
            pltpu.make_async_copy(w_new.at[c], w_out.at[span(c)], out_sems.at[c, 0]),
            pltpu.make_async_copy(m_new.at[c], m_out.at[span(c)], out_sems.at[c, 1]),
            pltpu.make_async_copy(v_new.at[c], v_out.at[span(c)], out_sems.at[c, 2]),
            pltpu.make_async_copy(dec_new.at[c], dec_out.at[:, span(c)], out_sems.at[c, 3]),
        )

    @pl.loop(0, PARTS)
    def _(c):
        for copy in fetches(c):
            copy.start()

    got = got_ref[...].astype(f32)
    turned[...] = got[:, :, :SHARD].reshape(TOKENS, OWN).T.astype(bf16)
    rms = jnp.sum(got_ref[core_ref[0]].astype(f32)[:, SHARD:], axis=0)
    row = jnp.sum(rms[:3], axis=0, keepdims=True) * (1.0 / LAYERS)
    column = jnp.broadcast_to(row, (OWN, OWN)).T[:, :1]

    @pl.loop(0, PARTS)
    def _(c):
        for copy in fetches(c):
            copy.wait()
        grad = jnp.dot(turned[...], acts[c], preferred_element_type=f32) * ENC_SCALE
        grad = grad.astype(bf16).astype(f32).T
        stepped, one, two = adam_step(
            w_ref[span(c), :].astype(f32), grad, m_ref[span(c), :].astype(f32), v_ref[span(c), :].astype(f32)
        )
        w_new[c] = (stepped * row).astype(bf16)
        m_new[c] = one.astype(bf16)
        v_new[c] = two.astype(bf16)
        dec_new[c] = (dec[c] / column).astype(bf16)
        for copy in stores(c):
            copy.start()

    @pl.loop(0, PARTS)
    def _(c):
        for copy in stores(c):
            copy.wait()


def encoder_adam(core, got, acts, w, m, v, stepped_dec):
    held = pl.BlockSpec(memory_space=pltpu.VMEM)
    anywhere = pl.BlockSpec(memory_space=pl.ANY)
    return pl.pallas_call(
        encoder_kernel,
        in_specs=[pl.BlockSpec(memory_space=pltpu.SMEM)] + [held] * 4 + [anywhere] * 2,
        out_specs=[anywhere] * 4,
        out_shape=[jax.ShapeDtypeStruct((D, OWN), bf16)] * 3 + [jax.ShapeDtypeStruct((OWN, D), bf16)],
        scratch_shapes=[
            pltpu.VMEM((PARTS, TOKENS, PART), bf16),
            pltpu.VMEM((PARTS, OWN, PART), f32),
            pltpu.VMEM((PARTS, PART, OWN), bf16),
            pltpu.VMEM((PARTS, PART, OWN), bf16),
            pltpu.VMEM((PARTS, PART, OWN), bf16),
            pltpu.VMEM((PARTS, OWN, PART), bf16),
            pltpu.VMEM((OWN, TOKENS), bf16),
            pltpu.SemaphoreType.DMA((PARTS, 2)),
            pltpu.SemaphoreType.DMA((PARTS, 4)),
        ],
        compiler_params=params(52),
        cost_estimate=cost(2 * TOKENS * D * OWN, 20000000),
        name="encoder_adam",
    )(core, got, w, m, v, acts, stepped_dec)


def swap(array):
    return lax.ppermute(array, "core", [(0, 1), (1, 0)])


def shift(array, steps):
    return lax.ppermute(array, "x", [(i, (i + steps) % NX) for i in range(NX)])


def exchange(array, axes):
    flat = array.reshape(-1, array.shape[-1])
    return lax.all_to_all(flat, axes, split_axis=0, concat_axis=0, tiled=True).reshape(array.shape)


LAYER_AXES = ("y", "z")
TOKEN_AXES = ("core", "y", "z")


def local(acts, active, w_enc, m_enc, v_enc, w_dec, m_dec, v_dec):
    core = lax.axis_index("core")
    layer = lax.axis_index(LAYER_AXES)
    place = jnp.stack([core, lax.axis_index("x")]).astype(jnp.int32)
    acts, w_dec, m_dec, v_dec = (array[:, 0, :] for array in (acts, w_dec, m_dec, v_dec))

    alive = active.astype(bf16).reshape(2, LAYERS, SHARD, OWN)
    alive = lax.dynamic_index_in_dim(alive, layer, 1, keepdims=False)
    alive_own = lax.dynamic_index_in_dim(alive, core, 0, keepdims=False)
    alive_other = swap(lax.dynamic_index_in_dim(alive, 1 - core, 0, keepdims=False))
    alive = jnp.stack([alive_own, alive_other])

    share, *mine = preact_share(acts, w_enc[0], w_dec)
    own_cols = [mine[0]] + [shift(mine[r], r) for r in range(1, NX)]
    share = exchange(share.reshape(2, LAYERS, SHARD, OWN), TOKEN_AXES)
    codes, slope = make_codes(place, share, alive)
    codes = spread_codes([codes] + [shift(codes, r) for r in range(1, NX)])
    codes = exchange(codes, LAYER_AXES)
    other_cols = [swap(piece) for piece in own_cols]
    grad_share, wide, own, other = residue_part(place, codes, acts, own_cols + other_cols)
    grad_share = exchange(grad_share, LAYER_AXES)

    grad_dec = decoder_gradient(own, wide, swap(other), swap(wide))
    grad_dec = [grad_dec[0]] + [shift(grad_dec[r], NX - r) for r in range(1, NX)]
    m_dec_new, v_dec_new, stepped_dec, rms = decoder_adam(place, grad_dec, w_dec, m_dec, v_dec)

    parts = sum_layers(grad_share)
    parts = [parts[0]] + [shift(parts[r], NX - r) for r in range(1, NX)]
    messages = exchange(make_grad_pre(place, parts, slope, rms), TOKEN_AXES)
    w_enc_new, m_enc_new, v_enc_new, w_dec_new = encoder_adam(
        place, messages, acts, w_enc[0], m_enc[0], v_enc[0], stepped_dec
    )
    return (
        w_enc_new[None],
        m_enc_new[None],
        v_enc_new[None],
        w_dec_new[:, None, :],
        m_dec_new[:, None, :],
        v_dec_new[:, None, :],
    )


def solution(mesh):
    fine = Mesh(mesh.devices.reshape(4, 4, NX, 2), ("y", "z", "x", "core"))
    layer = ("y", "z")
    latent = ("x", "core")
    return jax.shard_map(
        local,
        mesh=fine,
        in_specs=(
            P(None, layer, None),
            P(None, latent),
            P(layer, None, latent),
            P(layer, None, latent),
            P(layer, None, latent),
            P(latent, layer, None),
            P(latent, layer, None),
            P(latent, layer, None),
        ),
        out_specs=(
            P(layer, None, latent),
            P(layer, None, latent),
            P(layer, None, latent),
            P(latent, layer, None),
            P(latent, layer, None),
            P(latent, layer, None),
        ),
        check_vma=False,
    )
```

time: 157 us -> 135 us (0.86)
  waiting for transfers between devices: 58.6 us -> 39.8 us
  blocking collectives: 31.7 us -> 18.3 us
  starting transfers between devices: 22.5 us -> 33.3 us
  local copies, waits for them, and re-layouts: 12.5 us -> 4.45 us
  Pallas kernels: 30 us -> 36.4 us
    all_to_all x4 -> x3, waiting for transfers between devices: 54.8 us -> 21.2 us  [exchange(): lax.all_to_all(flat, axes, split_axis=0, concat_axis=0, tiled=True)]
    ppermute x3 -> x19, starting transfers between devices: 0.17 us -> 16.9 us  [the longest x12 15.7 us: shift(): return lax.ppermute(array, 'x', [(i, (i + steps) % NX) for i in range(NX)])]
    ppermute x3 -> x19, waiting for transfers between devices: 3.82 us -> 18.5 us  [the longest x12 14.2 us: shift(): return lax.ppermute(array, 'x', [(i, (i + steps) % NX) for i in range(NX)])]
    all_to_all x2 -> x1, blocking collectives: 31.7 us -> 18.3 us  [exchange(): lax.all_to_all(flat, axes, split_axis=0, concat_axis=0, tiled=True)]
    unnamed x27 -> x46, local copies, waits for them, and re-layouts: 11.2 us -> 4.44 us
    all_to_all x4 -> x3, starting transfers between devices: 22.3 us -> 16.3 us  [exchange(): lax.all_to_all(flat, axes, split_axis=0, concat_axis=0, tiled=True)]
    pallas_call x5 -> x7, Pallas kernels: 29.6 us -> 35.2 us  [the longest x1 9.03 us: encoder_adam(): pl.pallas_call(encoder_kernel, in_specs=[pl.BlockSpec(memory_space=pltpu....]
  transfers between devices with their start and end apart: 7 -> 22, of which waited for: 6 -> 13; matrix products, arithmetic and copies ran while one was open for 1% -> 0% of each run, Pallas kernels for 2% -> 8%
where the time goes in v2:
time: 135 us; the launch traced here: 133 us
  waiting for transfers between devices  39.8 us (29%)
  Pallas kernels  36.4 us (27%)
  starting transfers between devices  33.3 us (25%)
  blocking collectives  18.3 us (14%)
  local copies, waits for them, and re-layouts  4.45 us (3%)
    all_to_all x3, waiting for transfers between devices, exchange(): lax.all_to_all(flat, axes, split_axis=0, concat_axis=0, tiled=True)  21.2 us
    all_to_all x1, blocking collectives, exchange(): lax.all_to_all(flat, axes, split_axis=0, concat_axis=0, tiled=True)  18.3 us
    all_to_all x3, starting transfers between devices, exchange(): lax.all_to_all(flat, axes, split_axis=0, concat_axis=0, tiled=True)  16.3 us
    ppermute x12, starting transfers between devices, shift(): return lax.ppermute(array, 'x', [(i, (i + steps) % NX) for i in range(NX)])  15.7 us
    ppermute x12, waiting for transfers between devices, shift(): return lax.ppermute(array, 'x', [(i, (i + steps) % NX) for i in range(NX)])  14.2 us
    pallas_call x1, Pallas kernels, encoder_adam(): pl.pallas_call(encoder_kernel, in_specs=[pl.BlockSpec(memory_space=pltpu....  9.03 us
    pallas_call x1, Pallas kernels, residue_part(): pl.pallas_call(residue_kernel, in_specs=[pl.BlockSpec(memory_space=pltpu....  7.43 us
    pallas_call x1, Pallas kernels, preact_share(): pl.pallas_call(preact_kernel, in_specs=[anywhere] * 3, out_specs=[pl.Bloc...  6.82 us
  transfers between devices with their start and end apart: 22, of which 13 were waited for; matrix products, arithmetic and copies ran while one was open for 0% of the time, Pallas kernels for 8%

profile of v2, /device:TPU:0, one launch (start us, length us, event | category | flops | bytes accessed | tf_op | source)
XLA Modules:
  0.0 133.5 jit_solution(1781168248230865270)
XLA Ops:
  0.6 6.8 %preact_share.1 = (bf16[1280,128]{1,0:T(8,128)(2,1)}, bf16[128,1024]{1,0:T(8,128)(2,1)}, bf16[128,1024]{1,0:T(8,128)(2,1)}, bf16[128,1024]{1,0:T(8,128)(2,1)}, bf16[128,1024]{1,0:T(8,128)(2,1)}) custom-call(bf16[1280,4096]{1,0:T(8,128)(2,1)} %bitcast.35, bf16[4096,128]{1,0:T(8,128)(2,1)} %bitcast.30, bf16[128,4096]{1,0:T(8,128)(2,1)} %bitcast.39), custom_call_target="tpu_custom_call" | custom-call | flops 1342177280 | bytes 10485760 | tf_op jit(solution)/shard_map/preact_share/pallas_call | solution.py:95
  7.5 8.4 %all-to-all-start = ((bf16[32,40,128]{2,1,0:T(8,128)(2,1)}), bf16[32,40,128]{2,1,0:T(8,128)(2,1)S(1)}, u32[]{:S(2)}, u32[]{:S(2)}) async-start(bf16[32,40,128]{2,1,0:T(8,128)(2,1)} %bitcast.47), calls=%async_computation | async-start | bytes 655360 | tf_op jit(solution)/shard_map/all_to_all | solution.py:499
  16.0 0.4 collective-permute-start
  16.4 0.1 pad_add_fusion.place_ref.core_ref
  16.4 0.8 collective-permute-done
  17.3 8.6 %all-to-all-done = bf16[32,40,128]{2,1,0:T(8,128)(2,1)S(1)} async-done(((bf16[32,40,128]{2,1,0:T(8,128)(2,1)}), bf16[32,40,128]{2,1,0:T(8,128)(2,1)S(1)}, u32[]{:S(2)}, u32[]{:S(2)}) %all-to-all-start) | async-done | bytes 327712 | tf_op jit(solution)/shard_map/all_to_all | solution.py:499
  25.8 0.6 make_codes.1
  26.5 2.8 %collective-permute-start.3 = (bf16[80,128]{1,0:T(8,128)(2,1)S(1)}, bf16[80,128]{1,0:T(8,128)(2,1)S(1)}, u32[]{:S(2)}, u32[]{:S(2)}) collective-permute-start(bf16[80,128]{1,0:T(8,128)(2,1)S(1)} %get-tuple-element.34.refs_0_), channel_id=1, source_target_pairs={{0,6},{2,0},{4,2},{6,4},{1,7},{3,1},{5,3},{7,5},{8,14},{10,8},{12,... | collective-permute-start | bytes 61448 | tf_op jit(solution)/shard_map/ppermute | solution.py:494
  29.3 0.8 collective-permute-start.2
  30.1 0.9 collective-permute-start.1
  30.9 3.6 %collective-permute-done.2.refs_2_ = bf16[80,128]{1,0:T(8,128)(2,1)S(1)} collective-permute-done((bf16[80,128]{1,0:T(8,128)(2,1)S(1)}, bf16[80,128]{1,0:T(8,128)(2,1)S(1)}, u32[]{:S(2)}, u32[]{:S(2)}) %collective-permute-start.2) | collective-permute-done | bytes 20512 | tf_op jit(solution)/shard_map/ppermute | solution.py:494
  34.5 0.5 collective-permute-done.1.refs_1_
  35.1 1.4 %spread_codes.1 = bf16[16,4,80,128]{3,2,1,0:T(8,128)(2,1)} custom-call(bf16[80,128]{1,0:T(8,128)(2,1)S(1)} %get-tuple-element.34.refs_0_, bf16[80,128]{1,0:T(8,128)(2,1)S(1)} %collective-permute-done.1.refs_1_, bf16[80,128]{1,0:T(8,128)(2,1)S(1)} %collective-permute-done.2.refs_2_, bf16[80,128]{1,0:T(8,128)(2,1)S(1)} %collective-permute-done.3.refs_3_), custom_call_target="tpu_custom_call" | custom-call | flops 1000000 | bytes 2000000 | tf_op jit(solution)/shard_map/spread_codes/pallas_call | solution.py:150
  36.5 3.8 %all-to-all-start.1 = ((bf16[16,320,128]{2,1,0:T(8,128)(2,1)}), bf16[16,320,128]{2,1,0:T(8,128)(2,1)S(1)}, u32[]{:S(2)}, u32[]{:S(2)}) async-start(bf16[16,320,128]{2,1,0:T(8,128)(2,1)} %bitcast.11), calls=%async_computation.1 | async-start | bytes 2621440 | tf_op jit(solution)/shard_map/all_to_all | solution.py:499
  40.3 0.1 collective-permute-start.4
  40.4 1.7 %collective-permute-start.5 = (bf16[128,1024]{1,0:T(8,128)(2,1)S(1)}, bf16[128,1024]{1,0:T(8,128)(2,1)S(1)}, u32[]{:S(2)}, u32[]{:S(2)}) collective-permute-start(bf16[128,1024]{1,0:T(8,128)(2,1)S(1)} %copy-done.21), channel_id=1, source_target_pairs={{0,4},{2,6},{4,0},{6,2},{1,5},{3,7},{5,1},{7,3},{8,12},{10,14},{12... | collective-permute-start | bytes 786440 | tf_op jit(solution)/shard_map/ppermute | solution.py:494
  42.2 2.4 %collective-permute-start.6 = (bf16[128,1024]{1,0:T(8,128)(2,1)S(1)}, bf16[128,1024]{1,0:T(8,128)(2,1)S(1)}, u32[]{:S(2)}, u32[]{:S(2)}) collective-permute-start(bf16[128,1024]{1,0:T(8,128)(2,1)S(1)} %copy-done.20), channel_id=1, source_target_pairs={{0,6},{2,0},{4,2},{6,4},{1,7},{3,1},{5,3},{7,5},{8,14},{10,8},{12,... | collective-permute-start | bytes 786440 | tf_op jit(solution)/shard_map/ppermute | solution.py:494
  44.5 9.0 %collective-permute-done.4.rest_1_ = bf16[128,1024]{1,0:T(8,128)(2,1)S(1)} collective-permute-done((bf16[128,1024]{1,0:T(8,128)(2,1)S(1)}, bf16[128,1024]{1,0:T(8,128)(2,1)S(1)}, u32[]{:S(2)}, u32[]{:S(2)}) %collective-permute-start.4) | collective-permute-done | bytes 262176 | tf_op jit(solution)/shard_map/ppermute | solution.py:494
  53.5 0.5 collective-permute-start.9
  54.0 0.1 collective-permute-done.6.rest_3_
  54.2 0.9 collective-permute-done.8.rest_5_
  55.1 0.4 collective-permute-done.9.rest_6_
  55.4 0.4 collective-permute-done.10.rest_7_
  55.8 3.1 %all-to-all-done.1 = bf16[16,320,128]{2,1,0:T(8,128)(2,1)S(1)} async-done(((bf16[16,320,128]{2,1,0:T(8,128)(2,1)}), bf16[16,320,128]{2,1,0:T(8,128)(2,1)S(1)}, u32[]{:S(2)}, u32[]{:S(2)}) %all-to-all-start.1) | async-done | bytes 1310752 | tf_op jit(solution)/shard_map/all_to_all | solution.py:499
  59.0 1.0 copy-done.4
  60.0 7.4 %residue_part.1 = (bf16[16,4,80,128]{3,2,1,0:T(8,128)(2,1)}, bf16[640,1024]{1,0:T(8,128)(2,1)}, bf16[640,512]{1,0:T(8,128)(2,1)}, bf16[640,512]{1,0:T(8,128)(2,1)}) custom-call(s32[2]{0:T(128)} %copy-done.1, bf16[16,4,80,128]{3,2,1,0:T(8,128)(2,1)} %bitcast.38, bf16[1280,4096]{1,0:T(8,128)(2,1)} %bitcast.36, bf16[128,1024]{1,0:T(8,128)(2,1)} %get-tuple-element.35.rest_0_, ...), custom_call_target="tpu_custom_call" | custom-call | flops 2684354560 | bytes 10000000 | tf_op jit(solution)/shard_map/residue_part/pallas_call | solution.py:222
  67.5 0.1 collective-permute-start.15
  67.6 4.1 %all-to-all-start.2 = ((bf16[16,320,128]{2,1,0:T(8,128)(2,1)}), bf16[16,320,128]{2,1,0:T(8,128)(2,1)S(1)}, u32[]{:S(2)}, u32[]{:S(2)}) async-start(bf16[16,320,128]{2,1,0:T(8,128)(2,1)} %bitcast.41), calls=%async_computation.2 | async-start | bytes 2621440 | tf_op jit(solution)/shard_map/all_to_all | solution.py:499
  71.7 0.3 collective-permute-start.14
  72.0 1.9 %collective-permute-done.14.own_got_ref = bf16[640,512]{1,0:T(8,128)(2,1)S(1)} collective-permute-done((bf16[640,512]{1,0:T(8,128)(2,1)S(1)}, bf16[640,512]{1,0:T(8,128)(2,1)S(1)}, u32[]{:S(2)}, u32[]{:S(2)}) %collective-permute-start.14) | collective-permute-done | bytes 655392 | tf_op jit(solution)/shard_map/ppermute | solution.py:490
  73.9 0.8 copy-done.19
  74.7 1.1 copy-done.17
  75.8 4.5 %decoder_gradient.1 = (bf16[128,1024]{1,0:T(8,128)(2,1)}, bf16[128,1024]{1,0:T(8,128)(2,1)}, bf16[128,1024]{1,0:T(8,128)(2,1)}, bf16[128,1024]{1,0:T(8,128)(2,1)}) custom-call(bf16[640,512]{1,0:T(8,128)(2,1)} %get-tuple-element.45.own_ref, bf16[640,1024]{1,0:T(8,128)(2,1)} %get-tuple-element.46.wide_ref, bf16[640,512]{1,0:T(8,128)(2,1)} %copy-done.19, ...), custom_call_target="tpu_custom_call" | custom-call | flops 1342177280 | bytes 5000000 | tf_op jit(solution)/shard_map/decoder_gradient/pallas_call | solution.py:276
  80.3 2.6 %collective-permute-start.16 = (bf16[128,1024]{1,0:T(8,128)(2,1)}, bf16[128,1024]{1,0:T(8,128)(2,1)S(1)}, u32[]{:S(2)}, u32[]{:S(2)}) collective-permute-start(bf16[128,1024]{1,0:T(8,128)(2,1)} %get-tuple-element.49), channel_id=1, source_target_pairs={{0,6},{2,0},{4,2},{6,4},{1,7},{3,1},{5,3},{7,5},{8,14},{10,8},{12,... | collective-permute-start | bytes 786440 | tf_op jit(solution)/shard_map/ppermute | solution.py:494
  82.8 0.3 collective-permute-start.17
  83.1 0.7 collective-permute-start.18
  83.8 9.5 %all-to-all-done.2 = bf16[16,320,128]{2,1,0:T(8,128)(2,1)S(1)} async-done(((bf16[16,320,128]{2,1,0:T(8,128)(2,1)}), bf16[16,320,128]{2,1,0:T(8,128)(2,1)S(1)}, u32[]{:S(2)}, u32[]{:S(2)}) %all-to-all-start.2) | async-done | bytes 1310752 | tf_op jit(solution)/shard_map/all_to_all | solution.py:499
  93.3 0.2 sum_layers.1
  93.5 2.5 %collective-permute-start.11 = (bf16[2,40,128]{2,1,0:T(8,128)(2,1)S(1)}, bf16[2,40,128]{2,1,0:T(8,128)(2,1)S(1)}, u32[]{:S(2)}, u32[]{:S(2)}) collective-permute-start(bf16[2,40,128]{2,1,0:T(8,128)(2,1)S(1)} %get-tuple-element.41), channel_id=1, source_target_pairs={{0,6},{2,0},{4,2},{6,4},{1,7},{3,1},{5,3},{7,5},{8,14},{10,8},{12,... | collective-permute-start | bytes 61448 | tf_op jit(solution)/shard_map/ppermute | solution.py:494
  96.0 0.3 collective-permute-start.12
  96.3 0.7 collective-permute-start.13
  97.0 1.0 collective-permute-done.18.refs_3_
  97.9 0.7 copy-done.14
  98.6 5.9 %decoder_adam.1 = (bf16[128,4096]{1,0:T(8,128)(2,1)}, bf16[128,4096]{1,0:T(8,128)(2,1)}, f32[128,4096]{1,0:T(8,128)}, f32[8,128]{1,0:T(8,128)}) custom-call(s32[2]{0:T(128)} %copy-done.1, bf16[128,1024]{1,0:T(8,128)(2,1)} %get-tuple-element.48.refs_0_, bf16[128,1024]{1,0:T(8,128)(2,1)} %copy-done.11, bf16[128,1024]{1,0:T(8,128)(2,1)} %copy-done.12, ...), custom_call_target="tpu_custom_call" | custom-call | flops 10485760 | bytes 8000000 | tf_op jit(solution)/shard_map/decoder_adam/pallas_call | solution.py:333
  104.6 0.7 copy-done.3
  105.4 0.6 make_grad_pre.1
  105.9 18.3 %all_to_all.36 = bf16[32,48,128]{2,1,0:T(8,128)(2,1)S(1)} all-to-all(bf16[32,48,128]{2,1,0:T(8,128)(2,1)S(1)} %bitcast.32), channel_id=1, replica_groups=mesh['y'=4,'z'=4,'x'=4,'core'=2] {'core','y','z'}, dimensions={0} | all-to-all | bytes 786432 | tf_op jit(solution)/shard_map/all_to_all | solution.py:499
  124.3 9.0 %encoder_adam.1 = (bf16[4096,128]{1,0:T(8,128)(2,1)}, bf16[4096,128]{1,0:T(8,128)(2,1)}, bf16[4096,128]{1,0:T(8,128)(2,1)}, bf16[128,4096]{1,0:T(8,128)(2,1)}) custom-call(s32[2]{0:T(128)S(1)} %copy-done.2, bf16[2,16,48,128]{3,2,1,0:T(8,128)(2,1)S(1)} %bitcast.33, bf16[4096,128]{1,0:T(8,128)(2,1)S(1)} %bitcast.31, bf16[4096,128]{1,0:T(8,128)(2,1)} %bitcast.44, ...), custom_call_target="tpu_custom_call" | custom-call | flops 1342177280 | bytes 20000000 | tf_op jit(solution)/shard_map/encoder_adam/pallas_call | solution.py:467
  (56 shorter events, 0.2 us)
Async XLA Ops:
  0.6 15.3 %copy-start.5 = (s32[1280,128]{1,0:T(8,128)S(1)}, s32[1280,128]{1,0:T(8,128)}, u32[]{:S(2)}) copy-start(s32[1280,128]{1,0:T(8,128)} %param.9) | copy-start | bytes 1966084
  7.5 18.4 %all-to-all-start = ((bf16[32,40,128]{2,1,0:T(8,128)(2,1)}), bf16[32,40,128]{2,1,0:T(8,128)(2,1)S(1)}, u32[]{:S(2)}, u32[]{:S(2)}) async-start(bf16[32,40,128]{2,1,0:T(8,128)(2,1)} %bitcast.47), calls=%async_computation | async-start | bytes 655360 | tf_op jit(solution)/shard_map/all_to_all | solution.py:499
  16.0 1.3 collective-permute-start
  16.4 20.0 %copy-start.1 = (s32[2]{0:T(128)}, s32[2]{0:T(128)S(1)}, u32[]{:S(2)}) copy-start(s32[2]{0:T(128)S(1)} %pad_add_fusion.place_ref.core_ref) | copy-start | bytes 28
  26.5 4.5 %collective-permute-start.3 = (bf16[80,128]{1,0:T(8,128)(2,1)S(1)}, bf16[80,128]{1,0:T(8,128)(2,1)S(1)}, u32[]{:S(2)}, u32[]{:S(2)}) collective-permute-start(bf16[80,128]{1,0:T(8,128)(2,1)S(1)} %get-tuple-element.34.refs_0_), channel_id=1, source_target_pairs={{0,6},{2,0},{4,2},{6,4},{1,7},{3,1},{5,3},{7,5},{8,14},{10,8},{12,... | collective-permute-start | bytes 61448 | tf_op jit(solution)/shard_map/ppermute | solution.py:494
  29.3 5.3 %collective-permute-start.2 = (bf16[80,128]{1,0:T(8,128)(2,1)S(1)}, bf16[80,128]{1,0:T(8,128)(2,1)S(1)}, u32[]{:S(2)}, u32[]{:S(2)}) collective-permute-start(bf16[80,128]{1,0:T(8,128)(2,1)S(1)} %get-tuple-element.34.refs_0_), channel_id=1, source_target_pairs={{0,4},{2,6},{4,0},{6,2},{1,5},{3,7},{5,1},{7,3},{8,12},{10,14},{12... | collective-permute-start | bytes 61448 | tf_op jit(solution)/shard_map/ppermute | solution.py:494
  30.1 5.0 %collective-permute-start.1 = (bf16[80,128]{1,0:T(8,128)(2,1)S(1)}, bf16[80,128]{1,0:T(8,128)(2,1)S(1)}, u32[]{:S(2)}, u32[]{:S(2)}) collective-permute-start(bf16[80,128]{1,0:T(8,128)(2,1)S(1)} %get-tuple-element.34.refs_0_), channel_id=1, source_target_pairs={{0,2},{2,4},{4,6},{6,0},{1,3},{3,5},{5,7},{7,1},{8,10},{10,12},{12... | collective-permute-start | bytes 61448 | tf_op jit(solution)/shard_map/ppermute | solution.py:494
  36.5 3.9 %copy-start.22 = (bf16[128,1024]{1,0:T(8,128)(2,1)S(1)}, bf16[128,1024]{1,0:T(8,128)(2,1)}, u32[]{:S(2)}) copy-start(bf16[128,1024]{1,0:T(8,128)(2,1)} %get-tuple-element.36) | copy-start | bytes 786436
  36.5 4.0 %copy-start.21 = (bf16[128,1024]{1,0:T(8,128)(2,1)S(1)}, bf16[128,1024]{1,0:T(8,128)(2,1)}, u32[]{:S(2)}) copy-start(bf16[128,1024]{1,0:T(8,128)(2,1)} %get-tuple-element.37) | copy-start | bytes 786436
  36.5 5.7 %copy-start.20 = (bf16[128,1024]{1,0:T(8,128)(2,1)S(1)}, bf16[128,1024]{1,0:T(8,128)(2,1)}, u32[]{:S(2)}) copy-start(bf16[128,1024]{1,0:T(8,128)(2,1)} %get-tuple-element.38) | copy-start | bytes 786436
  36.5 8.1 %copy-start.6 = (bf16[128,1024]{1,0:T(8,128)(2,1)S(1)}, bf16[128,1024]{1,0:T(8,128)(2,1)}, u32[]{:S(2)}) copy-start(bf16[128,1024]{1,0:T(8,128)(2,1)} %get-tuple-element.35.rest_0_) | copy-start | bytes 786436
  36.5 22.5 %all-to-all-start.1 = ((bf16[16,320,128]{2,1,0:T(8,128)(2,1)}), bf16[16,320,128]{2,1,0:T(8,128)(2,1)S(1)}, u32[]{:S(2)}, u32[]{:S(2)}) async-start(bf16[16,320,128]{2,1,0:T(8,128)(2,1)} %bitcast.11), calls=%async_computation.1 | async-start | bytes 2621440 | tf_op jit(solution)/shard_map/all_to_all | solution.py:499
  40.3 13.2 %collective-permute-start.4 = (bf16[128,1024]{1,0:T(8,128)(2,1)S(1)}, bf16[128,1024]{1,0:T(8,128)(2,1)S(1)}, u32[]{:S(2)}, u32[]{:S(2)}) collective-permute-start(bf16[128,1024]{1,0:T(8,128)(2,1)S(1)} %copy-done.22), channel_id=1, source_target_pairs={{0,2},{2,4},{4,6},{6,0},{1,3},{3,5},{5,7},{7,1},{8,10},{10,12},{12... | collective-permute-start | bytes 786440 | tf_op jit(solution)/shard_map/ppermute | solution.py:494
  40.4 13.1 %collective-permute-start.5 = (bf16[128,1024]{1,0:T(8,128)(2,1)S(1)}, bf16[128,1024]{1,0:T(8,128)(2,1)S(1)}, u32[]{:S(2)}, u32[]{:S(2)}) collective-permute-start(bf16[128,1024]{1,0:T(8,128)(2,1)S(1)} %copy-done.21), channel_id=1, source_target_pairs={{0,4},{2,6},{4,0},{6,2},{1,5},{3,7},{5,1},{7,3},{8,12},{10,14},{12... | collective-permute-start | bytes 786440 | tf_op jit(solution)/shard_map/ppermute | solution.py:494
  42.2 12.0 %collective-permute-start.6 = (bf16[128,1024]{1,0:T(8,128)(2,1)S(1)}, bf16[128,1024]{1,0:T(8,128)(2,1)S(1)}, u32[]{:S(2)}, u32[]{:S(2)}) collective-permute-start(bf16[128,1024]{1,0:T(8,128)(2,1)S(1)} %copy-done.20), channel_id=1, source_target_pairs={{0,6},{2,0},{4,2},{6,4},{1,7},{3,1},{5,3},{7,5},{8,14},{10,8},{12,... | collective-permute-start | bytes 786440 | tf_op jit(solution)/shard_map/ppermute | solution.py:494
  44.5 9.6 %collective-permute-start.7 = (bf16[128,1024]{1,0:T(8,128)(2,1)S(1)}, bf16[128,1024]{1,0:T(8,128)(2,1)S(1)}, u32[]{:S(2)}, u32[]{:S(2)}) collective-permute-start(bf16[128,1024]{1,0:T(8,128)(2,1)S(1)} %copy-done.6), channel_id=1, source_target_pairs={{0,1},{1,0},{2,3},{3,2},{4,5},{5,4},{6,7},{7,6},{8,9},{9,8},{10,11... | collective-permute-start | bytes 786440 | tf_op jit(solution)/shard_map/ppermute | solution.py:490
  53.5 5.4 %copy-start.7 = (bf16[128,1024]{1,0:T(8,128)(2,1)}, bf16[128,1024]{1,0:T(8,128)(2,1)S(1)}, u32[]{:S(2)}) copy-start(bf16[128,1024]{1,0:T(8,128)(2,1)S(1)} %collective-permute-done.4.rest_1_) | copy-start | bytes 786436
  53.5 1.5 %collective-permute-start.8 = (bf16[128,1024]{1,0:T(8,128)(2,1)S(1)}, bf16[128,1024]{1,0:T(8,128)(2,1)S(1)}, u32[]{:S(2)}, u32[]{:S(2)}) collective-permute-start(bf16[128,1024]{1,0:T(8,128)(2,1)S(1)} %collective-permute-done.4.rest_1_), channel_id=1, source_target_pairs={{0,1},{1,0},{2,3},{3,2},{4,5},{5,4},{6,7},{7,6},{8,9},{9,8},{10,11... | collective-permute-start | bytes 786440 | tf_op jit(solution)/shard_map/ppermute | solution.py:490
  53.5 5.4 %copy-start.8 = (bf16[128,1024]{1,0:T(8,128)(2,1)}, bf16[128,1024]{1,0:T(8,128)(2,1)S(1)}, u32[]{:S(2)}) copy-start(bf16[128,1024]{1,0:T(8,128)(2,1)S(1)} %collective-permute-done.5.rest_2_) | copy-start | bytes 786436
  53.5 1.9 %collective-permute-start.9 = (bf16[128,1024]{1,0:T(8,128)(2,1)S(1)}, bf16[128,1024]{1,0:T(8,128)(2,1)S(1)}, u32[]{:S(2)}, u32[]{:S(2)}) collective-permute-start(bf16[128,1024]{1,0:T(8,128)(2,1)S(1)} %collective-permute-done.5.rest_2_), channel_id=1, source_target_pairs={{0,1},{1,0},{2,3},{3,2},{4,5},{5,4},{6,7},{7,6},{8,9},{9,8},{10,11... | collective-permute-start | bytes 786440 | tf_op jit(solution)/shard_map/ppermute | solution.py:490
  54.1 4.8 %copy-start.9 = (bf16[128,1024]{1,0:T(8,128)(2,1)}, bf16[128,1024]{1,0:T(8,128)(2,1)S(1)}, u32[]{:S(2)}) copy-start(bf16[128,1024]{1,0:T(8,128)(2,1)S(1)} %collective-permute-done.6.rest_3_) | copy-start | bytes 786436
  54.2 1.7 %collective-permute-start.10 = (bf16[128,1024]{1,0:T(8,128)(2,1)S(1)}, bf16[128,1024]{1,0:T(8,128)(2,1)S(1)}, u32[]{:S(2)}, u32[]{:S(2)}) collective-permute-start(bf16[128,1024]{1,0:T(8,128)(2,1)S(1)} %collective-permute-done.6.rest_3_), channel_id=1, source_target_pairs={{0,1},{1,0},{2,3},{3,2},{4,5},{5,4},{6,7},{7,6},{8,9},{9,8},{10,11... | collective-permute-start | bytes 786440 | tf_op jit(solution)/shard_map/ppermute | solution.py:490
  54.2 4.8 %copy-start.10 = (bf16[128,1024]{1,0:T(8,128)(2,1)}, bf16[128,1024]{1,0:T(8,128)(2,1)S(1)}, u32[]{:S(2)}) copy-start(bf16[128,1024]{1,0:T(8,128)(2,1)S(1)} %collective-permute-done.7.rest_4_) | copy-start | bytes 786436
  55.1 3.9 %copy-start.13 = (bf16[128,1024]{1,0:T(8,128)(2,1)}, bf16[128,1024]{1,0:T(8,128)(2,1)S(1)}, u32[]{:S(2)}) copy-start(bf16[128,1024]{1,0:T(8,128)(2,1)S(1)} %collective-permute-done.8.rest_5_) | copy-start | bytes 786436
  55.4 3.6 %copy-start.15 = (bf16[128,1024]{1,0:T(8,128)(2,1)}, bf16[128,1024]{1,0:T(8,128)(2,1)S(1)}, u32[]{:S(2)}) copy-start(bf16[128,1024]{1,0:T(8,128)(2,1)S(1)} %collective-permute-done.9.rest_6_) | copy-start | bytes 786436
  55.8 3.2 %copy-start.16 = (bf16[128,1024]{1,0:T(8,128)(2,1)}, bf16[128,1024]{1,0:T(8,128)(2,1)S(1)}, u32[]{:S(2)}) copy-start(bf16[128,1024]{1,0:T(8,128)(2,1)S(1)} %collective-permute-done.10.rest_7_) | copy-start | bytes 786436
  59.0 1.1 copy-start.4
  67.5 6.4 %collective-permute-start.15 = (bf16[640,1024]{1,0:T(8,128)(2,1)}, bf16[640,1024]{1,0:T(8,128)(2,1)S(1)}, u32[]{:S(2)}, u32[]{:S(2)}) collective-permute-start(bf16[640,1024]{1,0:T(8,128)(2,1)} %get-tuple-element.46.wide_ref), channel_id=1, source_target_pairs={{0,1},{1,0},{2,3},{3,2},{4,5},{5,4},{6,7},{7,6},{8,9},{9,8},{10,11... | collective-permute-start | bytes 3932168 | tf_op jit(solution)/shard_map/ppermute | solution.py:490
  67.6 4.1 %copy-start.18 = (bf16[640,512]{1,0:T(8,128)(2,1)S(1)}, bf16[640,512]{1,0:T(8,128)(2,1)}, u32[]{:S(2)}) copy-start(bf16[640,512]{1,0:T(8,128)(2,1)} %get-tuple-element.47) | copy-start | bytes 1966084
  67.6 25.7 %all-to-all-start.2 = ((bf16[16,320,128]{2,1,0:T(8,128)(2,1)}), bf16[16,320,128]{2,1,0:T(8,128)(2,1)S(1)}, u32[]{:S(2)}, u32[]{:S(2)}) async-start(bf16[16,320,128]{2,1,0:T(8,128)(2,1)} %bitcast.41), calls=%async_computation.2 | async-start | bytes 2621440 | tf_op jit(solution)/shard_map/all_to_all | solution.py:499
  71.7 2.2 %collective-permute-start.14 = (bf16[640,512]{1,0:T(8,128)(2,1)S(1)}, bf16[640,512]{1,0:T(8,128)(2,1)S(1)}, u32[]{:S(2)}, u32[]{:S(2)}) collective-permute-start(bf16[640,512]{1,0:T(8,128)(2,1)S(1)} %copy-done.18), channel_id=1, source_target_pairs={{0,1},{1,0},{2,3},{3,2},{4,5},{5,4},{6,7},{7,6},{8,9},{9,8},{10,11... | collective-permute-start | bytes 1966088 | tf_op jit(solution)/shard_map/ppermute | solution.py:490
  73.8 0.8 copy-start.19
  74.7 1.1 copy-start.17
  80.3 16.0 %collective-permute-start.16 = (bf16[128,1024]{1,0:T(8,128)(2,1)}, bf16[128,1024]{1,0:T(8,128)(2,1)S(1)}, u32[]{:S(2)}, u32[]{:S(2)}) collective-permute-start(bf16[128,1024]{1,0:T(8,128)(2,1)} %get-tuple-element.49), channel_id=1, source_target_pairs={{0,6},{2,0},{4,2},{6,4},{1,7},{3,1},{5,3},{7,5},{8,14},{10,8},{12,... | collective-permute-start | bytes 786440 | tf_op jit(solution)/shard_map/ppermute | solution.py:494
  82.8 14.2 %collective-permute-start.17 = (bf16[128,1024]{1,0:T(8,128)(2,1)}, bf16[128,1024]{1,0:T(8,128)(2,1)S(1)}, u32[]{:S(2)}, u32[]{:S(2)}) collective-permute-start(bf16[128,1024]{1,0:T(8,128)(2,1)} %get-tuple-element.50), channel_id=1, source_target_pairs={{0,4},{2,6},{4,0},{6,2},{1,5},{3,7},{5,1},{7,3},{8,12},{10,14},{12... | collective-permute-start | bytes 786440 | tf_op jit(solution)/shard_map/ppermute | solution.py:494
  83.1 14.8 %collective-permute-start.18 = (bf16[128,1024]{1,0:T(8,128)(2,1)}, bf16[128,1024]{1,0:T(8,128)(2,1)S(1)}, u32[]{:S(2)}, u32[]{:S(2)}) collective-permute-start(bf16[128,1024]{1,0:T(8,128)(2,1)} %get-tuple-element.51), channel_id=1, source_target_pairs={{0,2},{2,4},{4,6},{6,0},{1,3},{3,5},{5,7},{7,1},{8,10},{10,12},{12... | collective-permute-start | bytes 786440 | tf_op jit(solution)/shard_map/ppermute | solution.py:494
  93.5 11.1 %collective-permute-start.11 = (bf16[2,40,128]{2,1,0:T(8,128)(2,1)S(1)}, bf16[2,40,128]{2,1,0:T(8,128)(2,1)S(1)}, u32[]{:S(2)}, u32[]{:S(2)}) collective-permute-start(bf16[2,40,128]{2,1,0:T(8,128)(2,1)S(1)} %get-tuple-element.41), channel_id=1, source_target_pairs={{0,6},{2,0},{4,2},{6,4},{1,7},{3,1},{5,3},{7,5},{8,14},{10,8},{12,... | collective-permute-start | bytes 61448 | tf_op jit(solution)/shard_map/ppermute | solution.py:494
  96.0 8.6 %collective-permute-start.12 = (bf16[2,40,128]{2,1,0:T(8,128)(2,1)S(1)}, bf16[2,40,128]{2,1,0:T(8,128)(2,1)S(1)}, u32[]{:S(2)}, u32[]{:S(2)}) collective-permute-start(bf16[2,40,128]{2,1,0:T(8,128)(2,1)S(1)} %get-tuple-element.42), channel_id=1, source_target_pairs={{0,4},{2,6},{4,0},{6,2},{1,5},{3,7},{5,1},{7,3},{8,12},{10,14},{12... | collective-permute-start | bytes 61448 | tf_op jit(solution)/shard_map/ppermute | solution.py:494
  96.3 1.6 %copy-start.11 = (bf16[128,1024]{1,0:T(8,128)(2,1)}, bf16[128,1024]{1,0:T(8,128)(2,1)S(1)}, u32[]{:S(2)}) copy-start(bf16[128,1024]{1,0:T(8,128)(2,1)S(1)} %collective-permute-done.16.refs_1_) | copy-start | bytes 786436
  96.3 8.3 %collective-permute-start.13 = (bf16[2,40,128]{2,1,0:T(8,128)(2,1)S(1)}, bf16[2,40,128]{2,1,0:T(8,128)(2,1)S(1)}, u32[]{:S(2)}, u32[]{:S(2)}) collective-permute-start(bf16[2,40,128]{2,1,0:T(8,128)(2,1)S(1)} %get-tuple-element.43), channel_id=1, source_target_pairs={{0,2},{2,4},{4,6},{6,0},{1,3},{3,5},{5,7},{7,1},{8,10},{10,12},{12... | collective-permute-start | bytes 61448 | tf_op jit(solution)/shard_map/ppermute | solution.py:494
  97.0 1.0 copy-start.12
  97.9 0.7 copy-start.14
  98.6 6.0 %copy-start.2 = (s32[2]{0:T(128)S(1)}, s32[2]{0:T(128)}, u32[]{:S(2)}) copy-start(s32[2]{0:T(128)} %copy-done.1) | copy-start | bytes 28
  104.6 19.7 %copy-start = (bf16[1,4096,128]{2,1,0:T(8,128)(2,1)S(1)}, bf16[1,4096,128]{2,1,0:T(8,128)(2,1)}, u32[]{:S(2)}) copy-start(bf16[1,4096,128]{2,1,0:T(8,128)(2,1)} %param.10) | copy-start | bytes 3145732
  104.6 0.8 copy-start.3

commit v3 on v2

--- a/solution.py
+++ b/solution.py
@@ -158,49 +158,28 @@
     )(*parts)
 
 
-ROWS = 160
-
-
-def residue_kernel(place_ref, codes_ref, acts_ref, *rest):
+COLUMNS = 256
+
+
+def residue_kernel(codes_ref, acts_ref, *rest):
     pieces, rest = rest[:2 * NX], rest[2 * NX:]
-    share_ref, wide_ref, own_ref, other_ref, got, own_acts, flat, cols, wide, share, in_sems, out_sems = rest
-    here = place_ref[1]
-    fetch_codes, fetch_cols = [], []
+    share_ref, keep_ref, send_ref, flat, cols, wide, share, halves, out_sems = rest
     for r in range(NX):
-        fetch_codes.append(pltpu.make_async_copy(codes_ref.at[:, r], got.at[r], in_sems.at[r]))
-        for rel in range(2):
-            fetch_cols.append(
-                pltpu.make_async_copy(
-                    pieces[NX * rel + r], cols.at[rel, pl.ds(r * OWN, OWN)], in_sems.at[NX + 2 * r + rel]
-                )
-            )
-    tokens = pl.ds(pl.multiple_of(place_ref[0] * HALF, HALF), HALF)
-    width = pl.ds(pl.multiple_of(here * WIDE, WIDE), WIDE)
-    fetch_acts = pltpu.make_async_copy(acts_ref.at[tokens, width], own_acts, in_sems.at[3 * NX])
-    for copy in fetch_codes + fetch_cols + [fetch_acts]:
-        copy.start()
-    for r in range(NX):
-        fetch_codes[r].wait()
-        part = got[r].astype(f32)
+        part = codes_ref[:, r].astype(f32)
         for rel in range(2):
             half = part[:, rel * SHARD:(rel + 1) * SHARD].reshape(HALF, OWN).astype(bf16)
             flat[rel, :, r * OWN:(r + 1) * OWN] = half
+            cols[rel, r * OWN:(r + 1) * OWN, :] = pieces[NX * rel + r][...]
     stores = [
-        pltpu.make_async_copy(flat.at[0], own_ref, out_sems.at[0]),
-        pltpu.make_async_copy(flat.at[1], other_ref, out_sems.at[1]),
-        pltpu.make_async_copy(wide, wide_ref, out_sems.at[2]),
-        pltpu.make_async_copy(share, share_ref, out_sems.at[3]),
+        pltpu.make_async_copy(share, share_ref, out_sems.at[0]),
+        pltpu.make_async_copy(halves.at[1], send_ref, out_sems.at[1]),
+        pltpu.make_async_copy(halves.at[0], keep_ref, out_sems.at[2]),
     ]
-    stores[0].start()
-    stores[1].start()
-    for copy in fetch_cols + [fetch_acts]:
-        copy.wait()
-    for c in range(HALF // ROWS):
-        rows = slice(c * ROWS, (c + 1) * ROWS)
-        rebuilt = jnp.dot(flat[0, rows, :], cols[0], preferred_element_type=f32)
-        rebuilt += jnp.dot(flat[1, rows, :], cols[1], preferred_element_type=f32)
-        wide[rows, :] = (rebuilt * DEC_SCALE - own_acts[rows, :].astype(f32)).astype(bf16)
-    stores[2].start()
+    for c in range(WIDE // COLUMNS):
+        block = slice(c * COLUMNS, (c + 1) * COLUMNS)
+        rebuilt = jnp.dot(flat[0], cols[0, :, block], preferred_element_type=f32)
+        rebuilt += jnp.dot(flat[1], cols[1, :, block], preferred_element_type=f32)
+        wide[:, block] = (rebuilt * DEC_SCALE - acts_ref[:, block].astype(f32)).astype(bf16)
     for pair in range(NX // 2):
         span = slice(2 * pair * OWN, 2 * (pair + 1) * OWN)
         grads = [
@@ -212,120 +191,129 @@
         for i in range(2):
             parts = [grads[rel][:, i * OWN:(i + 1) * OWN].reshape(LAYERS, SHARD, OWN) for rel in range(2)]
             share[:, 2 * pair + i] = jnp.concatenate(parts, axis=1).astype(bf16)
-    stores[3].start()
+    stores[0].start()
+    for i, rel in enumerate((1, 0)):
+        for c in range(WIDE // COLUMNS):
+            block = slice(c * COLUMNS, (c + 1) * COLUMNS)
+            grad = lax.dot_general(
+                flat[rel], wide[:, block], (((0,), (0,)), ((), ())), preferred_element_type=f32
+            ) * DEC_SCALE
+            for r in range(NX):
+                halves[rel, r, :, block] = grad[r * OWN:(r + 1) * OWN].astype(bf16)
+        stores[1 + i].start()
     for copy in stores:
         copy.wait()
 
 
-def residue_part(place, codes, acts, pieces):
+def residue_part(codes, acts, pieces):
+    held = pl.BlockSpec(memory_space=pltpu.VMEM)
     anywhere = pl.BlockSpec(memory_space=pl.ANY)
     return pl.pallas_call(
         residue_kernel,
-        in_specs=[pl.BlockSpec(memory_space=pltpu.SMEM)] + [anywhere] * (2 + 2 * NX),
-        out_specs=[anywhere] * 4,
+        in_specs=[held] * (2 + 2 * NX),
+        out_specs=[anywhere] * 3,
         scratch_shapes=[
-            pltpu.VMEM((NX, LAYERS, 2 * SHARD, OWN), bf16),
-            pltpu.VMEM((HALF, WIDE), bf16),
             pltpu.VMEM((2, HALF, NX * OWN), bf16),
             pltpu.VMEM((2, NX * OWN, WIDE), bf16),
             pltpu.VMEM((HALF, WIDE), bf16),
             pltpu.VMEM((LAYERS, NX, 2 * SHARD, OWN), bf16),
-            pltpu.SemaphoreType.DMA((3 * NX + 1,)),
-            pltpu.SemaphoreType.DMA((4,)),
+            pltpu.VMEM((2, NX, OWN, WIDE), bf16),
+            pltpu.SemaphoreType.DMA((3,)),
         ],
         out_shape=[
             jax.ShapeDtypeStruct((LAYERS, NX, 2 * SHARD, OWN), bf16),
-            jax.ShapeDtypeStruct((HALF, WIDE), bf16),
-            jax.ShapeDtypeStruct((HALF, NX * OWN), bf16),
-            jax.ShapeDtypeStruct((HALF, NX * OWN), bf16),
-        ],
-        compiler_params=params(60),
-        cost_estimate=cost(4 * HALF * LAT * WIDE, 10000000),
+            jax.ShapeDtypeStruct((NX, OWN, WIDE), bf16),
+            jax.ShapeDtypeStruct((NX, OWN, WIDE), bf16),
+        ],
+        compiler_params=params(58),
+        cost_estimate=cost(6 * HALF * LAT * WIDE, 10000000),
         name="residue_part",
-    )(place, codes, acts, *pieces)
-
-
-def gradient_kernel(own_ref, wide_ref, own_got_ref, wide_got_ref, *rest):
-    outs, (codes, wide, grads, in_sems, out_sems) = rest[:NX], rest[NX:]
+    )(codes, acts, *pieces)
+
+
+def join_kernel(keep_ref, got_ref, *outs):
+    for r in range(NX):
+        outs[r][...] = (keep_ref[r].astype(f32) + got_ref[r].astype(f32)).astype(bf16)
+
+
+def join_halves(keep, got):
+    held = pl.BlockSpec(memory_space=pltpu.VMEM)
+    return pl.pallas_call(
+        join_kernel,
+        in_specs=[held] * 2,
+        out_specs=[held] * NX,
+        out_shape=[jax.ShapeDtypeStruct((OWN, WIDE), bf16)] * NX,
+        compiler_params=params(16),
+        cost_estimate=cost(1000000, 4000000),
+        name="join_halves",
+    )(keep, got)
+
+
+def decoder_spans(place_ref):
+    return [pl.ds(pl.multiple_of(lax.rem(place_ref[1] + r, NX) * WIDE, WIDE), WIDE) for r in range(NX)]
+
+
+def decoder_fetches(spans, grads, sources, taken, sems):
     fetches = []
-    for i, (left, right) in enumerate(((own_ref, wide_ref), (own_got_ref, wide_got_ref))):
-        rows = pl.ds(i * HALF, HALF)
-        fetches.append(pltpu.make_async_copy(left, codes.at[rows], in_sems.at[2 * i]))
-        fetches.append(pltpu.make_async_copy(right, wide.at[rows], in_sems.at[2 * i + 1]))
-    for copy in fetches:
-        copy.start()
-    for copy in fetches:
-        copy.wait()
-    stores = []
-    for pair in range(NX // 2):
-        span = slice(2 * pair * OWN, 2 * (pair + 1) * OWN)
-        grad = lax.dot_general(
-            codes[:, span], wide[...], (((0,), (0,)), ((), ())), preferred_element_type=f32
-        ) * DEC_SCALE
-        for i in range(2):
-            r = 2 * pair + i
-            grads[r] = grad[i * OWN:(i + 1) * OWN].astype(bf16)
-            stores.append(pltpu.make_async_copy(grads.at[r], outs[r], out_sems.at[r]))
-            stores[r].start()
-    for copy in stores:
-        copy.wait()
-
-
-def decoder_gradient(own, wide, own_got, wide_got):
-    anywhere = pl.BlockSpec(memory_space=pl.ANY)
-    return pl.pallas_call(
-        gradient_kernel,
-        in_specs=[anywhere] * 4,
-        out_specs=[anywhere] * NX,
-        out_shape=[jax.ShapeDtypeStruct((OWN, WIDE), bf16)] * NX,
-        scratch_shapes=[
-            pltpu.VMEM((TOKENS, NX * OWN), bf16),
-            pltpu.VMEM((TOKENS, WIDE), bf16),
-            pltpu.VMEM((NX, OWN, WIDE), bf16),
-            pltpu.SemaphoreType.DMA((4,)),
-            pltpu.SemaphoreType.DMA((NX,)),
-        ],
-        compiler_params=params(60),
-        cost_estimate=cost(2 * HALF * LAT * WIDE, 5000000),
-        name="decoder_gradient",
-    )(own, wide, own_got, wide_got)
-
-
-def decoder_kernel(place_ref, *refs):
-    grads, refs = refs[:NX], refs[NX:]
-    w_ref, m_ref, v_ref, m_out, v_out, stepped_out, rms_out, taken, moved, held, in_sems, out_sems = refs
-    fetches, stores = [], []
-    for r in range(NX):
-        span = pl.ds(pl.multiple_of(lax.rem(place_ref[1] + r, NX) * WIDE, WIDE), WIDE)
-        sources = (grads[r], w_ref.at[:, span], m_ref.at[:, span], v_ref.at[:, span])
-        fetches.append([
-            pltpu.make_async_copy(source, taken.at[r, i], in_sems.at[r, i]) for i, source in enumerate(sources)
-        ])
-        stores.append([
-            pltpu.make_async_copy(moved.at[r, 0], m_out.at[:, span], out_sems.at[r, 0]),
-            pltpu.make_async_copy(moved.at[r, 1], v_out.at[:, span], out_sems.at[r, 1]),
-            pltpu.make_async_copy(held.at[r], stepped_out.at[:, span], out_sems.at[r, 2]),
-        ])
+    for r, span in enumerate(spans):
+        parts = [grads[r]] + [source.at[:, span] for source in sources]
+        fetches.append([pltpu.make_async_copy(part, taken.at[r, i], sems.at[r, i]) for i, part in enumerate(parts)])
     for copies in fetches:
         for copy in copies:
             copy.start()
-    total = jnp.zeros((OWN, 1), f32)
+    return fetches
+
+
+def decoder_step(fetches, taken, r):
+    for copy in fetches[r]:
+        copy.wait()
+    grad, w, m, v = (taken[r, i].astype(f32) for i in range(4))
+    return adam_step(w, grad, m, v)
+
+
+def size_kernel(place_ref, *refs):
+    grads, (w_ref, m_ref, v_ref, rms_out) = refs[:NX], refs[NX:]
+    total = jnp.zeros((OWN, OWN), f32)
+    for r, span in enumerate(decoder_spans(place_ref)):
+        grad, w, m, v = (part.astype(f32) for part in (grads[r][...], w_ref[:, span], m_ref[:, span], v_ref[:, span]))
+        stepped = adam_step(w, grad, m, v)[0]
+        square = stepped * stepped
+        for c in range(WIDE // OWN):
+            total += square[:, c * OWN:(c + 1) * OWN]
+    rms = jnp.sqrt(jnp.sum(total.T, axis=0, keepdims=True) * (1.0 / D) + 1e-06)
+    rms_out[...] = jnp.broadcast_to(rms, (8, OWN))
+
+
+def decoder_size(place, grads, w, m, v):
+    held = pl.BlockSpec(memory_space=pltpu.VMEM)
+    return pl.pallas_call(
+        size_kernel,
+        in_specs=[pl.BlockSpec(memory_space=pltpu.SMEM)] + [held] * (NX + 3),
+        out_specs=held,
+        out_shape=jax.ShapeDtypeStruct((8, OWN), f32),
+        compiler_params=params(24),
+        cost_estimate=cost(20 * OWN * D, 4000000),
+        name="decoder_size",
+    )(place, *grads, w, m, v)
+
+
+def decoder_kernel(place_ref, *refs):
+    grads, (w_ref, m_ref, v_ref, *rest) = refs[:NX], refs[NX:]
+    m_out, v_out, stepped_out, taken, moved, held, in_sems, out_sems = rest
+    spans = decoder_spans(place_ref)
+    fetches = decoder_fetches(spans, grads, (w_ref, m_ref, v_ref), taken, in_sems)
+    stores = []
     for r in range(NX):
-        for copy in fetches[r]:
-            copy.wait()
-        grad, w, m, v = (taken[r, i].astype(f32) for i in range(4))
-        stepped, one, two = adam_step(w, grad, m, v)
+        stepped, one, two = decoder_step(fetches, taken, r)
         moved[r, 0] = one.astype(bf16)
         moved[r, 1] = two.astype(bf16)
         held[r] = stepped
-        for copy in stores[r]:
-            copy.start()
-        total += jnp.sum(stepped * stepped, axis=1, keepdims=True)
-    rms = jnp.sqrt(total * (1.0 / D) + 1e-06)
-    rms_out[...] = jnp.broadcast_to(rms, (OWN, OWN)).T[:8]
-    for copies in stores:
-        for copy in copies:
-            copy.wait()
+        sources = (moved.at[r, 0], moved.at[r, 1], held.at[r])
+        for i, target in enumerate((m_out, v_out, stepped_out)):
+            stores.append(pltpu.make_async_copy(sources[i], target.at[:, spans[r]], out_sems.at[r, i]))
+            stores[-1].start()
+    for copy in stores:
+        copy.wait()
 
 
 def decoder_adam(place, grads, w, m, v):
@@ -333,12 +321,11 @@
     return pl.pallas_call(
         decoder_kernel,
         in_specs=[pl.BlockSpec(memory_space=pltpu.SMEM)] + [anywhere] * (NX + 3),
-        out_specs=[anywhere] * 3 + [pl.BlockSpec(memory_space=pltpu.VMEM)],
+        out_specs=[anywhere] * 3,
         out_shape=[
             jax.ShapeDtypeStruct((OWN, D), bf16),
             jax.ShapeDtypeStruct((OWN, D), bf16),
             jax.ShapeDtypeStruct((OWN, D), f32),
-            jax.ShapeDtypeStruct((8, OWN), f32),
         ],
         scratch_shapes=[
             pltpu.VMEM((NX, 4, OWN, WIDE), bf16),
@@ -347,7 +334,7 @@
             pltpu.SemaphoreType.DMA((NX, 4)),
             pltpu.SemaphoreType.DMA((NX, 3)),
         ],
-        compiler_params=params(60),
+        compiler_params=params(54),
         cost_estimate=cost(20 * OWN * D, 8000000),
         name="decoder_adam",
     )(place, *grads, w, m, v)
@@ -522,12 +509,14 @@
     codes = spread_codes([codes] + [shift(codes, r) for r in range(1, NX)])
     codes = exchange(codes, LAYER_AXES)
     other_cols = [swap(piece) for piece in own_cols]
-    grad_share, wide, own, other = residue_part(place, codes, acts, own_cols + other_cols)
+    own_acts = lax.dynamic_slice(acts, (core * HALF, lax.axis_index("x") * WIDE), (HALF, WIDE))
+    grad_share, keep, send = residue_part(codes, own_acts, own_cols + other_cols)
     grad_share = exchange(grad_share, LAYER_AXES)
 
-    grad_dec = decoder_gradient(own, wide, swap(other), swap(wide))
+    grad_dec = join_halves(keep, swap(send))
     grad_dec = [grad_dec[0]] + [shift(grad_dec[r], NX - r) for r in range(1, NX)]
-    m_dec_new, v_dec_new, stepped_dec, rms = decoder_adam(place, grad_dec, w_dec, m_dec, v_dec)
+    rms = decoder_size(place, grad_dec, w_dec, m_dec, v_dec)
+    m_dec_new, v_dec_new, stepped_dec = decoder_adam(place, grad_dec, w_dec, m_dec, v_dec)
 
     parts = sum_layers(grad_share)
     parts = [parts[0]] + [shift(parts[r], NX - r) for r in range(1, NX)]

time: 135 us -> 129 us (0.956)
  blocking collectives: 18.3 us -> 0 us
  starting transfers between devices: 33.3 us -> 38.7 us
  waiting for transfers between devices: 39.8 us -> 44 us
  local copies, waits for them, and re-layouts: 4.45 us -> 7.84 us
    all_to_all x1 -> x0, blocking collectives: 18.3 us -> none  [exchange(): lax.all_to_all(flat, axes, split_axis=0, concat_axis=0, tiled=True)]
    all_to_all x3 -> x4, waiting for transfers between devices: 21.2 us -> 29 us  [exchange(): lax.all_to_all(flat, axes, split_axis=0, concat_axis=0, tiled=True)]
    all_to_all x3 -> x4, starting transfers between devices: 16.3 us -> 21.7 us  [exchange(): lax.all_to_all(flat, axes, split_axis=0, concat_axis=0, tiled=True)]
    ppermute x7 -> x6, waiting for transfers between devices: 4.31 us -> 0.83 us  [swap(): return lax.ppermute(array, 'core', [(0, 1), (1, 0)])]
    dynamic_slice x0 -> x1, local copies, waits for them, and re-layouts: none -> 2.57 us  [local(): lax.dynamic_slice(acts, (core * HALF, lax.axis_index('x') * WIDE), (HALF,...]
    unnamed x46 -> x48, local copies, waits for them, and re-layouts: 4.44 us -> 5.25 us
    pallas_call x2 -> x3, Pallas kernels: 11.9 us -> 12.3 us  [the longest x1 7.81 us: residue_part(): pl.pallas_call(residue_kernel, in_specs=[held] * (2 + 2 * NX), out_specs=...]
  transfers between devices with their start and end apart: 22 -> 22, of which waited for: 13 -> 11; matrix products, arithmetic and copies ran while one was open for 0% -> 2% of each run, Pallas kernels for 8% -> 7%
where the time goes in v3:
time: 129 us; the launch traced here: 128 us
  waiting for transfers between devices  44 us (34%)
  starting transfers between devices  38.7 us (30%)
  Pallas kernels  36.4 us (28%)
  local copies, waits for them, and re-layouts  7.84 us (6%)
    all_to_all x4, waiting for transfers between devices, exchange(): lax.all_to_all(flat, axes, split_axis=0, concat_axis=0, tiled=True)  29 us
    all_to_all x4, starting transfers between devices, exchange(): lax.all_to_all(flat, axes, split_axis=0, concat_axis=0, tiled=True)  21.7 us
    ppermute x12, starting transfers between devices, shift(): return lax.ppermute(array, 'x', [(i, (i + steps) % NX) for i in range(NX)])  16 us
    ppermute x12, waiting for transfers between devices, shift(): return lax.ppermute(array, 'x', [(i, (i + steps) % NX) for i in range(NX)])  14.1 us
    pallas_call x1, Pallas kernels, encoder_adam(): pl.pallas_call(encoder_kernel, in_specs=[pl.BlockSpec(memory_space=pltpu....  9.02 us
    pallas_call x1, Pallas kernels, residue_part(): pl.pallas_call(residue_kernel, in_specs=[held] * (2 + 2 * NX), out_specs=...  7.81 us
    pallas_call x1, Pallas kernels, preact_share(): pl.pallas_call(preact_kernel, in_specs=[anywhere] * 3, out_specs=[pl.Bloc...  6.8 us
    unnamed x48, local copies, waits for them, and re-layouts  5.25 us
  transfers between devices with their start and end apart: 22, of which 11 were waited for; matrix products, arithmetic and copies ran while one was open for 2% of the time, Pallas kernels for 7%

profile of v3, /device:TPU:0, one launch (start us, length us, event | category | flops | bytes accessed | tf_op | source)
XLA Modules:
  0.0 128.1 jit_solution(2599810110458258090)
XLA Ops:
  0.6 6.8 %preact_share.1 = (bf16[1280,128]{1,0:T(8,128)(2,1)}, bf16[128,1024]{1,0:T(8,128)(2,1)}, bf16[128,1024]{1,0:T(8,128)(2,1)}, bf16[128,1024]{1,0:T(8,128)(2,1)}, bf16[128,1024]{1,0:T(8,128)(2,1)}) custom-call(bf16[1280,4096]{1,0:T(8,128)(2,1)} %bitcast.43, bf16[4096,128]{1,0:T(8,128)(2,1)} %bitcast.39, bf16[128,4096]{1,0:T(8,128)(2,1)} %bitcast.31), custom_call_target="tpu_custom_call" | custom-call | flops 1342177280 | bytes 10485760 | tf_op jit(solution)/shard_map/preact_share/pallas_call | solution.py:95
  7.4 8.4 %all-to-all-start = ((bf16[32,40,128]{2,1,0:T(8,128)(2,1)}), bf16[32,40,128]{2,1,0:T(8,128)(2,1)S(1)}, u32[]{:S(2)}, u32[]{:S(2)}) async-start(bf16[32,40,128]{2,1,0:T(8,128)(2,1)} %bitcast.50), calls=%async_computation | async-start | bytes 655360 | tf_op jit(solution)/shard_map/all_to_all | solution.py:486
  16.0 0.4 collective-permute-start
  16.3 0.1 pad_add_fusion.place_ref.core_ref
  16.4 0.8 collective-permute-done
  17.2 8.6 %all-to-all-done = bf16[32,40,128]{2,1,0:T(8,128)(2,1)S(1)} async-done(((bf16[32,40,128]{2,1,0:T(8,128)(2,1)}), bf16[32,40,128]{2,1,0:T(8,128)(2,1)S(1)}, u32[]{:S(2)}, u32[]{:S(2)}) %all-to-all-start) | async-done | bytes 327712 | tf_op jit(solution)/shard_map/all_to_all | solution.py:486
  25.8 0.6 make_codes.1
  26.4 2.8 %collective-permute-start.3 = (bf16[80,128]{1,0:T(8,128)(2,1)S(1)}, bf16[80,128]{1,0:T(8,128)(2,1)S(1)}, u32[]{:S(2)}, u32[]{:S(2)}) collective-permute-start(bf16[80,128]{1,0:T(8,128)(2,1)S(1)} %get-tuple-element.32.refs_0_), channel_id=1, source_target_pairs={{0,6},{2,0},{4,2},{6,4},{1,7},{3,1},{5,3},{7,5},{8,14},{10,8},{12,... | collective-permute-start | bytes 61448 | tf_op jit(solution)/shard_map/ppermute | solution.py:481
  29.3 0.8 collective-permute-start.2
  30.1 0.9 collective-permute-start.1
  31.0 3.6 %collective-permute-done.2.refs_2_ = bf16[80,128]{1,0:T(8,128)(2,1)S(1)} collective-permute-done((bf16[80,128]{1,0:T(8,128)(2,1)S(1)}, bf16[80,128]{1,0:T(8,128)(2,1)S(1)}, u32[]{:S(2)}, u32[]{:S(2)}) %collective-permute-start.2) | collective-permute-done | bytes 20512 | tf_op jit(solution)/shard_map/ppermute | solution.py:481
  34.6 0.5 collective-permute-done.1.refs_1_
  35.1 1.4 %spread_codes.1 = bf16[16,4,80,128]{3,2,1,0:T(8,128)(2,1)} custom-call(bf16[80,128]{1,0:T(8,128)(2,1)S(1)} %get-tuple-element.32.refs_0_, bf16[80,128]{1,0:T(8,128)(2,1)S(1)} %collective-permute-done.1.refs_1_, bf16[80,128]{1,0:T(8,128)(2,1)S(1)} %collective-permute-done.2.refs_2_, bf16[80,128]{1,0:T(8,128)(2,1)S(1)} %collective-permute-done.3.refs_3_), custom_call_target="tpu_custom_call" | custom-call | flops 1000000 | bytes 2000000 | tf_op jit(solution)/shard_map/spread_codes/pallas_call | solution.py:150
  36.5 3.8 %all-to-all-start.1 = ((bf16[16,320,128]{2,1,0:T(8,128)(2,1)}), bf16[16,320,128]{2,1,0:T(8,128)(2,1)S(1)}, u32[]{:S(2)}, u32[]{:S(2)}) async-start(bf16[16,320,128]{2,1,0:T(8,128)(2,1)} %bitcast.11), calls=%async_computation.1 | async-start | bytes 2621440 | tf_op jit(solution)/shard_map/all_to_all | solution.py:486
  40.3 0.1 collective-permute-start.4
  40.4 1.8 %collective-permute-start.5 = (bf16[128,1024]{1,0:T(8,128)(2,1)S(1)}, bf16[128,1024]{1,0:T(8,128)(2,1)S(1)}, u32[]{:S(2)}, u32[]{:S(2)}) collective-permute-start(bf16[128,1024]{1,0:T(8,128)(2,1)S(1)} %copy-done.15), channel_id=1, source_target_pairs={{0,4},{2,6},{4,0},{6,2},{1,5},{3,7},{5,1},{7,3},{8,12},{10,14},{12... | collective-permute-start | bytes 786440 | tf_op jit(solution)/shard_map/ppermute | solution.py:481
  42.2 2.4 %collective-permute-start.6 = (bf16[128,1024]{1,0:T(8,128)(2,1)S(1)}, bf16[128,1024]{1,0:T(8,128)(2,1)S(1)}, u32[]{:S(2)}, u32[]{:S(2)}) collective-permute-start(bf16[128,1024]{1,0:T(8,128)(2,1)S(1)} %copy-done.14), channel_id=1, source_target_pairs={{0,6},{2,0},{4,2},{6,4},{1,7},{3,1},{5,3},{7,5},{8,14},{10,8},{12,... | collective-permute-start | bytes 786440 | tf_op jit(solution)/shard_map/ppermute | solution.py:481
  44.5 9.0 %collective-permute-done.4.rest_1_ = bf16[128,1024]{1,0:T(8,128)(2,1)S(1)} collective-permute-done((bf16[128,1024]{1,0:T(8,128)(2,1)S(1)}, bf16[128,1024]{1,0:T(8,128)(2,1)S(1)}, u32[]{:S(2)}, u32[]{:S(2)}) %collective-permute-start.4) | collective-permute-done | bytes 262176 | tf_op jit(solution)/shard_map/ppermute | solution.py:481
  53.5 0.5 collective-permute-start.9
  54.0 0.1 collective-permute-done.6.rest_3_
  54.1 2.6 %dynamic-slice_bitcast_fusion.acts_ref = bf16[640,1024]{1,0:T(8,128)(2,1)} fusion(bf16[1280,1,4096]{2,0,1:T(8,128)(2,1)} %param.8, s32[]{:T(128)S(6)} %select_n.29, s32[]{:T(128)S(6)} %select_n.30), kind=kLoop, calls=%fused_computation | loop fusion | bytes 2621448 | tf_op jit(solution)/shard_map/dynamic_slice | solution.py:512
  56.8 2.1 %all-to-all-done.1 = bf16[16,320,128]{2,1,0:T(8,128)(2,1)S(1)} async-done(((bf16[16,320,128]{2,1,0:T(8,128)(2,1)}), bf16[16,320,128]{2,1,0:T(8,128)(2,1)S(1)}, u32[]{:S(2)}, u32[]{:S(2)}) %all-to-all-start.1) | async-done | bytes 1310752 | tf_op jit(solution)/shard_map/all_to_all | solution.py:486
  59.0 1.1 copy-done.11
  60.0 7.8 %residue_part.1 = (bf16[16,4,80,128]{3,2,1,0:T(8,128)(2,1)}, bf16[4,128,1024]{2,1,0:T(8,128)(2,1)}, bf16[4,128,1024]{2,1,0:T(8,128)(2,1)}) custom-call(bf16[16,4,80,128]{3,2,1,0:T(8,128)(2,1)} %bitcast.45, bf16[640,1024]{1,0:T(8,128)(2,1)} %dynamic-slice_bitcast_fusion.acts_ref, bf16[128,1024]{1,0:T(8,128)(2,1)} %get-tuple-element.33.rest_0_, ...), custom_call_target="tpu_custom_call" | custom-call | flops 4026531840 | bytes 10000000 | tf_op jit(solution)/shard_map/residue_part/pallas_call | solution.py:211
  67.8 0.1 collective-permute-start.14
  67.9 5.4 %all-to-all-start.2 = ((bf16[16,320,128]{2,1,0:T(8,128)(2,1)}), bf16[16,320,128]{2,1,0:T(8,128)(2,1)S(1)}, u32[]{:S(2)}, u32[]{:S(2)}) async-start(bf16[16,320,128]{2,1,0:T(8,128)(2,1)} %bitcast.46), calls=%async_computation.2 | async-start | bytes 2621440 | tf_op jit(solution)/shard_map/all_to_all | solution.py:486
  73.3 1.0 copy-done.7
  74.3 1.2 copy-done.6
  75.5 1.2 copy-done.8
  76.8 1.0 join_halves.1
  77.8 0.7 copy-done.4
  78.5 2.6 %collective-permute-start.15 = (bf16[128,1024]{1,0:T(8,128)(2,1)}, bf16[128,1024]{1,0:T(8,128)(2,1)}, u32[]{:S(2)}, u32[]{:S(2)}) collective-permute-start(bf16[128,1024]{1,0:T(8,128)(2,1)} %get-tuple-element.46), channel_id=1, source_target_pairs={{0,6},{2,0},{4,2},{6,4},{1,7},{3,1},{5,3},{7,5},{8,14},{10,8},{12,... | collective-permute-start | bytes 786440 | tf_op jit(solution)/shard_map/ppermute | solution.py:481
  81.1 0.3 collective-permute-start.16
  81.4 0.6 collective-permute-start.17
  81.9 12.4 %all-to-all-done.2 = bf16[16,320,128]{2,1,0:T(8,128)(2,1)S(1)} async-done(((bf16[16,320,128]{2,1,0:T(8,128)(2,1)}), bf16[16,320,128]{2,1,0:T(8,128)(2,1)S(1)}, u32[]{:S(2)}, u32[]{:S(2)}) %all-to-all-start.2) | async-done | bytes 1310752 | tf_op jit(solution)/shard_map/all_to_all | solution.py:486
  94.4 0.2 sum_layers.1
  94.6 2.9 %collective-permute-start.11 = (bf16[2,40,128]{2,1,0:T(8,128)(2,1)S(1)}, bf16[2,40,128]{2,1,0:T(8,128)(2,1)S(1)}, u32[]{:S(2)}, u32[]{:S(2)}) collective-permute-start(bf16[2,40,128]{2,1,0:T(8,128)(2,1)S(1)} %get-tuple-element.39), channel_id=1, source_target_pairs={{0,6},{2,0},{4,2},{6,4},{1,7},{3,1},{5,3},{7,5},{8,14},{10,8},{12,... | collective-permute-start | bytes 61448 | tf_op jit(solution)/shard_map/ppermute | solution.py:481
  97.4 0.3 collective-permute-start.12
  97.7 0.6 collective-permute-start.13
  98.4 3.5 %decoder_size.1.rms_ref = f32[8,128]{1,0:T(8,128)S(1)} custom-call(s32[2]{0:T(128)S(1)} %pad_add_fusion.place_ref.core_ref, bf16[128,1024]{1,0:T(8,128)(2,1)S(1)} %copy-done.5, bf16[128,1024]{1,0:T(8,128)(2,1)} %collective-permute-done.15.refs_1_, bf16[128,1024]{1,0:T(8,128)(2,1)} %collective-permute-done.16.refs_2_, ...), custom_call_target="tpu_custom_call" | custom-call | flops 10485760 | bytes 4000000 | tf_op jit(solution)/shard_map/decoder_size/pallas_call | solution.py:289
  102.0 0.8 collective-permute-done.12.two_ref
  102.7 0.2 collective-permute-done.13.three_ref
  102.9 1.3 %make_grad_pre.1 = bf16[2,16,48,128]{3,2,1,0:T(8,128)(2,1)} custom-call(s32[2]{0:T(128)S(1)} %pad_add_fusion.place_ref.core_ref, f32[2,40,128]{2,1,0:T(8,128)S(1)} %get-tuple-element.38.keep_ref, bf16[2,40,128]{2,1,0:T(8,128)(2,1)S(1)} %collective-permute-done.11.one_ref, bf16[2,40,128]{2,1,0:T(8,128)(2,1)S(1)} %collective-permute-done.12.two_ref, ...), custom_call_target="tpu_custom_call" | custom-call | flops 1000000 | bytes 2000000 | tf_op jit(solution)/shard_map/make_grad_pre/pallas_call | solution.py:383
  104.3 4.0 %all-to-all-start.3 = ((bf16[32,48,128]{2,1,0:T(8,128)(2,1)}), bf16[32,48,128]{2,1,0:T(8,128)(2,1)S(1)}, u32[]{:S(2)}, u32[]{:S(2)}) async-start(bf16[32,48,128]{2,1,0:T(8,128)(2,1)} %bitcast.18), calls=%async_computation.3 | async-start | bytes 786432 | tf_op jit(solution)/shard_map/all_to_all | solution.py:486
  108.3 0.0 copy-start.3
  108.3 4.7 %decoder_adam.1 = (bf16[128,4096]{1,0:T(8,128)(2,1)}, bf16[128,4096]{1,0:T(8,128)(2,1)}, f32[128,4096]{1,0:T(8,128)}) custom-call(s32[2]{0:T(128)} %copy-done.9, bf16[128,1024]{1,0:T(8,128)(2,1)} %copy-done.4, bf16[128,1024]{1,0:T(8,128)(2,1)} %collective-permute-done.15.refs_1_, bf16[128,1024]{1,0:T(8,128)(2,1)} %collective-permute-done.16.refs_2_, ...), custom_call_target="tpu_custom_call" | custom-call | flops 10485760 | bytes 8000000 | tf_op jit(solution)/shard_map/decoder_adam/pallas_call | solution.py:321
  113.1 5.8 %all-to-all-done.3 = bf16[32,48,128]{2,1,0:T(8,128)(2,1)S(1)} async-done(((bf16[32,48,128]{2,1,0:T(8,128)(2,1)}), bf16[32,48,128]{2,1,0:T(8,128)(2,1)S(1)}, u32[]{:S(2)}, u32[]{:S(2)}) %all-to-all-start.3) | async-done | bytes 393248 | tf_op jit(solution)/shard_map/all_to_all | solution.py:486
  118.9 9.0 %encoder_adam.1 = (bf16[4096,128]{1,0:T(8,128)(2,1)}, bf16[4096,128]{1,0:T(8,128)(2,1)}, bf16[4096,128]{1,0:T(8,128)(2,1)}, bf16[128,4096]{1,0:T(8,128)(2,1)}) custom-call(s32[2]{0:T(128)S(1)} %copy-done.10, bf16[2,16,48,128]{3,2,1,0:T(8,128)(2,1)S(1)} %bitcast.41, bf16[4096,128]{1,0:T(8,128)(2,1)S(1)} %bitcast.40, bf16[4096,128]{1,0:T(8,128)(2,1)} %bitcast.47, ...), custom_call_target="tpu_custom_call" | custom-call | flops 1342177280 | bytes 20000000 | tf_op jit(solution)/shard_map/encoder_adam/pallas_call | solution.py:454
  (59 shorter events, 0.2 us)
Async XLA Ops:
  0.6 15.3 %copy-start.12 = (s32[1280,128]{1,0:T(8,128)S(1)}, s32[1280,128]{1,0:T(8,128)}, u32[]{:S(2)}) copy-start(s32[1280,128]{1,0:T(8,128)} %param.9) | copy-start | bytes 1966084
  7.4 18.4 %all-to-all-start = ((bf16[32,40,128]{2,1,0:T(8,128)(2,1)}), bf16[32,40,128]{2,1,0:T(8,128)(2,1)S(1)}, u32[]{:S(2)}, u32[]{:S(2)}) async-start(bf16[32,40,128]{2,1,0:T(8,128)(2,1)} %bitcast.50), calls=%async_computation | async-start | bytes 655360 | tf_op jit(solution)/shard_map/all_to_all | solution.py:486
  16.0 1.3 collective-permute-start
  16.4 86.5 %copy-start.9 = (s32[2]{0:T(128)}, s32[2]{0:T(128)S(1)}, u32[]{:S(2)}) copy-start(s32[2]{0:T(128)S(1)} %pad_add_fusion.place_ref.core_ref) | copy-start | bytes 28
  26.4 4.5 %collective-permute-start.3 = (bf16[80,128]{1,0:T(8,128)(2,1)S(1)}, bf16[80,128]{1,0:T(8,128)(2,1)S(1)}, u32[]{:S(2)}, u32[]{:S(2)}) collective-permute-start(bf16[80,128]{1,0:T(8,128)(2,1)S(1)} %get-tuple-element.32.refs_0_), channel_id=1, source_target_pairs={{0,6},{2,0},{4,2},{6,4},{1,7},{3,1},{5,3},{7,5},{8,14},{10,8},{12,... | collective-permute-start | bytes 61448 | tf_op jit(solution)/shard_map/ppermute | solution.py:481
  29.3 5.3 %collective-permute-start.2 = (bf16[80,128]{1,0:T(8,128)(2,1)S(1)}, bf16[80,128]{1,0:T(8,128)(2,1)S(1)}, u32[]{:S(2)}, u32[]{:S(2)}) collective-permute-start(bf16[80,128]{1,0:T(8,128)(2,1)S(1)} %get-tuple-element.32.refs_0_), channel_id=1, source_target_pairs={{0,4},{2,6},{4,0},{6,2},{1,5},{3,7},{5,1},{7,3},{8,12},{10,14},{12... | collective-permute-start | bytes 61448 | tf_op jit(solution)/shard_map/ppermute | solution.py:481
  30.1 5.0 %collective-permute-start.1 = (bf16[80,128]{1,0:T(8,128)(2,1)S(1)}, bf16[80,128]{1,0:T(8,128)(2,1)S(1)}, u32[]{:S(2)}, u32[]{:S(2)}) collective-permute-start(bf16[80,128]{1,0:T(8,128)(2,1)S(1)} %get-tuple-element.32.refs_0_), channel_id=1, source_target_pairs={{0,2},{2,4},{4,6},{6,0},{1,3},{3,5},{5,7},{7,1},{8,10},{10,12},{12... | collective-permute-start | bytes 61448 | tf_op jit(solution)/shard_map/ppermute | solution.py:481
  36.4 3.9 %copy-start.16 = (bf16[128,1024]{1,0:T(8,128)(2,1)S(1)}, bf16[128,1024]{1,0:T(8,128)(2,1)}, u32[]{:S(2)}) copy-start(bf16[128,1024]{1,0:T(8,128)(2,1)} %get-tuple-element.34) | copy-start | bytes 786436
  36.4 4.0 %copy-start.15 = (bf16[128,1024]{1,0:T(8,128)(2,1)S(1)}, bf16[128,1024]{1,0:T(8,128)(2,1)}, u32[]{:S(2)}) copy-start(bf16[128,1024]{1,0:T(8,128)(2,1)} %get-tuple-element.35) | copy-start | bytes 786436
  36.4 5.7 %copy-start.14 = (bf16[128,1024]{1,0:T(8,128)(2,1)S(1)}, bf16[128,1024]{1,0:T(8,128)(2,1)}, u32[]{:S(2)}) copy-start(bf16[128,1024]{1,0:T(8,128)(2,1)} %get-tuple-element.36) | copy-start | bytes 786436
  36.4 8.1 %copy-start.13 = (bf16[128,1024]{1,0:T(8,128)(2,1)S(1)}, bf16[128,1024]{1,0:T(8,128)(2,1)}, u32[]{:S(2)}) copy-start(bf16[128,1024]{1,0:T(8,128)(2,1)} %get-tuple-element.33.rest_0_) | copy-start | bytes 786436
  36.5 22.5 %all-to-all-start.1 = ((bf16[16,320,128]{2,1,0:T(8,128)(2,1)}), bf16[16,320,128]{2,1,0:T(8,128)(2,1)S(1)}, u32[]{:S(2)}, u32[]{:S(2)}) async-start(bf16[16,320,128]{2,1,0:T(8,128)(2,1)} %bitcast.11), calls=%async_computation.1 | async-start | bytes 2621440 | tf_op jit(solution)/shard_map/all_to_all | solution.py:486
  40.3 13.2 %collective-permute-start.4 = (bf16[128,1024]{1,0:T(8,128)(2,1)S(1)}, bf16[128,1024]{1,0:T(8,128)(2,1)S(1)}, u32[]{:S(2)}, u32[]{:S(2)}) collective-permute-start(bf16[128,1024]{1,0:T(8,128)(2,1)S(1)} %copy-done.16), channel_id=1, source_target_pairs={{0,2},{2,4},{4,6},{6,0},{1,3},{3,5},{5,7},{7,1},{8,10},{10,12},{12... | collective-permute-start | bytes 786440 | tf_op jit(solution)/shard_map/ppermute | solution.py:481
  40.4 13.1 %collective-permute-start.5 = (bf16[128,1024]{1,0:T(8,128)(2,1)S(1)}, bf16[128,1024]{1,0:T(8,128)(2,1)S(1)}, u32[]{:S(2)}, u32[]{:S(2)}) collective-permute-start(bf16[128,1024]{1,0:T(8,128)(2,1)S(1)} %copy-done.15), channel_id=1, source_target_pairs={{0,4},{2,6},{4,0},{6,2},{1,5},{3,7},{5,1},{7,3},{8,12},{10,14},{12... | collective-permute-start | bytes 786440 | tf_op jit(solution)/shard_map/ppermute | solution.py:481
  42.2 12.0 %collective-permute-start.6 = (bf16[128,1024]{1,0:T(8,128)(2,1)S(1)}, bf16[128,1024]{1,0:T(8,128)(2,1)S(1)}, u32[]{:S(2)}, u32[]{:S(2)}) collective-permute-start(bf16[128,1024]{1,0:T(8,128)(2,1)S(1)} %copy-done.14), channel_id=1, source_target_pairs={{0,6},{2,0},{4,2},{6,4},{1,7},{3,1},{5,3},{7,5},{8,14},{10,8},{12,... | collective-permute-start | bytes 786440 | tf_op jit(solution)/shard_map/ppermute | solution.py:481
  44.5 12.2 %collective-permute-start.7 = (bf16[128,1024]{1,0:T(8,128)(2,1)S(1)}, bf16[128,1024]{1,0:T(8,128)(2,1)S(1)}, u32[]{:S(2)}, u32[]{:S(2)}) collective-permute-start(bf16[128,1024]{1,0:T(8,128)(2,1)S(1)} %copy-done.13), channel_id=1, source_target_pairs={{0,1},{1,0},{2,3},{3,2},{4,5},{5,4},{6,7},{7,6},{8,9},{9,8},{10,11... | collective-permute-start | bytes 786440 | tf_op jit(solution)/shard_map/ppermute | solution.py:477
  53.5 3.2 %copy-start.17 = (bf16[128,1024]{1,0:T(8,128)(2,1)}, bf16[128,1024]{1,0:T(8,128)(2,1)S(1)}, u32[]{:S(2)}) copy-start(bf16[128,1024]{1,0:T(8,128)(2,1)S(1)} %collective-permute-done.4.rest_1_) | copy-start | bytes 786436
  53.5 3.2 %collective-permute-start.8 = (bf16[128,1024]{1,0:T(8,128)(2,1)S(1)}, bf16[128,1024]{1,0:T(8,128)(2,1)S(1)}, u32[]{:S(2)}, u32[]{:S(2)}) collective-permute-start(bf16[128,1024]{1,0:T(8,128)(2,1)S(1)} %collective-permute-done.4.rest_1_), channel_id=1, source_target_pairs={{0,1},{1,0},{2,3},{3,2},{4,5},{5,4},{6,7},{7,6},{8,9},{9,8},{10,11... | collective-permute-start | bytes 786440 | tf_op jit(solution)/shard_map/ppermute | solution.py:477
  53.5 3.2 %copy-start.18 = (bf16[128,1024]{1,0:T(8,128)(2,1)}, bf16[128,1024]{1,0:T(8,128)(2,1)S(1)}, u32[]{:S(2)}) copy-start(bf16[128,1024]{1,0:T(8,128)(2,1)S(1)} %collective-permute-done.5.rest_2_) | copy-start | bytes 786436
  53.5 3.2 %collective-permute-start.9 = (bf16[128,1024]{1,0:T(8,128)(2,1)S(1)}, bf16[128,1024]{1,0:T(8,128)(2,1)S(1)}, u32[]{:S(2)}, u32[]{:S(2)}) collective-permute-start(bf16[128,1024]{1,0:T(8,128)(2,1)S(1)} %collective-permute-done.5.rest_2_), channel_id=1, source_target_pairs={{0,1},{1,0},{2,3},{3,2},{4,5},{5,4},{6,7},{7,6},{8,9},{9,8},{10,11... | collective-permute-start | bytes 786440 | tf_op jit(solution)/shard_map/ppermute | solution.py:477
  54.1 2.6 %copy-start.19 = (bf16[128,1024]{1,0:T(8,128)(2,1)}, bf16[128,1024]{1,0:T(8,128)(2,1)S(1)}, u32[]{:S(2)}) copy-start(bf16[128,1024]{1,0:T(8,128)(2,1)S(1)} %collective-permute-done.6.rest_3_) | copy-start | bytes 786436
  54.1 2.6 %collective-permute-start.10 = (bf16[128,1024]{1,0:T(8,128)(2,1)S(1)}, bf16[128,1024]{1,0:T(8,128)(2,1)S(1)}, u32[]{:S(2)}, u32[]{:S(2)}) collective-permute-start(bf16[128,1024]{1,0:T(8,128)(2,1)S(1)} %collective-permute-done.6.rest_3_), channel_id=1, source_target_pairs={{0,1},{1,0},{2,3},{3,2},{4,5},{5,4},{6,7},{7,6},{8,9},{9,8},{10,11... | collective-permute-start | bytes 786440 | tf_op jit(solution)/shard_map/ppermute | solution.py:477
  56.7 2.2 %copy-start.20 = (bf16[128,1024]{1,0:T(8,128)(2,1)}, bf16[128,1024]{1,0:T(8,128)(2,1)S(1)}, u32[]{:S(2)}) copy-start(bf16[128,1024]{1,0:T(8,128)(2,1)S(1)} %collective-permute-done.7.rest_4_) | copy-start | bytes 786436
  56.7 2.2 %copy-start.21 = (bf16[128,1024]{1,0:T(8,128)(2,1)}, bf16[128,1024]{1,0:T(8,128)(2,1)S(1)}, u32[]{:S(2)}) copy-start(bf16[128,1024]{1,0:T(8,128)(2,1)S(1)} %collective-permute-done.8.rest_5_) | copy-start | bytes 786436
  56.8 2.2 %copy-start.22 = (bf16[128,1024]{1,0:T(8,128)(2,1)}, bf16[128,1024]{1,0:T(8,128)(2,1)S(1)}, u32[]{:S(2)}) copy-start(bf16[128,1024]{1,0:T(8,128)(2,1)S(1)} %collective-permute-done.9.rest_6_) | copy-start | bytes 786436
  56.8 2.2 %copy-start.23 = (bf16[128,1024]{1,0:T(8,128)(2,1)}, bf16[128,1024]{1,0:T(8,128)(2,1)S(1)}, u32[]{:S(2)}) copy-start(bf16[128,1024]{1,0:T(8,128)(2,1)S(1)} %collective-permute-done.10.rest_7_) | copy-start | bytes 786436
  58.9 1.1 copy-start.11
  67.8 5.5 %collective-permute-start.14 = (bf16[4,128,1024]{2,1,0:T(8,128)(2,1)}, bf16[4,128,1024]{2,1,0:T(8,128)(2,1)S(1)}, u32[]{:S(2)}, u32[]{:S(2)}) collective-permute-start(bf16[4,128,1024]{2,1,0:T(8,128)(2,1)} %get-tuple-element.44), channel_id=1, source_target_pairs={{0,1},{1,0},{2,3},{3,2},{4,5},{5,4},{6,7},{7,6},{8,9},{9,8},{10,11... | collective-permute-start | bytes 3145736 | tf_op jit(solution)/shard_map/ppermute | solution.py:477
  67.9 26.5 %all-to-all-start.2 = ((bf16[16,320,128]{2,1,0:T(8,128)(2,1)}), bf16[16,320,128]{2,1,0:T(8,128)(2,1)S(1)}, u32[]{:S(2)}, u32[]{:S(2)}) async-start(bf16[16,320,128]{2,1,0:T(8,128)(2,1)} %bitcast.46), calls=%async_computation.2 | async-start | bytes 2621440 | tf_op jit(solution)/shard_map/all_to_all | solution.py:486
  73.3 1.0 copy-start.7
  74.3 1.2 copy-start.6
  75.5 1.2 copy-start.8
  76.8 21.6 %copy-start = (bf16[128,1,4096]{2,0,1:T(8,128)(2,1)S(1)}, bf16[128,1,4096]{2,0,1:T(8,128)(2,1)}, u32[]{:S(2)}) copy-start(bf16[128,1,4096]{2,0,1:T(8,128)(2,1)} %param.13) | copy-start | bytes 3145732
  76.8 21.6 %copy-start.1 = (bf16[128,1,4096]{2,0,1:T(8,128)(2,1)S(1)}, bf16[128,1,4096]{2,0,1:T(8,128)(2,1)}, u32[]{:S(2)}) copy-start(bf16[128,1,4096]{2,0,1:T(8,128)(2,1)} %param.14) | copy-start | bytes 3145732
  77.7 0.7 copy-start.4
  78.5 19.3 %collective-permute-start.15 = (bf16[128,1024]{1,0:T(8,128)(2,1)}, bf16[128,1024]{1,0:T(8,128)(2,1)}, u32[]{:S(2)}, u32[]{:S(2)}) collective-permute-start(bf16[128,1024]{1,0:T(8,128)(2,1)} %get-tuple-element.46), channel_id=1, source_target_pairs={{0,6},{2,0},{4,2},{6,4},{1,7},{3,1},{5,3},{7,5},{8,14},{10,8},{12,... | collective-permute-start | bytes 786440 | tf_op jit(solution)/shard_map/ppermute | solution.py:481
  81.1 17.3 %collective-permute-start.16 = (bf16[128,1024]{1,0:T(8,128)(2,1)}, bf16[128,1024]{1,0:T(8,128)(2,1)}, u32[]{:S(2)}, u32[]{:S(2)}) collective-permute-start(bf16[128,1024]{1,0:T(8,128)(2,1)} %get-tuple-element.47), channel_id=1, source_target_pairs={{0,4},{2,6},{4,0},{6,2},{1,5},{3,7},{5,1},{7,3},{8,12},{10,14},{12... | collective-permute-start | bytes 786440 | tf_op jit(solution)/shard_map/ppermute | solution.py:481
  81.4 17.0 %collective-permute-start.17 = (bf16[128,1024]{1,0:T(8,128)(2,1)}, bf16[128,1024]{1,0:T(8,128)(2,1)}, u32[]{:S(2)}, u32[]{:S(2)}) collective-permute-start(bf16[128,1024]{1,0:T(8,128)(2,1)} %get-tuple-element.48), channel_id=1, source_target_pairs={{0,2},{2,4},{4,6},{6,0},{1,3},{3,5},{5,7},{7,1},{8,10},{10,12},{12... | collective-permute-start | bytes 786440 | tf_op jit(solution)/shard_map/ppermute | solution.py:481
  94.4 4.0 %copy-start.2 = (bf16[128,1,4096]{2,0,1:T(8,128)(2,1)S(1)}, bf16[128,1,4096]{2,0,1:T(8,128)(2,1)}, u32[]{:S(2)}) copy-start(bf16[128,1,4096]{2,0,1:T(8,128)(2,1)} %param.15) | copy-start | bytes 3145732
  94.4 4.0 %copy-start.5 = (bf16[128,1024]{1,0:T(8,128)(2,1)S(1)}, bf16[128,1024]{1,0:T(8,128)(2,1)}, u32[]{:S(2)}) copy-start(bf16[128,1024]{1,0:T(8,128)(2,1)} %copy-done.4) | copy-start | bytes 786436
  94.6 7.4 %collective-permute-start.11 = (bf16[2,40,128]{2,1,0:T(8,128)(2,1)S(1)}, bf16[2,40,128]{2,1,0:T(8,128)(2,1)S(1)}, u32[]{:S(2)}, u32[]{:S(2)}) collective-permute-start(bf16[2,40,128]{2,1,0:T(8,128)(2,1)S(1)} %get-tuple-element.39), channel_id=1, source_target_pairs={{0,6},{2,0},{4,2},{6,4},{1,7},{3,1},{5,3},{7,5},{8,14},{10,8},{12,... | collective-permute-start | bytes 61448 | tf_op jit(solution)/shard_map/ppermute | solution.py:481
  97.4 5.3 %collective-permute-start.12 = (bf16[2,40,128]{2,1,0:T(8,128)(2,1)S(1)}, bf16[2,40,128]{2,1,0:T(8,128)(2,1)S(1)}, u32[]{:S(2)}, u32[]{:S(2)}) collective-permute-start(bf16[2,40,128]{2,1,0:T(8,128)(2,1)S(1)} %get-tuple-element.40), channel_id=1, source_target_pairs={{0,4},{2,6},{4,0},{6,2},{1,5},{3,7},{5,1},{7,3},{8,12},{10,14},{12... | collective-permute-start | bytes 61448 | tf_op jit(solution)/shard_map/ppermute | solution.py:481
  97.7 5.2 %collective-permute-start.13 = (bf16[2,40,128]{2,1,0:T(8,128)(2,1)S(1)}, bf16[2,40,128]{2,1,0:T(8,128)(2,1)S(1)}, u32[]{:S(2)}, u32[]{:S(2)}) collective-permute-start(bf16[2,40,128]{2,1,0:T(8,128)(2,1)S(1)} %get-tuple-element.41), channel_id=1, source_target_pairs={{0,2},{2,4},{4,6},{6,0},{1,3},{3,5},{5,7},{7,1},{8,10},{10,12},{12... | collective-permute-start | bytes 61448 | tf_op jit(solution)/shard_map/ppermute | solution.py:481
  104.3 14.6 %all-to-all-start.3 = ((bf16[32,48,128]{2,1,0:T(8,128)(2,1)}), bf16[32,48,128]{2,1,0:T(8,128)(2,1)S(1)}, u32[]{:S(2)}, u32[]{:S(2)}) async-start(bf16[32,48,128]{2,1,0:T(8,128)(2,1)} %bitcast.18), calls=%async_computation.3 | async-start | bytes 786432 | tf_op jit(solution)/shard_map/all_to_all | solution.py:486
  108.3 10.6 %copy-start.3 = (bf16[1,4096,128]{2,1,0:T(8,128)(2,1)S(1)}, bf16[1,4096,128]{2,1,0:T(8,128)(2,1)}, u32[]{:S(2)}) copy-start(bf16[1,4096,128]{2,1,0:T(8,128)(2,1)} %param.10) | copy-start | bytes 3145732
  108.3 10.6 %copy-start.10 = (s32[2]{0:T(128)S(1)}, s32[2]{0:T(128)}, u32[]{:S(2)}) copy-start(s32[2]{0:T(128)} %copy-done.9) | copy-start | bytes 28

commit v4 on v3

--- a/solution.py
+++ b/solution.py
@@ -17,7 +17,7 @@
 WIDE = D // NX
 ENC_SCALE = (LAYERS * D) ** (-0.5)
 DEC_SCALE = LAT ** (-0.5)
-MESSAGE = 48
+MESSAGE = 96
 
 bf16 = jnp.bfloat16
 f32 = jnp.float32
@@ -40,11 +40,13 @@
 
 CHUNKS = 8
 CHUNK = TOKENS // CHUNKS
+BLOCKS = CHUNK // SHARD
 
 
 def preact_kernel(acts_ref, w_ref, dec_ref, out_ref, *rest):
-    pieces, (rows, weights, dec, row_sems, weight_sem, cut_sems) = rest[:NX], rest[NX:]
-    here = lax.axis_index("x")
+    pieces, (own_ref, rows, weights, dec, row_sems, weight_sem, cut_sems, own_sems) = rest[:NX], rest[NX:]
+    here, core = lax.axis_index("x"), lax.axis_index("core")
+    width = pl.ds(pl.multiple_of(here * WIDE, WIDE), WIDE)
     fetch = pltpu.make_async_copy(w_ref, weights, weight_sem)
     fetch.start()
 
@@ -67,16 +69,27 @@
     def _(c):
         block(c).start()
 
-    def multiply(c):
+    def own(c):
+        place = lax.rem(c, CHUNKS // 2)
+        target = own_ref.at[pl.ds(pl.multiple_of(place * CHUNK, CHUNK), CHUNK)]
+        return pltpu.make_async_copy(rows.at[c, :, width], target, own_sems.at[place])
+
+    def multiply(c, half):
         block(c).wait()
+
+        @pl.when(core == half)
+        def _():
+            own(c).start()
+
         share = jnp.dot(rows[c], weights[...], preferred_element_type=f32)
-        out_ref[pl.ds(pl.multiple_of(c * CHUNK, CHUNK), CHUNK), :] = (share * ENC_SCALE).astype(out_ref.dtype)
+        blocks = pl.ds((c - half * (CHUNKS // 2)) * BLOCKS, BLOCKS)
+        out_ref[blocks, half] = (share * ENC_SCALE).reshape(BLOCKS, SHARD, OWN).astype(bf16)
 
     fetch.wait()
 
     @pl.loop(0, CHUNKS // 2)
     def _(c):
-        multiply(c)
+        multiply(c, 0)
 
     for take, give in cuts:
         take.wait()
@@ -84,19 +97,25 @@
 
     @pl.loop(CHUNKS // 2, CHUNKS)
     def _(c):
-        multiply(c)
+        multiply(c, 1)
 
     for _, give in cuts:
         give.wait()
 
+    @pl.loop(0, CHUNKS // 2)
+    def _(c):
+        own(c + core * (CHUNKS // 2)).wait()
+
 
 def preact_share(acts, w_enc, w_dec):
     anywhere = pl.BlockSpec(memory_space=pl.ANY)
     return pl.pallas_call(
         preact_kernel,
         in_specs=[anywhere] * 3,
-        out_specs=[pl.BlockSpec(memory_space=pltpu.VMEM)] + [anywhere] * NX,
-        out_shape=[jax.ShapeDtypeStruct((TOKENS, OWN), bf16)] + [jax.ShapeDtypeStruct((OWN, WIDE), bf16)] * NX,
+        out_specs=[pl.BlockSpec(memory_space=pltpu.VMEM)] + [anywhere] * (NX + 1),
+        out_shape=[jax.ShapeDtypeStruct((LAYERS, 2, SHARD, OWN), bf16)]
+        + [jax.ShapeDtypeStruct((OWN, WIDE), bf16)] * NX
+        + [jax.ShapeDtypeStruct((HALF, WIDE), bf16)],
         scratch_shapes=[
             pltpu.VMEM((CHUNKS, CHUNK, D), bf16),
             pltpu.VMEM((D, OWN), bf16),
@@ -104,6 +123,7 @@
             pltpu.SemaphoreType.DMA((CHUNKS,)),
             pltpu.SemaphoreType.DMA,
             pltpu.SemaphoreType.DMA((2, NX)),
+            pltpu.SemaphoreType.DMA((CHUNKS // 2,)),
         ],
         compiler_params=params(60),
         cost_estimate=cost(2 * TOKENS * D * OWN, 2 * TOKENS * D),
@@ -111,38 +131,34 @@
     )(acts, w_enc, w_dec)
 
 
-def codes_kernel(place_ref, got_ref, alive_ref, codes_ref, slope_ref):
-    core = place_ref[0]
-    codes = []
-    for rel in range(2):
-        src = core if rel == 0 else 1 - core
-        preact = jnp.sum(got_ref[src].astype(f32), axis=0)
-        alive = alive_ref[rel].astype(f32)
-        codes.append(alive * jax.nn.softplus(preact))
-        slope_ref[rel] = alive * jax.nn.sigmoid(preact)
-    codes_ref[...] = jnp.concatenate(codes, axis=0).astype(bf16)
-
-
-def make_codes(place, got, alive):
+def codes_kernel(got_ref, alive_ref, codes_ref, slope_ref):
+    preact = jnp.sum(got_ref[...].astype(f32), axis=0)
+    alive = alive_ref[...].astype(f32)
+    codes_ref[...] = (alive * jax.nn.softplus(preact)).astype(bf16)
+    slope_ref[...] = alive * jax.nn.sigmoid(preact)
+
+
+def make_codes(got, alive):
     held = pl.BlockSpec(memory_space=pltpu.VMEM)
     return pl.pallas_call(
         codes_kernel,
-        in_specs=[pl.BlockSpec(memory_space=pltpu.SMEM), held, held],
+        in_specs=[held] * 2,
         out_specs=[held] * 2,
         out_shape=[
-            jax.ShapeDtypeStruct((2 * SHARD, OWN), bf16),
+            jax.ShapeDtypeStruct((2, SHARD, OWN), bf16),
             jax.ShapeDtypeStruct((2, SHARD, OWN), f32),
         ],
         compiler_params=params(16),
         cost_estimate=cost(1000000, 2000000),
         name="make_codes",
-    )(place, got, alive)
+    )(got, alive)
 
 
 def spread_kernel(*refs):
     out_ref = refs[NX]
     for r in range(NX):
-        out_ref[:, r] = jnp.broadcast_to(refs[r][...][None], (LAYERS, 2 * SHARD, OWN))
+        for half in range(2):
+            out_ref[half, :, r] = jnp.broadcast_to(refs[r][half][None], (LAYERS, SHARD, OWN))
 
 
 def spread_codes(parts):
@@ -151,7 +167,7 @@
         spread_kernel,
         in_specs=[held] * NX,
         out_specs=held,
-        out_shape=jax.ShapeDtypeStruct((LAYERS, NX, 2 * SHARD, OWN), bf16),
+        out_shape=jax.ShapeDtypeStruct((2, LAYERS, NX, SHARD, OWN), bf16),
         compiler_params=params(16),
         cost_estimate=cost(1000000, 2000000),
         name="spread_codes",
@@ -162,13 +178,14 @@
 
 
 def residue_kernel(codes_ref, acts_ref, *rest):
+    core = lax.axis_index("core")
+    order = (core, 1 - core)
     pieces, rest = rest[:2 * NX], rest[2 * NX:]
     share_ref, keep_ref, send_ref, flat, cols, wide, share, halves, out_sems = rest
     for r in range(NX):
-        part = codes_ref[:, r].astype(f32)
         for rel in range(2):
-            half = part[:, rel * SHARD:(rel + 1) * SHARD].reshape(HALF, OWN).astype(bf16)
-            flat[rel, :, r * OWN:(r + 1) * OWN] = half
+            part = codes_ref[order[rel], :, r].astype(f32)
+            flat[rel, :, r * OWN:(r + 1) * OWN] = part.reshape(HALF, OWN).astype(bf16)
             cols[rel, r * OWN:(r + 1) * OWN, :] = pieces[NX * rel + r][...]
     stores = [
         pltpu.make_async_copy(share, share_ref, out_sems.at[0]),
@@ -189,8 +206,9 @@
             for rel in range(2)
         ]
         for i in range(2):
-            parts = [grads[rel][:, i * OWN:(i + 1) * OWN].reshape(LAYERS, SHARD, OWN) for rel in range(2)]
-            share[:, 2 * pair + i] = jnp.concatenate(parts, axis=1).astype(bf16)
+            for rel in range(2):
+                part = grads[rel][:, i * OWN:(i + 1) * OWN].reshape(LAYERS, SHARD, OWN)
+                share[order[rel], :, 2 * pair + i] = part.astype(bf16)
     stores[0].start()
     for i, rel in enumerate((1, 0)):
         for c in range(WIDE // COLUMNS):
@@ -216,12 +234,12 @@
             pltpu.VMEM((2, HALF, NX * OWN), bf16),
             pltpu.VMEM((2, NX * OWN, WIDE), bf16),
             pltpu.VMEM((HALF, WIDE), bf16),
-            pltpu.VMEM((LAYERS, NX, 2 * SHARD, OWN), bf16),
+            pltpu.VMEM((2, LAYERS, NX, SHARD, OWN), bf16),
             pltpu.VMEM((2, NX, OWN, WIDE), bf16),
             pltpu.SemaphoreType.DMA((3,)),
         ],
         out_shape=[
-            jax.ShapeDtypeStruct((LAYERS, NX, 2 * SHARD, OWN), bf16),
+            jax.ShapeDtypeStruct((2, LAYERS, NX, SHARD, OWN), bf16),
             jax.ShapeDtypeStruct((NX, OWN, WIDE), bf16),
             jax.ShapeDtypeStruct((NX, OWN, WIDE), bf16),
         ],
@@ -342,20 +360,19 @@
 
 def sum_kernel(got_ref, keep_ref, *outs):
     for r in range(NX):
-        both = jnp.sum(got_ref[:, r].astype(f32), axis=0)
-        for rel in range(2):
-            total = both[rel * SHARD:(rel + 1) * SHARD]
-            if r == 0:
-                keep_ref[rel] = total
-            else:
-                outs[r - 1][rel] = total.astype(bf16)
+        total = jnp.sum(got_ref[:, :, r].astype(f32), axis=1)
+        if r == 0:
+            keep_ref[...] = total
+        else:
+            outs[r - 1][...] = total.astype(bf16)
 
 
 def sum_layers(got):
+    held = pl.BlockSpec(memory_space=pltpu.VMEM)
     return pl.pallas_call(
         sum_kernel,
-        in_specs=[pl.BlockSpec(memory_space=pltpu.VMEM)],
-        out_specs=[pl.BlockSpec(memory_space=pltpu.VMEM)] * NX,
+        in_specs=[held],
+        out_specs=[held] * NX,
         out_shape=[jax.ShapeDtypeStruct((2, SHARD, OWN), f32)]
         + [jax.ShapeDtypeStruct((2, SHARD, OWN), bf16)] * (NX - 1),
         compiler_params=params(16),
@@ -364,38 +381,36 @@
     )(got)
 
 
-def grad_pre_kernel(core_ref, keep_ref, one_ref, two_ref, three_ref, slope_ref, rms_ref, out_ref):
-    core = core_ref[0]
+def grad_pre_kernel(zero_ref, one_ref, two_ref, three_ref, slope_ref, rms_ref, out_ref):
     rms = rms_ref[...]
     high = rms.astype(bf16).astype(f32)
     mid = (rms - high).astype(bf16).astype(f32)
     low = rms - high - mid
     row = lax.broadcasted_iota(jnp.int32, (8, OWN), 0)
     tail = jnp.where(row == 0, high, jnp.where(row == 1, mid, jnp.where(row == 2, low, 0.0)))
-    for rel in range(2):
-        grad = keep_ref[rel] + one_ref[rel].astype(f32) + two_ref[rel].astype(f32) + three_ref[rel].astype(f32)
-        message = jnp.concatenate([grad * slope_ref[rel], tail], axis=0).astype(bf16)
-        dest = core if rel == 0 else 1 - core
-        out_ref[dest] = jnp.broadcast_to(message[None], (LAYERS, MESSAGE, OWN))
-
-
-def make_grad_pre(core, parts, slope, rms):
+    grad = sum(ref[...].astype(f32) for ref in (zero_ref, one_ref, two_ref, three_ref)) * slope_ref[...]
+    message = jnp.concatenate([grad.reshape(2 * SHARD, OWN), tail, jnp.zeros((8, OWN), f32)], axis=0)
+    out_ref[...] = jnp.broadcast_to(message.astype(bf16)[None], (LAYERS, MESSAGE, OWN))
+
+
+def make_grad_pre(parts, slope, rms):
+    held = pl.BlockSpec(memory_space=pltpu.VMEM)
     return pl.pallas_call(
         grad_pre_kernel,
-        in_specs=[pl.BlockSpec(memory_space=pltpu.SMEM)] + [pl.BlockSpec(memory_space=pltpu.VMEM)] * 6,
-        out_specs=pl.BlockSpec(memory_space=pltpu.VMEM),
-        out_shape=jax.ShapeDtypeStruct((2, LAYERS, MESSAGE, OWN), bf16),
+        in_specs=[held] * 6,
+        out_specs=held,
+        out_shape=jax.ShapeDtypeStruct((LAYERS, MESSAGE, OWN), bf16),
         compiler_params=params(16),
         cost_estimate=cost(1000000, 2000000),
         name="make_grad_pre",
-    )(core, *parts, slope, rms)
+    )(*parts, slope, rms)
 
 
 PART = 1024
 PARTS = D // PART
 
 
-def encoder_kernel(core_ref, got_ref, w_ref, m_ref, v_ref, acts_ref, dec_ref, *rest):
+def encoder_kernel(got_ref, w_ref, m_ref, v_ref, acts_ref, dec_ref, *rest):
     w_out, m_out, v_out, dec_out, acts, dec, w_new, m_new, v_new, dec_new, turned, in_sems, out_sems = rest
 
     def span(c):
@@ -421,8 +436,10 @@
             copy.start()
 
     got = got_ref[...].astype(f32)
-    turned[...] = got[:, :, :SHARD].reshape(TOKENS, OWN).T.astype(bf16)
-    rms = jnp.sum(got_ref[core_ref[0]].astype(f32)[:, SHARD:], axis=0)
+    for half in range(2):
+        grad_pre = got[:, half * SHARD:(half + 1) * SHARD].reshape(HALF, OWN)
+        turned[:, half * HALF:(half + 1) * HALF] = grad_pre.T.astype(bf16)
+    rms = jnp.sum(got[:, 2 * SHARD:], axis=0)
     row = jnp.sum(rms[:3], axis=0, keepdims=True) * (1.0 / LAYERS)
     column = jnp.broadcast_to(row, (OWN, OWN)).T[:, :1]
 
@@ -448,12 +465,12 @@
             copy.wait()
 
 
-def encoder_adam(core, got, acts, w, m, v, stepped_dec):
+def encoder_adam(got, acts, w, m, v, stepped_dec):
     held = pl.BlockSpec(memory_space=pltpu.VMEM)
     anywhere = pl.BlockSpec(memory_space=pl.ANY)
     return pl.pallas_call(
         encoder_kernel,
-        in_specs=[pl.BlockSpec(memory_space=pltpu.SMEM)] + [held] * 4 + [anywhere] * 2,
+        in_specs=[held] * 4 + [anywhere] * 2,
         out_specs=[anywhere] * 4,
         out_shape=[jax.ShapeDtypeStruct((D, OWN), bf16)] * 3 + [jax.ShapeDtypeStruct((OWN, D), bf16)],
         scratch_shapes=[
@@ -470,7 +487,7 @@
         compiler_params=params(52),
         cost_estimate=cost(2 * TOKENS * D * OWN, 20000000),
         name="encoder_adam",
-    )(core, got, w, m, v, acts, stepped_dec)
+    )(got, w, m, v, acts, stepped_dec)
 
 
 def swap(array):
@@ -498,20 +515,15 @@
 
     alive = active.astype(bf16).reshape(2, LAYERS, SHARD, OWN)
     alive = lax.dynamic_index_in_dim(alive, layer, 1, keepdims=False)
-    alive_own = lax.dynamic_index_in_dim(alive, core, 0, keepdims=False)
-    alive_other = swap(lax.dynamic_index_in_dim(alive, 1 - core, 0, keepdims=False))
-    alive = jnp.stack([alive_own, alive_other])
-
-    share, *mine = preact_share(acts, w_enc[0], w_dec)
+
+    share, *mine, own_acts = preact_share(acts, w_enc[0], w_dec)
     own_cols = [mine[0]] + [shift(mine[r], r) for r in range(1, NX)]
-    share = exchange(share.reshape(2, LAYERS, SHARD, OWN), TOKEN_AXES)
-    codes, slope = make_codes(place, share, alive)
+    codes, slope = make_codes(exchange(share, LAYER_AXES), alive)
     codes = spread_codes([codes] + [shift(codes, r) for r in range(1, NX)])
-    codes = exchange(codes, LAYER_AXES)
+    codes = exchange(codes, TOKEN_AXES)
     other_cols = [swap(piece) for piece in own_cols]
-    own_acts = lax.dynamic_slice(acts, (core * HALF, lax.axis_index("x") * WIDE), (HALF, WIDE))
     grad_share, keep, send = residue_part(codes, own_acts, own_cols + other_cols)
-    grad_share = exchange(grad_share, LAYER_AXES)
+    grad_share = exchange(grad_share, TOKEN_AXES)
 
     grad_dec = join_halves(keep, swap(send))
     grad_dec = [grad_dec[0]] + [shift(grad_dec[r], NX - r) for r in range(1, NX)]
@@ -520,9 +532,9 @@
 
     parts = sum_layers(grad_share)
     parts = [parts[0]] + [shift(parts[r], NX - r) for r in range(1, NX)]
-    messages = exchange(make_grad_pre(place, parts, slope, rms), TOKEN_AXES)
+    messages = exchange(make_grad_pre(parts, slope, rms), LAYER_AXES)
     w_enc_new, m_enc_new, v_enc_new, w_dec_new = encoder_adam(
-        place, messages, acts, w_enc[0], m_enc[0], v_enc[0], stepped_dec
+        messages, acts, w_enc[0], m_enc[0], v_enc[0], stepped_dec
     )
     return (
         w_enc_new[None],

time: 129 us -> 127 us (0.984)
  local copies, waits for them, and re-layouts: 7.84 us -> 5.21 us
  waiting for transfers between devices: 44 us -> 46.1 us
    dynamic_slice x2 -> x0, local copies, waits for them, and re-layouts: 2.58 us -> none  [the longest x1 2.57 us: local(): lax.dynamic_slice(acts, (core * HALF, lax.axis_index('x') * WIDE), (HALF,...]
    ppermute x12, waiting for transfers between devices: 14.1 us -> 16.1 us  [shift(): return lax.ppermute(array, 'x', [(i, (i + steps) % NX) for i in range(NX)])]
    unnamed x48 -> x46, local copies, waits for them, and re-layouts: 5.25 us -> 5.2 us
  transfers between devices with their start and end apart: 22 -> 21, of which waited for: 11 -> 13; matrix products, arithmetic and copies ran while one was open for 2% -> 0% of each run, Pallas kernels for 7% -> 7%
where the time goes in v4:
time: 127 us
  waiting for transfers between devices  46.1 us (36%)
  starting transfers between devices  38.6 us (30%)
  Pallas kernels  35.4 us (28%)
  local copies, waits for them, and re-layouts  5.21 us (4%)
    all_to_all x4, waiting for transfers between devices, exchange(): lax.all_to_all(flat, axes, split_axis=0, concat_axis=0, tiled=True)  28.4 us
    all_to_all x4, starting transfers between devices, exchange(): lax.all_to_all(flat, axes, split_axis=0, concat_axis=0, tiled=True)  22.2 us
    ppermute x12, waiting for transfers between devices, shift(): return lax.ppermute(array, 'x', [(i, (i + steps) % NX) for i in range(NX)])  16.1 us
    ppermute x12, starting transfers between devices, shift(): return lax.ppermute(array, 'x', [(i, (i + steps) % NX) for i in range(NX)])  15.8 us
    pallas_call x1, Pallas kernels, encoder_adam(): pl.pallas_call(encoder_kernel, in_specs=[held] * 4 + [anywhere] * 2, out_...  9.03 us
    pallas_call x1, Pallas kernels, residue_part(): pl.pallas_call(residue_kernel, in_specs=[held] * (2 + 2 * NX), out_specs=...  7.81 us
    pallas_call x1, Pallas kernels, preact_share(): pl.pallas_call(preact_kernel, in_specs=[anywhere] * 3, out_specs=[pl.Bloc...  6.99 us
    unnamed x46, local copies, waits for them, and re-layouts  5.2 us
  transfers between devices with their start and end apart: 21, of which 13 were waited for; matrix products, arithmetic and copies ran while one was open for 0% of the time, Pallas kernels for 7%

profile of v4, /device:TPU:0, one launch (start us, length us, event | category | flops | bytes accessed | tf_op | source)
XLA Modules:
  0.0 126.6 jit_solution(10134330657695960351)
XLA Ops:
  0.6 7.0 %preact_share.1 = (bf16[16,2,40,128]{3,2,1,0:T(8,128)(2,1)}, bf16[128,1024]{1,0:T(8,128)(2,1)}, bf16[128,1024]{1,0:T(8,128)(2,1)}, bf16[128,1024]{1,0:T(8,128)(2...) custom-call(bf16[1280,4096]{1,0:T(8,128)(2,1)} %bitcast.37, bf16[4096,128]{1,0:T(8,128)(2,1)} %bitcast.34, ...), custom_call_target="tpu_custom_call" | custom-call | flops 1342177280 | bytes 10485760 | tf_op jit(solution)/shard_map/preact_share/pallas_call | solution.py:112
  7.6 8.1 %all-to-all-start = ((bf16[16,80,128]{2,1,0:T(8,128)(2,1)}), bf16[16,80,128]{2,1,0:T(8,128)(2,1)S(1)}, u32[]{:S(2)}, u32[]{:S(2)}) async-start(bf16[16,80,128]{2,1,0:T(8,128)(2,1)} %bitcast.44), calls=%async_computation | async-start | bytes 655360 | tf_op jit(solution)/shard_map/all_to_all | solution.py:503
  15.9 9.2 %all-to-all-done = bf16[16,80,128]{2,1,0:T(8,128)(2,1)S(1)} async-done(((bf16[16,80,128]{2,1,0:T(8,128)(2,1)}), bf16[16,80,128]{2,1,0:T(8,128)(2,1)S(1)}, u32[]{:S(2)}, u32[]{:S(2)}) %all-to-all-start) | async-done | bytes 327712 | tf_op jit(solution)/shard_map/all_to_all | solution.py:503
  25.1 0.1 make_codes.1
  25.1 2.8 %collective-permute-start.2 = (bf16[2,40,128]{2,1,0:T(8,128)(2,1)S(1)}, bf16[2,40,128]{2,1,0:T(8,128)(2,1)S(1)}, u32[]{:S(2)}, u32[]{:S(2)}) collective-permute-start(bf16[2,40,128]{2,1,0:T(8,128)(2,1)S(1)} %get-tuple-element.33.refs_0_), channel_id=1, source_target_pairs={{0,6},{2,0},{4,2},{6,4},{1,7},{3,1},{5,3},{7,5},{8,14},{10,8},{12,... | collective-permute-start | bytes 61448 | tf_op jit(solution)/shard_map/ppermute | solution.py:498
  28.0 0.8 collective-permute-start.1
  28.8 0.9 collective-permute-start
  29.6 3.6 %collective-permute-done.1.refs_2_ = bf16[2,40,128]{2,1,0:T(8,128)(2,1)S(1)} collective-permute-done((bf16[2,40,128]{2,1,0:T(8,128)(2,1)S(1)}, bf16[2,40,128]{2,1,0:T(8,128)(2,1)S(1)}, u32[]{:S(2)}, u32[]{:S(2)}) %collective-permute-start.1) | collective-permute-done | bytes 20512 | tf_op jit(solution)/shard_map/ppermute | solution.py:498
  33.2 0.5 collective-permute-done.refs_1_
  33.7 1.3 %spread_codes.1 = bf16[2,16,4,40,128]{4,3,2,1,0:T(8,128)(2,1)} custom-call(bf16[2,40,128]{2,1,0:T(8,128)(2,1)S(1)} %get-tuple-element.33.refs_0_, bf16[2,40,128]{2,1,0:T(8,128)(2,1)S(1)} %collective-permute-done.refs_1_, bf16[2,40,128]{2,1,0:T(8,128)(2,1)S(1)} %collective-permute-done.1.refs_2_, bf16[2,40,128]{2,1,0:T(8,128)(2,1)S(1)} %collective-permute-done.2.refs_3_), custom_call_target="tpu_custom_call" | custom-call | flops 1000000 | bytes 2000000 | tf_op jit(solution)/shard_map/spread_codes/pallas_call | solution.py:166
  35.0 4.1 %all-to-all-start.1 = ((bf16[32,160,128]{2,1,0:T(8,128)(2,1)}), bf16[32,160,128]{2,1,0:T(8,128)(2,1)S(1)}, u32[]{:S(2)}, u32[]{:S(2)}) async-start(bf16[32,160,128]{2,1,0:T(8,128)(2,1)} %bitcast.7), calls=%async_computation.1 | async-start | bytes 2621440 | tf_op jit(solution)/shard_map/all_to_all | solution.py:503
  39.2 0.1 collective-permute-start.3
  39.3 1.8 %collective-permute-start.4 = (bf16[128,1024]{1,0:T(8,128)(2,1)S(1)}, bf16[128,1024]{1,0:T(8,128)(2,1)S(1)}, u32[]{:S(2)}, u32[]{:S(2)}) collective-permute-start(bf16[128,1024]{1,0:T(8,128)(2,1)S(1)} %copy-done.14), channel_id=1, source_target_pairs={{0,4},{2,6},{4,0},{6,2},{1,5},{3,7},{5,1},{7,3},{8,12},{10,14},{12... | collective-permute-start | bytes 786440 | tf_op jit(solution)/shard_map/ppermute | solution.py:498
  41.0 2.4 %collective-permute-start.5 = (bf16[128,1024]{1,0:T(8,128)(2,1)S(1)}, bf16[128,1024]{1,0:T(8,128)(2,1)S(1)}, u32[]{:S(2)}, u32[]{:S(2)}) collective-permute-start(bf16[128,1024]{1,0:T(8,128)(2,1)S(1)} %copy-done.13), channel_id=1, source_target_pairs={{0,6},{2,0},{4,2},{6,4},{1,7},{3,1},{5,3},{7,5},{8,14},{10,8},{12,... | collective-permute-start | bytes 786440 | tf_op jit(solution)/shard_map/ppermute | solution.py:498
  43.4 11.2 %collective-permute-done.3.rest_1_ = bf16[128,1024]{1,0:T(8,128)(2,1)S(1)} collective-permute-done((bf16[128,1024]{1,0:T(8,128)(2,1)S(1)}, bf16[128,1024]{1,0:T(8,128)(2,1)S(1)}, u32[]{:S(2)}, u32[]{:S(2)}) %collective-permute-start.3) | collective-permute-done | bytes 262176 | tf_op jit(solution)/shard_map/ppermute | solution.py:498
  54.6 0.0 copy-start.17
  54.6 0.5 collective-permute-start.8
  55.1 0.1 collective-permute-done.5.rest_3_
  55.2 0.9 collective-permute-done.7.rest_5_
  56.1 0.4 collective-permute-done.8.rest_6_
  56.5 0.4 collective-permute-done.9.rest_7_
  56.8 2.6 %all-to-all-done.1 = bf16[32,160,128]{2,1,0:T(8,128)(2,1)S(1)} async-done(((bf16[32,160,128]{2,1,0:T(8,128)(2,1)}), bf16[32,160,128]{2,1,0:T(8,128)(2,1)S(1)}, u32[]{:S(2)}, u32[]{:S(2)}) %all-to-all-start.1) | async-done | bytes 1310752 | tf_op jit(solution)/shard_map/all_to_all | solution.py:503
  59.5 1.0 copy-done.10
  60.5 7.8 %residue_part.1 = (bf16[2,16,4,40,128]{4,3,2,1,0:T(8,128)(2,1)}, bf16[4,128,1024]{2,1,0:T(8,128)(2,1)}, bf16[4,128,1024]{2,1,0:T(8,128)(2,1)}) custom-call(bf16[2,16,4,40,128]{4,3,2,1,0:T(8,128)(2,1)} %bitcast.39, bf16[640,1024]{1,0:T(8,128)(2,1)} %get-tuple-element.34.acts_ref, bf16[128,1024]{1,0:T(8,128)(2,1)} %get-tuple-element.35.rest_0_, ...), custom_call_target="tpu_custom_call" | custom-call | flops 4026531840 | bytes 10000000 | tf_op jit(solution)/shard_map/residue_part/pallas_call | solution.py:229
  68.3 0.1 collective-permute-start.13
  68.4 4.9 %all-to-all-start.2 = ((bf16[32,160,128]{2,1,0:T(8,128)(2,1)}), bf16[32,160,128]{2,1,0:T(8,128)(2,1)S(1)}, u32[]{:S(2)}, u32[]{:S(2)}) async-start(bf16[32,160,128]{2,1,0:T(8,128)(2,1)} %bitcast.40), calls=%async_computation.2 | async-start | bytes 2621440 | tf_op jit(solution)/shard_map/all_to_all | solution.py:503
  73.4 1.0 copy-done.7
  74.3 1.2 copy-done.6
  75.5 1.2 copy-done.8
  76.8 1.0 join_halves.1
  77.8 0.7 copy-done.4
  78.5 2.5 %collective-permute-start.14 = (bf16[128,1024]{1,0:T(8,128)(2,1)}, bf16[128,1024]{1,0:T(8,128)(2,1)}, u32[]{:S(2)}, u32[]{:S(2)}) collective-permute-start(bf16[128,1024]{1,0:T(8,128)(2,1)} %get-tuple-element.48), channel_id=1, source_target_pairs={{0,6},{2,0},{4,2},{6,4},{1,7},{3,1},{5,3},{7,5},{8,14},{10,8},{12,... | collective-permute-start | bytes 786440 | tf_op jit(solution)/shard_map/ppermute | solution.py:498
  81.0 0.3 collective-permute-start.15
  81.3 0.6 collective-permute-start.16
  81.8 11.8 %all-to-all-done.2 = bf16[32,160,128]{2,1,0:T(8,128)(2,1)S(1)} async-done(((bf16[32,160,128]{2,1,0:T(8,128)(2,1)}), bf16[32,160,128]{2,1,0:T(8,128)(2,1)S(1)}, u32[]{:S(2)}, u32[]{:S(2)}) %all-to-all-start.2) | async-done | bytes 1310752 | tf_op jit(solution)/shard_map/all_to_all | solution.py:503
  93.6 0.2 sum_layers.1
  93.8 2.6 %collective-permute-start.10 = (bf16[2,40,128]{2,1,0:T(8,128)(2,1)S(1)}, bf16[2,40,128]{2,1,0:T(8,128)(2,1)S(1)}, u32[]{:S(2)}, u32[]{:S(2)}) collective-permute-start(bf16[2,40,128]{2,1,0:T(8,128)(2,1)S(1)} %get-tuple-element.41), channel_id=1, source_target_pairs={{0,6},{2,0},{4,2},{6,4},{1,7},{3,1},{5,3},{7,5},{8,14},{10,8},{12,... | collective-permute-start | bytes 61448 | tf_op jit(solution)/shard_map/ppermute | solution.py:498
  96.3 0.3 collective-permute-start.11
  96.7 0.8 collective-permute-start.12
  97.5 0.1 pad_add_fusion.place_ref
  97.6 3.5 %decoder_size.1.rms_ref = f32[8,128]{1,0:T(8,128)S(1)} custom-call(s32[2]{0:T(128)S(1)} %pad_add_fusion.place_ref, bf16[128,1024]{1,0:T(8,128)(2,1)S(1)} %copy-done.5, bf16[128,1024]{1,0:T(8,128)(2,1)} %collective-permute-done.14.refs_1_, bf16[128,1024]{1,0:T(8,128)(2,1)} %collective-permute-done.15.refs_2_, ...), custom_call_target="tpu_custom_call" | custom-call | flops 10485760 | bytes 4000000 | tf_op jit(solution)/shard_map/decoder_size/pallas_call | solution.py:307
  101.2 0.5 collective-permute-done.11.two_ref
  101.7 0.2 collective-permute-done.12.three_ref
  101.9 0.8 make_grad_pre.1
  102.6 5.1 %all-to-all-start.3 = ((bf16[16,96,128]{2,1,0:T(8,128)(2,1)}), bf16[16,96,128]{2,1,0:T(8,128)(2,1)S(1)}, u32[]{:S(2)}, u32[]{:S(2)}) async-start(bf16[16,96,128]{2,1,0:T(8,128)(2,1)} %make_grad_pre.1), calls=%async_computation.3 | async-start | bytes 786432 | tf_op jit(solution)/shard_map/all_to_all | solution.py:503
  107.7 4.8 %decoder_adam.1 = (bf16[128,4096]{1,0:T(8,128)(2,1)}, bf16[128,4096]{1,0:T(8,128)(2,1)}, f32[128,4096]{1,0:T(8,128)}) custom-call(s32[2]{0:T(128)} %copy-done.9, bf16[128,1024]{1,0:T(8,128)(2,1)} %copy-done.4, bf16[128,1024]{1,0:T(8,128)(2,1)} %collective-permute-done.14.refs_1_, bf16[128,1024]{1,0:T(8,128)(2,1)} %collective-permute-done.15.refs_2_, ...), custom_call_target="tpu_custom_call" | custom-call | flops 10485760 | bytes 8000000 | tf_op jit(solution)/shard_map/decoder_adam/pallas_call | solution.py:339
  112.5 4.9 %all-to-all-done.3.got_ref = bf16[16,96,128]{2,1,0:T(8,128)(2,1)S(1)} async-done(((bf16[16,96,128]{2,1,0:T(8,128)(2,1)}), bf16[16,96,128]{2,1,0:T(8,128)(2,1)S(1)}, u32[]{:S(2)}, u32[]{:S(2)}) %all-to-all-start.3) | async-done | bytes 393248 | tf_op jit(solution)/shard_map/all_to_all | solution.py:503
  117.4 9.0 %encoder_adam.1 = (bf16[4096,128]{1,0:T(8,128)(2,1)}, bf16[4096,128]{1,0:T(8,128)(2,1)}, bf16[4096,128]{1,0:T(8,128)(2,1)}, bf16[128,4096]{1,0:T(8,128)(2,1)}) custom-call(bf16[16,96,128]{2,1,0:T(8,128)(2,1)S(1)} %all-to-all-done.3.got_ref, bf16[4096,128]{1,0:T(8,128)(2,1)S(1)} %bitcast.35, bf16[4096,128]{1,0:T(8,128)(2,1)} %bitcast.41, ...), custom_call_target="tpu_custom_call" | custom-call | flops 1342177280 | bytes 20000000 | tf_op jit(solution)/shard_map/encoder_adam/pallas_call | solution.py:471
  (53 shorter events, 0.2 us)
Async XLA Ops:
  0.6 15.2 %copy-start.11 = (s32[1280,128]{1,0:T(8,128)S(1)}, s32[1280,128]{1,0:T(8,128)}, u32[]{:S(2)}) copy-start(s32[1280,128]{1,0:T(8,128)} %param.9) | copy-start | bytes 1966084
  7.6 17.4 %all-to-all-start = ((bf16[16,80,128]{2,1,0:T(8,128)(2,1)}), bf16[16,80,128]{2,1,0:T(8,128)(2,1)S(1)}, u32[]{:S(2)}, u32[]{:S(2)}) async-start(bf16[16,80,128]{2,1,0:T(8,128)(2,1)} %bitcast.44), calls=%async_computation | async-start | bytes 655360 | tf_op jit(solution)/shard_map/all_to_all | solution.py:503
  25.1 4.5 %collective-permute-start.2 = (bf16[2,40,128]{2,1,0:T(8,128)(2,1)S(1)}, bf16[2,40,128]{2,1,0:T(8,128)(2,1)S(1)}, u32[]{:S(2)}, u32[]{:S(2)}) collective-permute-start(bf16[2,40,128]{2,1,0:T(8,128)(2,1)S(1)} %get-tuple-element.33.refs_0_), channel_id=1, source_target_pairs={{0,6},{2,0},{4,2},{6,4},{1,7},{3,1},{5,3},{7,5},{8,14},{10,8},{12,... | collective-permute-start | bytes 61448 | tf_op jit(solution)/shard_map/ppermute | solution.py:498
  28.0 5.3 %collective-permute-start.1 = (bf16[2,40,128]{2,1,0:T(8,128)(2,1)S(1)}, bf16[2,40,128]{2,1,0:T(8,128)(2,1)S(1)}, u32[]{:S(2)}, u32[]{:S(2)}) collective-permute-start(bf16[2,40,128]{2,1,0:T(8,128)(2,1)S(1)} %get-tuple-element.33.refs_0_), channel_id=1, source_target_pairs={{0,4},{2,6},{4,0},{6,2},{1,5},{3,7},{5,1},{7,3},{8,12},{10,14},{12... | collective-permute-start | bytes 61448 | tf_op jit(solution)/shard_map/ppermute | solution.py:498
  28.8 5.0 %collective-permute-start = (bf16[2,40,128]{2,1,0:T(8,128)(2,1)S(1)}, bf16[2,40,128]{2,1,0:T(8,128)(2,1)S(1)}, u32[]{:S(2)}, u32[]{:S(2)}) collective-permute-start(bf16[2,40,128]{2,1,0:T(8,128)(2,1)S(1)} %get-tuple-element.33.refs_0_), channel_id=1, source_target_pairs={{0,2},{2,4},{4,6},{6,0},{1,3},{3,5},{5,7},{7,1},{8,10},{10,12},{12... | collective-permute-start | bytes 61448 | tf_op jit(solution)/shard_map/ppermute | solution.py:498
  35.0 4.1 %copy-start.15 = (bf16[128,1024]{1,0:T(8,128)(2,1)S(1)}, bf16[128,1024]{1,0:T(8,128)(2,1)}, u32[]{:S(2)}) copy-start(bf16[128,1024]{1,0:T(8,128)(2,1)} %get-tuple-element.36) | copy-start | bytes 786436
  35.0 4.2 %copy-start.14 = (bf16[128,1024]{1,0:T(8,128)(2,1)S(1)}, bf16[128,1024]{1,0:T(8,128)(2,1)}, u32[]{:S(2)}) copy-start(bf16[128,1024]{1,0:T(8,128)(2,1)} %get-tuple-element.37) | copy-start | bytes 786436
  35.0 6.0 %copy-start.13 = (bf16[128,1024]{1,0:T(8,128)(2,1)S(1)}, bf16[128,1024]{1,0:T(8,128)(2,1)}, u32[]{:S(2)}) copy-start(bf16[128,1024]{1,0:T(8,128)(2,1)} %get-tuple-element.38) | copy-start | bytes 786436
  35.0 8.4 %copy-start.12 = (bf16[128,1024]{1,0:T(8,128)(2,1)S(1)}, bf16[128,1024]{1,0:T(8,128)(2,1)}, u32[]{:S(2)}) copy-start(bf16[128,1024]{1,0:T(8,128)(2,1)} %get-tuple-element.35.rest_0_) | copy-start | bytes 786436
  35.0 24.4 %all-to-all-start.1 = ((bf16[32,160,128]{2,1,0:T(8,128)(2,1)}), bf16[32,160,128]{2,1,0:T(8,128)(2,1)S(1)}, u32[]{:S(2)}, u32[]{:S(2)}) async-start(bf16[32,160,128]{2,1,0:T(8,128)(2,1)} %bitcast.7), calls=%async_computation.1 | async-start | bytes 2621440 | tf_op jit(solution)/shard_map/all_to_all | solution.py:503
  39.2 15.4 %collective-permute-start.3 = (bf16[128,1024]{1,0:T(8,128)(2,1)S(1)}, bf16[128,1024]{1,0:T(8,128)(2,1)S(1)}, u32[]{:S(2)}, u32[]{:S(2)}) collective-permute-start(bf16[128,1024]{1,0:T(8,128)(2,1)S(1)} %copy-done.15), channel_id=1, source_target_pairs={{0,2},{2,4},{4,6},{6,0},{1,3},{3,5},{5,7},{7,1},{8,10},{10,12},{12... | collective-permute-start | bytes 786440 | tf_op jit(solution)/shard_map/ppermute | solution.py:498
  39.3 15.3 %collective-permute-start.4 = (bf16[128,1024]{1,0:T(8,128)(2,1)S(1)}, bf16[128,1024]{1,0:T(8,128)(2,1)S(1)}, u32[]{:S(2)}, u32[]{:S(2)}) collective-permute-start(bf16[128,1024]{1,0:T(8,128)(2,1)S(1)} %copy-done.14), channel_id=1, source_target_pairs={{0,4},{2,6},{4,0},{6,2},{1,5},{3,7},{5,1},{7,3},{8,12},{10,14},{12... | collective-permute-start | bytes 786440 | tf_op jit(solution)/shard_map/ppermute | solution.py:498
  41.0 14.2 %collective-permute-start.5 = (bf16[128,1024]{1,0:T(8,128)(2,1)S(1)}, bf16[128,1024]{1,0:T(8,128)(2,1)S(1)}, u32[]{:S(2)}, u32[]{:S(2)}) collective-permute-start(bf16[128,1024]{1,0:T(8,128)(2,1)S(1)} %copy-done.13), channel_id=1, source_target_pairs={{0,6},{2,0},{4,2},{6,4},{1,7},{3,1},{5,3},{7,5},{8,14},{10,8},{12,... | collective-permute-start | bytes 786440 | tf_op jit(solution)/shard_map/ppermute | solution.py:498
  43.4 11.8 %collective-permute-start.6 = (bf16[128,1024]{1,0:T(8,128)(2,1)S(1)}, bf16[128,1024]{1,0:T(8,128)(2,1)S(1)}, u32[]{:S(2)}, u32[]{:S(2)}) collective-permute-start(bf16[128,1024]{1,0:T(8,128)(2,1)S(1)} %copy-done.12), channel_id=1, source_target_pairs={{0,1},{1,0},{2,3},{3,2},{4,5},{5,4},{6,7},{7,6},{8,9},{9,8},{10,11... | collective-permute-start | bytes 786440 | tf_op jit(solution)/shard_map/ppermute | solution.py:494
  54.6 4.9 %copy-start.16 = (bf16[128,1024]{1,0:T(8,128)(2,1)}, bf16[128,1024]{1,0:T(8,128)(2,1)S(1)}, u32[]{:S(2)}) copy-start(bf16[128,1024]{1,0:T(8,128)(2,1)S(1)} %collective-permute-done.3.rest_1_) | copy-start | bytes 786436
  54.6 1.5 %collective-permute-start.7 = (bf16[128,1024]{1,0:T(8,128)(2,1)S(1)}, bf16[128,1024]{1,0:T(8,128)(2,1)S(1)}, u32[]{:S(2)}, u32[]{:S(2)}) collective-permute-start(bf16[128,1024]{1,0:T(8,128)(2,1)S(1)} %collective-permute-done.3.rest_1_), channel_id=1, source_target_pairs={{0,1},{1,0},{2,3},{3,2},{4,5},{5,4},{6,7},{7,6},{8,9},{9,8},{10,11... | collective-permute-start | bytes 786440 | tf_op jit(solution)/shard_map/ppermute | solution.py:494
  54.6 4.9 %copy-start.17 = (bf16[128,1024]{1,0:T(8,128)(2,1)}, bf16[128,1024]{1,0:T(8,128)(2,1)S(1)}, u32[]{:S(2)}) copy-start(bf16[128,1024]{1,0:T(8,128)(2,1)S(1)} %collective-permute-done.4.rest_2_) | copy-start | bytes 786436
  54.6 1.9 %collective-permute-start.8 = (bf16[128,1024]{1,0:T(8,128)(2,1)S(1)}, bf16[128,1024]{1,0:T(8,128)(2,1)S(1)}, u32[]{:S(2)}, u32[]{:S(2)}) collective-permute-start(bf16[128,1024]{1,0:T(8,128)(2,1)S(1)} %collective-permute-done.4.rest_2_), channel_id=1, source_target_pairs={{0,1},{1,0},{2,3},{3,2},{4,5},{5,4},{6,7},{7,6},{8,9},{9,8},{10,11... | collective-permute-start | bytes 786440 | tf_op jit(solution)/shard_map/ppermute | solution.py:494
  55.2 4.2 %copy-start.18 = (bf16[128,1024]{1,0:T(8,128)(2,1)}, bf16[128,1024]{1,0:T(8,128)(2,1)S(1)}, u32[]{:S(2)}) copy-start(bf16[128,1024]{1,0:T(8,128)(2,1)S(1)} %collective-permute-done.5.rest_3_) | copy-start | bytes 786436
  55.2 1.7 %collective-permute-start.9 = (bf16[128,1024]{1,0:T(8,128)(2,1)S(1)}, bf16[128,1024]{1,0:T(8,128)(2,1)S(1)}, u32[]{:S(2)}, u32[]{:S(2)}) collective-permute-start(bf16[128,1024]{1,0:T(8,128)(2,1)S(1)} %collective-permute-done.5.rest_3_), channel_id=1, source_target_pairs={{0,1},{1,0},{2,3},{3,2},{4,5},{5,4},{6,7},{7,6},{8,9},{9,8},{10,11... | collective-permute-start | bytes 786440 | tf_op jit(solution)/shard_map/ppermute | solution.py:494
  55.2 4.2 %copy-start.19 = (bf16[128,1024]{1,0:T(8,128)(2,1)}, bf16[128,1024]{1,0:T(8,128)(2,1)S(1)}, u32[]{:S(2)}) copy-start(bf16[128,1024]{1,0:T(8,128)(2,1)S(1)} %collective-permute-done.6.rest_4_) | copy-start | bytes 786436
  56.1 3.3 %copy-start.20 = (bf16[128,1024]{1,0:T(8,128)(2,1)}, bf16[128,1024]{1,0:T(8,128)(2,1)S(1)}, u32[]{:S(2)}) copy-start(bf16[128,1024]{1,0:T(8,128)(2,1)S(1)} %collective-permute-done.7.rest_5_) | copy-start | bytes 786436
  56.5 3.0 %copy-start.21 = (bf16[128,1024]{1,0:T(8,128)(2,1)}, bf16[128,1024]{1,0:T(8,128)(2,1)S(1)}, u32[]{:S(2)}) copy-start(bf16[128,1024]{1,0:T(8,128)(2,1)S(1)} %collective-permute-done.8.rest_6_) | copy-start | bytes 786436
  56.8 2.6 %copy-start.22 = (bf16[128,1024]{1,0:T(8,128)(2,1)}, bf16[128,1024]{1,0:T(8,128)(2,1)S(1)}, u32[]{:S(2)}) copy-start(bf16[128,1024]{1,0:T(8,128)(2,1)S(1)} %collective-permute-done.9.rest_7_) | copy-start | bytes 786436
  59.4 1.1 copy-start.10
  68.3 5.0 %collective-permute-start.13 = (bf16[4,128,1024]{2,1,0:T(8,128)(2,1)}, bf16[4,128,1024]{2,1,0:T(8,128)(2,1)S(1)}, u32[]{:S(2)}, u32[]{:S(2)}) collective-permute-start(bf16[4,128,1024]{2,1,0:T(8,128)(2,1)} %get-tuple-element.46), channel_id=1, source_target_pairs={{0,1},{1,0},{2,3},{3,2},{4,5},{5,4},{6,7},{7,6},{8,9},{9,8},{10,11... | collective-permute-start | bytes 3145736 | tf_op jit(solution)/shard_map/ppermute | solution.py:494
  68.4 25.2 %all-to-all-start.2 = ((bf16[32,160,128]{2,1,0:T(8,128)(2,1)}), bf16[32,160,128]{2,1,0:T(8,128)(2,1)S(1)}, u32[]{:S(2)}, u32[]{:S(2)}) async-start(bf16[32,160,128]{2,1,0:T(8,128)(2,1)} %bitcast.40), calls=%async_computation.2 | async-start | bytes 2621440 | tf_op jit(solution)/shard_map/all_to_all | solution.py:503
  73.3 1.0 copy-start.7
  74.3 1.2 copy-start.6
  75.5 1.2 copy-start.8
  76.8 20.8 %copy-start = (bf16[128,1,4096]{2,0,1:T(8,128)(2,1)S(1)}, bf16[128,1,4096]{2,0,1:T(8,128)(2,1)}, u32[]{:S(2)}) copy-start(bf16[128,1,4096]{2,0,1:T(8,128)(2,1)} %param.13) | copy-start | bytes 3145732
  76.8 20.8 %copy-start.1 = (bf16[128,1,4096]{2,0,1:T(8,128)(2,1)S(1)}, bf16[128,1,4096]{2,0,1:T(8,128)(2,1)}, u32[]{:S(2)}) copy-start(bf16[128,1,4096]{2,0,1:T(8,128)(2,1)} %param.14) | copy-start | bytes 3145732
  77.7 0.7 copy-start.4
  78.5 18.2 %collective-permute-start.14 = (bf16[128,1024]{1,0:T(8,128)(2,1)}, bf16[128,1024]{1,0:T(8,128)(2,1)}, u32[]{:S(2)}, u32[]{:S(2)}) collective-permute-start(bf16[128,1024]{1,0:T(8,128)(2,1)} %get-tuple-element.48), channel_id=1, source_target_pairs={{0,6},{2,0},{4,2},{6,4},{1,7},{3,1},{5,3},{7,5},{8,14},{10,8},{12,... | collective-permute-start | bytes 786440 | tf_op jit(solution)/shard_map/ppermute | solution.py:498
  81.0 16.6 %collective-permute-start.15 = (bf16[128,1024]{1,0:T(8,128)(2,1)}, bf16[128,1024]{1,0:T(8,128)(2,1)}, u32[]{:S(2)}, u32[]{:S(2)}) collective-permute-start(bf16[128,1024]{1,0:T(8,128)(2,1)} %get-tuple-element.49), channel_id=1, source_target_pairs={{0,4},{2,6},{4,0},{6,2},{1,5},{3,7},{5,1},{7,3},{8,12},{10,14},{12... | collective-permute-start | bytes 786440 | tf_op jit(solution)/shard_map/ppermute | solution.py:498
  81.3 16.3 %collective-permute-start.16 = (bf16[128,1024]{1,0:T(8,128)(2,1)}, bf16[128,1024]{1,0:T(8,128)(2,1)}, u32[]{:S(2)}, u32[]{:S(2)}) collective-permute-start(bf16[128,1024]{1,0:T(8,128)(2,1)} %get-tuple-element.50), channel_id=1, source_target_pairs={{0,2},{2,4},{4,6},{6,0},{1,3},{3,5},{5,7},{7,1},{8,10},{10,12},{12... | collective-permute-start | bytes 786440 | tf_op jit(solution)/shard_map/ppermute | solution.py:498
  93.6 4.0 %copy-start.2 = (bf16[128,1,4096]{2,0,1:T(8,128)(2,1)S(1)}, bf16[128,1,4096]{2,0,1:T(8,128)(2,1)}, u32[]{:S(2)}) copy-start(bf16[128,1,4096]{2,0,1:T(8,128)(2,1)} %param.15) | copy-start | bytes 3145732
  93.6 4.0 %copy-start.5 = (bf16[128,1024]{1,0:T(8,128)(2,1)S(1)}, bf16[128,1024]{1,0:T(8,128)(2,1)}, u32[]{:S(2)}) copy-start(bf16[128,1024]{1,0:T(8,128)(2,1)} %copy-done.4) | copy-start | bytes 786436
  93.8 7.4 %collective-permute-start.10 = (bf16[2,40,128]{2,1,0:T(8,128)(2,1)S(1)}, bf16[2,40,128]{2,1,0:T(8,128)(2,1)S(1)}, u32[]{:S(2)}, u32[]{:S(2)}) collective-permute-start(bf16[2,40,128]{2,1,0:T(8,128)(2,1)S(1)} %get-tuple-element.41), channel_id=1, source_target_pairs={{0,6},{2,0},{4,2},{6,4},{1,7},{3,1},{5,3},{7,5},{8,14},{10,8},{12,... | collective-permute-start | bytes 61448 | tf_op jit(solution)/shard_map/ppermute | solution.py:498
  96.3 5.3 %collective-permute-start.11 = (bf16[2,40,128]{2,1,0:T(8,128)(2,1)S(1)}, bf16[2,40,128]{2,1,0:T(8,128)(2,1)S(1)}, u32[]{:S(2)}, u32[]{:S(2)}) collective-permute-start(bf16[2,40,128]{2,1,0:T(8,128)(2,1)S(1)} %get-tuple-element.42), channel_id=1, source_target_pairs={{0,4},{2,6},{4,0},{6,2},{1,5},{3,7},{5,1},{7,3},{8,12},{10,14},{12... | collective-permute-start | bytes 61448 | tf_op jit(solution)/shard_map/ppermute | solution.py:498
  96.7 5.2 %collective-permute-start.12 = (bf16[2,40,128]{2,1,0:T(8,128)(2,1)S(1)}, bf16[2,40,128]{2,1,0:T(8,128)(2,1)S(1)}, u32[]{:S(2)}, u32[]{:S(2)}) collective-permute-start(bf16[2,40,128]{2,1,0:T(8,128)(2,1)S(1)} %get-tuple-element.43), channel_id=1, source_target_pairs={{0,2},{2,4},{4,6},{6,0},{1,3},{3,5},{5,7},{7,1},{8,10},{10,12},{12... | collective-permute-start | bytes 61448 | tf_op jit(solution)/shard_map/ppermute | solution.py:498
  97.6 3.6 %copy-start.9 = (s32[2]{0:T(128)}, s32[2]{0:T(128)S(1)}, u32[]{:S(2)}) copy-start(s32[2]{0:T(128)S(1)} %pad_add_fusion.place_ref) | copy-start | bytes 28
  102.6 14.7 %all-to-all-start.3 = ((bf16[16,96,128]{2,1,0:T(8,128)(2,1)}), bf16[16,96,128]{2,1,0:T(8,128)(2,1)S(1)}, u32[]{:S(2)}, u32[]{:S(2)}) async-start(bf16[16,96,128]{2,1,0:T(8,128)(2,1)} %make_grad_pre.1), calls=%async_computation.3 | async-start | bytes 786432 | tf_op jit(solution)/shard_map/all_to_all | solution.py:503
  107.7 9.7 %copy-start.3 = (bf16[1,4096,128]{2,1,0:T(8,128)(2,1)S(1)}, bf16[1,4096,128]{2,1,0:T(8,128)(2,1)}, u32[]{:S(2)}) copy-start(bf16[1,4096,128]{2,1,0:T(8,128)(2,1)} %param.10) | copy-start | bytes 3145732

commit v5 on v4

--- a/solution.py
+++ b/solution.py
@@ -156,9 +156,9 @@
 
 def spread_kernel(*refs):
     out_ref = refs[NX]
-    for r in range(NX):
-        for half in range(2):
-            out_ref[half, :, r] = jnp.broadcast_to(refs[r][half][None], (LAYERS, SHARD, OWN))
+    for half in range(2):
+        rows = jnp.concatenate([refs[r][half].astype(f32) for r in range(NX)], axis=0).astype(bf16)
+        out_ref[half] = jnp.broadcast_to(rows[None], (LAYERS, NX * SHARD, OWN))
 
 
 def spread_codes(parts):
@@ -167,7 +167,7 @@
         spread_kernel,
         in_specs=[held] * NX,
         out_specs=held,
-        out_shape=jax.ShapeDtypeStruct((2, LAYERS, NX, SHARD, OWN), bf16),
+        out_shape=jax.ShapeDtypeStruct((2, LAYERS, NX * SHARD, OWN), bf16),
         compiler_params=params(16),
         cost_estimate=cost(1000000, 2000000),
         name="spread_codes",
@@ -178,15 +178,26 @@
 
 
 def residue_kernel(codes_ref, acts_ref, *rest):
+    pieces, rest = rest[:2 * NX], rest[2 * NX:]
+    share_ref, keep_ref, send_ref, got, acts, flat, cols, wide, share, halves, in_sems, out_sems = rest
     core = lax.axis_index("core")
     order = (core, 1 - core)
-    pieces, rest = rest[:2 * NX], rest[2 * NX:]
-    share_ref, keep_ref, send_ref, flat, cols, wide, share, halves, out_sems = rest
-    for r in range(NX):
-        for rel in range(2):
-            part = codes_ref[order[rel], :, r].astype(f32)
-            flat[rel, :, r * OWN:(r + 1) * OWN] = part.reshape(HALF, OWN).astype(bf16)
-            cols[rel, r * OWN:(r + 1) * OWN, :] = pieces[NX * rel + r][...]
+    fetch_codes = [pltpu.make_async_copy(codes_ref.at[order[rel]], got.at[rel], in_sems.at[rel]) for rel in range(2)]
+    fetch_rest = [pltpu.make_async_copy(acts_ref, acts, in_sems.at[2])]
+    for rel in range(2):
+        for r in range(NX):
+            rows = cols.at[rel, pl.ds(r * OWN, OWN)]
+            fetch_rest.append(pltpu.make_async_copy(pieces[NX * rel + r], rows, in_sems.at[3 + NX * rel + r]))
+    for copy in fetch_codes + fetch_rest:
+        copy.start()
+    for rel in range(2):
+        fetch_codes[rel].wait()
+        part = got[rel].astype(f32)
+        for r in range(NX):
+            rows = part[:, r * SHARD:(r + 1) * SHARD].reshape(HALF, OWN)
+            flat[rel, :, r * OWN:(r + 1) * OWN] = rows.astype(bf16)
+    for copy in fetch_rest:
+        copy.wait()
     stores = [
         pltpu.make_async_copy(share, share_ref, out_sems.at[0]),
         pltpu.make_async_copy(halves.at[1], send_ref, out_sems.at[1]),
@@ -196,19 +207,13 @@
         block = slice(c * COLUMNS, (c + 1) * COLUMNS)
         rebuilt = jnp.dot(flat[0], cols[0, :, block], preferred_element_type=f32)
         rebuilt += jnp.dot(flat[1], cols[1, :, block], preferred_element_type=f32)
-        wide[:, block] = (rebuilt * DEC_SCALE - acts_ref[:, block].astype(f32)).astype(bf16)
-    for pair in range(NX // 2):
-        span = slice(2 * pair * OWN, 2 * (pair + 1) * OWN)
-        grads = [
-            lax.dot_general(
-                wide[...], cols[rel, span, :], (((1,), (1,)), ((), ())), preferred_element_type=f32
-            ) * DEC_SCALE
-            for rel in range(2)
-        ]
-        for i in range(2):
-            for rel in range(2):
-                part = grads[rel][:, i * OWN:(i + 1) * OWN].reshape(LAYERS, SHARD, OWN)
-                share[order[rel], :, 2 * pair + i] = part.astype(bf16)
+        wide[:, block] = (rebuilt * DEC_SCALE - acts[:, block].astype(f32)).astype(bf16)
+    for rel in range(2):
+        grad = lax.dot_general(
+            wide[...], cols[rel], (((1,), (1,)), ((), ())), preferred_element_type=f32
+        ) * DEC_SCALE
+        parts = [grad[:, r * OWN:(r + 1) * OWN].reshape(LAYERS, SHARD, OWN) for r in range(NX)]
+        share[order[rel]] = jnp.concatenate(parts, axis=1).astype(bf16)
     stores[0].start()
     for i, rel in enumerate((1, 0)):
         for c in range(WIDE // COLUMNS):
@@ -224,26 +229,28 @@
 
 
 def residue_part(codes, acts, pieces):
-    held = pl.BlockSpec(memory_space=pltpu.VMEM)
     anywhere = pl.BlockSpec(memory_space=pl.ANY)
     return pl.pallas_call(
         residue_kernel,
-        in_specs=[held] * (2 + 2 * NX),
+        in_specs=[anywhere] * (2 + 2 * NX),
         out_specs=[anywhere] * 3,
         scratch_shapes=[
+            pltpu.VMEM((2, LAYERS, NX * SHARD, OWN), bf16),
+            pltpu.VMEM((HALF, WIDE), bf16),
             pltpu.VMEM((2, HALF, NX * OWN), bf16),
             pltpu.VMEM((2, NX * OWN, WIDE), bf16),
             pltpu.VMEM((HALF, WIDE), bf16),
-            pltpu.VMEM((2, LAYERS, NX, SHARD, OWN), bf16),
+            pltpu.VMEM((2, LAYERS, NX * SHARD, OWN), bf16),
             pltpu.VMEM((2, NX, OWN, WIDE), bf16),
+            pltpu.SemaphoreType.DMA((3 + 2 * NX,)),
             pltpu.SemaphoreType.DMA((3,)),
         ],
         out_shape=[
-            jax.ShapeDtypeStruct((2, LAYERS, NX, SHARD, OWN), bf16),
+            jax.ShapeDtypeStruct((2, LAYERS, NX * SHARD, OWN), bf16),
             jax.ShapeDtypeStruct((NX, OWN, WIDE), bf16),
             jax.ShapeDtypeStruct((NX, OWN, WIDE), bf16),
         ],
-        compiler_params=params(58),
+        compiler_params=params(60),
         cost_estimate=cost(6 * HALF * LAT * WIDE, 10000000),
         name="residue_part",
     )(codes, acts, *pieces)
@@ -359,8 +366,9 @@
 
 
 def sum_kernel(got_ref, keep_ref, *outs):
+    whole = jnp.sum(got_ref[...].astype(f32), axis=1)
     for r in range(NX):
-        total = jnp.sum(got_ref[:, :, r].astype(f32), axis=1)
+        total = whole[:, r * SHARD:(r + 1) * SHARD]
         if r == 0:
             keep_ref[...] = total
         else:

time: 127 us -> 127 us (level)
  no operation moved by 1% of the time
where the time goes in v5:
time: 127 us
  waiting for transfers between devices  46.1 us (36%)
  starting transfers between devices  38.6 us (30%)
  Pallas kernels  35.5 us (28%)
  local copies, waits for them, and re-layouts  5.21 us (4%)
    all_to_all x4, waiting for transfers between devices, exchange(): lax.all_to_all(flat, axes, split_axis=0, concat_axis=0, tiled=True)  28.4 us
    all_to_all x4, starting transfers between devices, exchange(): lax.all_to_all(flat, axes, split_axis=0, concat_axis=0, tiled=True)  22.2 us
    ppermute x12, waiting for transfers between devices, shift(): return lax.ppermute(array, 'x', [(i, (i + steps) % NX) for i in range(NX)])  16.1 us
    ppermute x12, starting transfers between devices, shift(): return lax.ppermute(array, 'x', [(i, (i + steps) % NX) for i in range(NX)])  15.8 us
    pallas_call x1, Pallas kernels, encoder_adam(): pl.pallas_call(encoder_kernel, in_specs=[held] * 4 + [anywhere] * 2, out_...  9.02 us
    pallas_call x1, Pallas kernels, residue_part(): pl.pallas_call(residue_kernel, in_specs=[anywhere] * (2 + 2 * NX), out_sp...  7.88 us
    pallas_call x1, Pallas kernels, preact_share(): pl.pallas_call(preact_kernel, in_specs=[anywhere] * 3, out_specs=[pl.Bloc...  6.99 us
    unnamed x46, local copies, waits for them, and re-layouts  5.2 us
  transfers between devices with their start and end apart: 21, of which 13 were waited for; matrix products, arithmetic and copies ran while one was open for 0% of the time, Pallas kernels for 7%

profile of v5, /device:TPU:0, one launch (start us, length us, event | category | flops | bytes accessed | tf_op | source)
XLA Modules:
  0.0 126.6 jit_solution(16751307576532348028)
XLA Ops:
  0.6 7.0 %preact_share.1 = (bf16[16,2,40,128]{3,2,1,0:T(8,128)(2,1)}, bf16[128,1024]{1,0:T(8,128)(2,1)}, bf16[128,1024]{1,0:T(8,128)(2,1)}, bf16[128,1024]{1,0:T(8,128)(2...) custom-call(bf16[1280,4096]{1,0:T(8,128)(2,1)} %bitcast.37, bf16[4096,128]{1,0:T(8,128)(2,1)} %bitcast.34, ...), custom_call_target="tpu_custom_call" | custom-call | flops 1342177280 | bytes 10485760 | tf_op jit(solution)/shard_map/preact_share/pallas_call | solution.py:112
  7.6 8.1 %all-to-all-start = ((bf16[16,80,128]{2,1,0:T(8,128)(2,1)}), bf16[16,80,128]{2,1,0:T(8,128)(2,1)S(1)}, u32[]{:S(2)}, u32[]{:S(2)}) async-start(bf16[16,80,128]{2,1,0:T(8,128)(2,1)} %bitcast.44), calls=%async_computation | async-start | bytes 655360 | tf_op jit(solution)/shard_map/all_to_all | solution.py:511
  15.9 9.2 %all-to-all-done = bf16[16,80,128]{2,1,0:T(8,128)(2,1)S(1)} async-done(((bf16[16,80,128]{2,1,0:T(8,128)(2,1)}), bf16[16,80,128]{2,1,0:T(8,128)(2,1)S(1)}, u32[]{:S(2)}, u32[]{:S(2)}) %all-to-all-start) | async-done | bytes 327712 | tf_op jit(solution)/shard_map/all_to_all | solution.py:511
  25.1 0.1 make_codes.1
  25.1 2.8 %collective-permute-start.2 = (bf16[2,40,128]{2,1,0:T(8,128)(2,1)S(1)}, bf16[2,40,128]{2,1,0:T(8,128)(2,1)S(1)}, u32[]{:S(2)}, u32[]{:S(2)}) collective-permute-start(bf16[2,40,128]{2,1,0:T(8,128)(2,1)S(1)} %get-tuple-element.33.refs_0_), channel_id=1, source_target_pairs={{0,6},{2,0},{4,2},{6,4},{1,7},{3,1},{5,3},{7,5},{8,14},{10,8},{12,... | collective-permute-start | bytes 61448 | tf_op jit(solution)/shard_map/ppermute | solution.py:506
  28.0 0.8 collective-permute-start.1
  28.8 0.9 collective-permute-start
  29.6 3.6 %collective-permute-done.1.refs_2_ = bf16[2,40,128]{2,1,0:T(8,128)(2,1)S(1)} collective-permute-done((bf16[2,40,128]{2,1,0:T(8,128)(2,1)S(1)}, bf16[2,40,128]{2,1,0:T(8,128)(2,1)S(1)}, u32[]{:S(2)}, u32[]{:S(2)}) %collective-permute-start.1) | collective-permute-done | bytes 20512 | tf_op jit(solution)/shard_map/ppermute | solution.py:506
  33.2 0.5 collective-permute-done.refs_1_
  33.7 1.3 %spread_codes.1 = bf16[2,16,160,128]{3,2,1,0:T(8,128)(2,1)} custom-call(bf16[2,40,128]{2,1,0:T(8,128)(2,1)S(1)} %get-tuple-element.33.refs_0_, bf16[2,40,128]{2,1,0:T(8,128)(2,1)S(1)} %collective-permute-done.refs_1_, bf16[2,40,128]{2,1,0:T(8,128)(2,1)S(1)} %collective-permute-done.1.refs_2_, bf16[2,40,128]{2,1,0:T(8,128)(2,1)S(1)} %collective-permute-done.2.refs_3_), custom_call_target="tpu_custom_call" | custom-call | flops 1000000 | bytes 2000000 | tf_op jit(solution)/shard_map/spread_codes/pallas_call | solution.py:166
  35.0 4.1 %all-to-all-start.1 = ((bf16[32,160,128]{2,1,0:T(8,128)(2,1)}), bf16[32,160,128]{2,1,0:T(8,128)(2,1)S(1)}, u32[]{:S(2)}, u32[]{:S(2)}) async-start(bf16[32,160,128]{2,1,0:T(8,128)(2,1)} %bitcast.7), calls=%async_computation.1 | async-start | bytes 2621440 | tf_op jit(solution)/shard_map/all_to_all | solution.py:511
  39.2 0.1 collective-permute-start.3
  39.3 1.8 %collective-permute-start.4 = (bf16[128,1024]{1,0:T(8,128)(2,1)S(1)}, bf16[128,1024]{1,0:T(8,128)(2,1)S(1)}, u32[]{:S(2)}, u32[]{:S(2)}) collective-permute-start(bf16[128,1024]{1,0:T(8,128)(2,1)S(1)} %copy-done.14), channel_id=1, source_target_pairs={{0,4},{2,6},{4,0},{6,2},{1,5},{3,7},{5,1},{7,3},{8,12},{10,14},{12... | collective-permute-start | bytes 786440 | tf_op jit(solution)/shard_map/ppermute | solution.py:506
  41.0 2.4 %collective-permute-start.5 = (bf16[128,1024]{1,0:T(8,128)(2,1)S(1)}, bf16[128,1024]{1,0:T(8,128)(2,1)S(1)}, u32[]{:S(2)}, u32[]{:S(2)}) collective-permute-start(bf16[128,1024]{1,0:T(8,128)(2,1)S(1)} %copy-done.13), channel_id=1, source_target_pairs={{0,6},{2,0},{4,2},{6,4},{1,7},{3,1},{5,3},{7,5},{8,14},{10,8},{12,... | collective-permute-start | bytes 786440 | tf_op jit(solution)/shard_map/ppermute | solution.py:506
  43.4 11.2 %collective-permute-done.3.rest_1_ = bf16[128,1024]{1,0:T(8,128)(2,1)S(1)} collective-permute-done((bf16[128,1024]{1,0:T(8,128)(2,1)S(1)}, bf16[128,1024]{1,0:T(8,128)(2,1)S(1)}, u32[]{:S(2)}, u32[]{:S(2)}) %collective-permute-start.3) | collective-permute-done | bytes 262176 | tf_op jit(solution)/shard_map/ppermute | solution.py:506
  54.6 0.0 copy-start.17
  54.6 0.5 collective-permute-start.8
  55.1 0.1 collective-permute-done.5.rest_3_
  55.2 0.9 collective-permute-done.7.rest_5_
  56.1 0.4 collective-permute-done.8.rest_6_
  56.5 0.4 collective-permute-done.9.rest_7_
  56.8 2.6 %all-to-all-done.1 = bf16[32,160,128]{2,1,0:T(8,128)(2,1)S(1)} async-done(((bf16[32,160,128]{2,1,0:T(8,128)(2,1)}), bf16[32,160,128]{2,1,0:T(8,128)(2,1)S(1)}, u32[]{:S(2)}, u32[]{:S(2)}) %all-to-all-start.1) | async-done | bytes 1310752 | tf_op jit(solution)/shard_map/all_to_all | solution.py:511
  59.5 1.0 copy-done.10
  60.5 7.9 %residue_part.1 = (bf16[2,16,160,128]{3,2,1,0:T(8,128)(2,1)}, bf16[4,128,1024]{2,1,0:T(8,128)(2,1)}, bf16[4,128,1024]{2,1,0:T(8,128)(2,1)}) custom-call(bf16[2,16,160,128]{3,2,1,0:T(8,128)(2,1)} %bitcast.39, bf16[640,1024]{1,0:T(8,128)(2,1)} %get-tuple-element.34.acts_ref, bf16[128,1024]{1,0:T(8,128)(2,1)} %get-tuple-element.35.rest_0_, ...), custom_call_target="tpu_custom_call" | custom-call | flops 4026531840 | bytes 10000000 | tf_op jit(solution)/shard_map/residue_part/pallas_call | solution.py:233
  68.4 0.1 collective-permute-start.13
  68.5 4.9 %all-to-all-start.2 = ((bf16[32,160,128]{2,1,0:T(8,128)(2,1)}), bf16[32,160,128]{2,1,0:T(8,128)(2,1)S(1)}, u32[]{:S(2)}, u32[]{:S(2)}) async-start(bf16[32,160,128]{2,1,0:T(8,128)(2,1)} %bitcast.40), calls=%async_computation.2 | async-start | bytes 2621440 | tf_op jit(solution)/shard_map/all_to_all | solution.py:511
  73.4 1.0 copy-done.7
  74.4 1.2 copy-done.6
  75.6 1.2 copy-done.8
  76.8 1.0 join_halves.1
  77.8 0.7 copy-done.4
  78.5 2.5 %collective-permute-start.14 = (bf16[128,1024]{1,0:T(8,128)(2,1)}, bf16[128,1024]{1,0:T(8,128)(2,1)}, u32[]{:S(2)}, u32[]{:S(2)}) collective-permute-start(bf16[128,1024]{1,0:T(8,128)(2,1)} %get-tuple-element.48), channel_id=1, source_target_pairs={{0,6},{2,0},{4,2},{6,4},{1,7},{3,1},{5,3},{7,5},{8,14},{10,8},{12,... | collective-permute-start | bytes 786440 | tf_op jit(solution)/shard_map/ppermute | solution.py:506
  81.0 0.3 collective-permute-start.15
  81.3 0.6 collective-permute-start.16
  81.9 11.8 %all-to-all-done.2 = bf16[32,160,128]{2,1,0:T(8,128)(2,1)S(1)} async-done(((bf16[32,160,128]{2,1,0:T(8,128)(2,1)}), bf16[32,160,128]{2,1,0:T(8,128)(2,1)S(1)}, u32[]{:S(2)}, u32[]{:S(2)}) %all-to-all-start.2) | async-done | bytes 1310752 | tf_op jit(solution)/shard_map/all_to_all | solution.py:511
  93.7 0.2 sum_layers.1
  93.8 2.6 %collective-permute-start.10 = (bf16[2,40,128]{2,1,0:T(8,128)(2,1)S(1)}, bf16[2,40,128]{2,1,0:T(8,128)(2,1)S(1)}, u32[]{:S(2)}, u32[]{:S(2)}) collective-permute-start(bf16[2,40,128]{2,1,0:T(8,128)(2,1)S(1)} %get-tuple-element.41), channel_id=1, source_target_pairs={{0,6},{2,0},{4,2},{6,4},{1,7},{3,1},{5,3},{7,5},{8,14},{10,8},{12,... | collective-permute-start | bytes 61448 | tf_op jit(solution)/shard_map/ppermute | solution.py:506
  96.4 0.3 collective-permute-start.11
  96.7 0.8 collective-permute-start.12
  97.5 0.1 pad_add_fusion.place_ref
  97.7 3.5 %decoder_size.1.rms_ref = f32[8,128]{1,0:T(8,128)S(1)} custom-call(s32[2]{0:T(128)S(1)} %pad_add_fusion.place_ref, bf16[128,1024]{1,0:T(8,128)(2,1)S(1)} %copy-done.5, bf16[128,1024]{1,0:T(8,128)(2,1)} %collective-permute-done.14.refs_1_, bf16[128,1024]{1,0:T(8,128)(2,1)} %collective-permute-done.15.refs_2_, ...), custom_call_target="tpu_custom_call" | custom-call | flops 10485760 | bytes 4000000 | tf_op jit(solution)/shard_map/decoder_size/pallas_call | solution.py:314
  101.2 0.5 collective-permute-done.11.two_ref
  101.7 0.2 collective-permute-done.12.three_ref
  101.9 0.8 make_grad_pre.1
  102.7 5.1 %all-to-all-start.3 = ((bf16[16,96,128]{2,1,0:T(8,128)(2,1)}), bf16[16,96,128]{2,1,0:T(8,128)(2,1)S(1)}, u32[]{:S(2)}, u32[]{:S(2)}) async-start(bf16[16,96,128]{2,1,0:T(8,128)(2,1)} %make_grad_pre.1), calls=%async_computation.3 | async-start | bytes 786432 | tf_op jit(solution)/shard_map/all_to_all | solution.py:511
  107.8 4.8 %decoder_adam.1 = (bf16[128,4096]{1,0:T(8,128)(2,1)}, bf16[128,4096]{1,0:T(8,128)(2,1)}, f32[128,4096]{1,0:T(8,128)}) custom-call(s32[2]{0:T(128)} %copy-done.9, bf16[128,1024]{1,0:T(8,128)(2,1)} %copy-done.4, bf16[128,1024]{1,0:T(8,128)(2,1)} %collective-permute-done.14.refs_1_, bf16[128,1024]{1,0:T(8,128)(2,1)} %collective-permute-done.15.refs_2_, ...), custom_call_target="tpu_custom_call" | custom-call | flops 10485760 | bytes 8000000 | tf_op jit(solution)/shard_map/decoder_adam/pallas_call | solution.py:346
  112.6 4.9 %all-to-all-done.3.got_ref = bf16[16,96,128]{2,1,0:T(8,128)(2,1)S(1)} async-done(((bf16[16,96,128]{2,1,0:T(8,128)(2,1)}), bf16[16,96,128]{2,1,0:T(8,128)(2,1)S(1)}, u32[]{:S(2)}, u32[]{:S(2)}) %all-to-all-start.3) | async-done | bytes 393248 | tf_op jit(solution)/shard_map/all_to_all | solution.py:511
  117.5 9.0 %encoder_adam.1 = (bf16[4096,128]{1,0:T(8,128)(2,1)}, bf16[4096,128]{1,0:T(8,128)(2,1)}, bf16[4096,128]{1,0:T(8,128)(2,1)}, bf16[128,4096]{1,0:T(8,128)(2,1)}) custom-call(bf16[16,96,128]{2,1,0:T(8,128)(2,1)S(1)} %all-to-all-done.3.got_ref, bf16[4096,128]{1,0:T(8,128)(2,1)S(1)} %bitcast.35, bf16[4096,128]{1,0:T(8,128)(2,1)} %bitcast.41, ...), custom_call_target="tpu_custom_call" | custom-call | flops 1342177280 | bytes 20000000 | tf_op jit(solution)/shard_map/encoder_adam/pallas_call | solution.py:479
  (53 shorter events, 0.2 us)
Async XLA Ops:
  0.6 15.2 %copy-start.11 = (s32[1280,128]{1,0:T(8,128)S(1)}, s32[1280,128]{1,0:T(8,128)}, u32[]{:S(2)}) copy-start(s32[1280,128]{1,0:T(8,128)} %param.9) | copy-start | bytes 1966084
  7.6 17.4 %all-to-all-start = ((bf16[16,80,128]{2,1,0:T(8,128)(2,1)}), bf16[16,80,128]{2,1,0:T(8,128)(2,1)S(1)}, u32[]{:S(2)}, u32[]{:S(2)}) async-start(bf16[16,80,128]{2,1,0:T(8,128)(2,1)} %bitcast.44), calls=%async_computation | async-start | bytes 655360 | tf_op jit(solution)/shard_map/all_to_all | solution.py:511
  25.1 4.5 %collective-permute-start.2 = (bf16[2,40,128]{2,1,0:T(8,128)(2,1)S(1)}, bf16[2,40,128]{2,1,0:T(8,128)(2,1)S(1)}, u32[]{:S(2)}, u32[]{:S(2)}) collective-permute-start(bf16[2,40,128]{2,1,0:T(8,128)(2,1)S(1)} %get-tuple-element.33.refs_0_), channel_id=1, source_target_pairs={{0,6},{2,0},{4,2},{6,4},{1,7},{3,1},{5,3},{7,5},{8,14},{10,8},{12,... | collective-permute-start | bytes 61448 | tf_op jit(solution)/shard_map/ppermute | solution.py:506
  28.0 5.3 %collective-permute-start.1 = (bf16[2,40,128]{2,1,0:T(8,128)(2,1)S(1)}, bf16[2,40,128]{2,1,0:T(8,128)(2,1)S(1)}, u32[]{:S(2)}, u32[]{:S(2)}) collective-permute-start(bf16[2,40,128]{2,1,0:T(8,128)(2,1)S(1)} %get-tuple-element.33.refs_0_), channel_id=1, source_target_pairs={{0,4},{2,6},{4,0},{6,2},{1,5},{3,7},{5,1},{7,3},{8,12},{10,14},{12... | collective-permute-start | bytes 61448 | tf_op jit(solution)/shard_map/ppermute | solution.py:506
  28.8 5.0 %collective-permute-start = (bf16[2,40,128]{2,1,0:T(8,128)(2,1)S(1)}, bf16[2,40,128]{2,1,0:T(8,128)(2,1)S(1)}, u32[]{:S(2)}, u32[]{:S(2)}) collective-permute-start(bf16[2,40,128]{2,1,0:T(8,128)(2,1)S(1)} %get-tuple-element.33.refs_0_), channel_id=1, source_target_pairs={{0,2},{2,4},{4,6},{6,0},{1,3},{3,5},{5,7},{7,1},{8,10},{10,12},{12... | collective-permute-start | bytes 61448 | tf_op jit(solution)/shard_map/ppermute | solution.py:506
  35.0 4.1 %copy-start.15 = (bf16[128,1024]{1,0:T(8,128)(2,1)S(1)}, bf16[128,1024]{1,0:T(8,128)(2,1)}, u32[]{:S(2)}) copy-start(bf16[128,1024]{1,0:T(8,128)(2,1)} %get-tuple-element.36) | copy-start | bytes 786436
  35.0 4.2 %copy-start.14 = (bf16[128,1024]{1,0:T(8,128)(2,1)S(1)}, bf16[128,1024]{1,0:T(8,128)(2,1)}, u32[]{:S(2)}) copy-start(bf16[128,1024]{1,0:T(8,128)(2,1)} %get-tuple-element.37) | copy-start | bytes 786436
  35.0 6.0 %copy-start.13 = (bf16[128,1024]{1,0:T(8,128)(2,1)S(1)}, bf16[128,1024]{1,0:T(8,128)(2,1)}, u32[]{:S(2)}) copy-start(bf16[128,1024]{1,0:T(8,128)(2,1)} %get-tuple-element.38) | copy-start | bytes 786436
  35.0 8.4 %copy-start.12 = (bf16[128,1024]{1,0:T(8,128)(2,1)S(1)}, bf16[128,1024]{1,0:T(8,128)(2,1)}, u32[]{:S(2)}) copy-start(bf16[128,1024]{1,0:T(8,128)(2,1)} %get-tuple-element.35.rest_0_) | copy-start | bytes 786436
  35.0 24.4 %all-to-all-start.1 = ((bf16[32,160,128]{2,1,0:T(8,128)(2,1)}), bf16[32,160,128]{2,1,0:T(8,128)(2,1)S(1)}, u32[]{:S(2)}, u32[]{:S(2)}) async-start(bf16[32,160,128]{2,1,0:T(8,128)(2,1)} %bitcast.7), calls=%async_computation.1 | async-start | bytes 2621440 | tf_op jit(solution)/shard_map/all_to_all | solution.py:511
  39.2 15.4 %collective-permute-start.3 = (bf16[128,1024]{1,0:T(8,128)(2,1)S(1)}, bf16[128,1024]{1,0:T(8,128)(2,1)S(1)}, u32[]{:S(2)}, u32[]{:S(2)}) collective-permute-start(bf16[128,1024]{1,0:T(8,128)(2,1)S(1)} %copy-done.15), channel_id=1, source_target_pairs={{0,2},{2,4},{4,6},{6,0},{1,3},{3,5},{5,7},{7,1},{8,10},{10,12},{12... | collective-permute-start | bytes 786440 | tf_op jit(solution)/shard_map/ppermute | solution.py:506
  39.3 15.3 %collective-permute-start.4 = (bf16[128,1024]{1,0:T(8,128)(2,1)S(1)}, bf16[128,1024]{1,0:T(8,128)(2,1)S(1)}, u32[]{:S(2)}, u32[]{:S(2)}) collective-permute-start(bf16[128,1024]{1,0:T(8,128)(2,1)S(1)} %copy-done.14), channel_id=1, source_target_pairs={{0,4},{2,6},{4,0},{6,2},{1,5},{3,7},{5,1},{7,3},{8,12},{10,14},{12... | collective-permute-start | bytes 786440 | tf_op jit(solution)/shard_map/ppermute | solution.py:506
  41.0 14.2 %collective-permute-start.5 = (bf16[128,1024]{1,0:T(8,128)(2,1)S(1)}, bf16[128,1024]{1,0:T(8,128)(2,1)S(1)}, u32[]{:S(2)}, u32[]{:S(2)}) collective-permute-start(bf16[128,1024]{1,0:T(8,128)(2,1)S(1)} %copy-done.13), channel_id=1, source_target_pairs={{0,6},{2,0},{4,2},{6,4},{1,7},{3,1},{5,3},{7,5},{8,14},{10,8},{12,... | collective-permute-start | bytes 786440 | tf_op jit(solution)/shard_map/ppermute | solution.py:506
  43.4 11.8 %collective-permute-start.6 = (bf16[128,1024]{1,0:T(8,128)(2,1)S(1)}, bf16[128,1024]{1,0:T(8,128)(2,1)S(1)}, u32[]{:S(2)}, u32[]{:S(2)}) collective-permute-start(bf16[128,1024]{1,0:T(8,128)(2,1)S(1)} %copy-done.12), channel_id=1, source_target_pairs={{0,1},{1,0},{2,3},{3,2},{4,5},{5,4},{6,7},{7,6},{8,9},{9,8},{10,11... | collective-permute-start | bytes 786440 | tf_op jit(solution)/shard_map/ppermute | solution.py:502
  54.6 4.9 %copy-start.16 = (bf16[128,1024]{1,0:T(8,128)(2,1)}, bf16[128,1024]{1,0:T(8,128)(2,1)S(1)}, u32[]{:S(2)}) copy-start(bf16[128,1024]{1,0:T(8,128)(2,1)S(1)} %collective-permute-done.3.rest_1_) | copy-start | bytes 786436
  54.6 1.5 %collective-permute-start.7 = (bf16[128,1024]{1,0:T(8,128)(2,1)S(1)}, bf16[128,1024]{1,0:T(8,128)(2,1)S(1)}, u32[]{:S(2)}, u32[]{:S(2)}) collective-permute-start(bf16[128,1024]{1,0:T(8,128)(2,1)S(1)} %collective-permute-done.3.rest_1_), channel_id=1, source_target_pairs={{0,1},{1,0},{2,3},{3,2},{4,5},{5,4},{6,7},{7,6},{8,9},{9,8},{10,11... | collective-permute-start | bytes 786440 | tf_op jit(solution)/shard_map/ppermute | solution.py:502
  54.6 4.9 %copy-start.17 = (bf16[128,1024]{1,0:T(8,128)(2,1)}, bf16[128,1024]{1,0:T(8,128)(2,1)S(1)}, u32[]{:S(2)}) copy-start(bf16[128,1024]{1,0:T(8,128)(2,1)S(1)} %collective-permute-done.4.rest_2_) | copy-start | bytes 786436
  54.6 1.9 %collective-permute-start.8 = (bf16[128,1024]{1,0:T(8,128)(2,1)S(1)}, bf16[128,1024]{1,0:T(8,128)(2,1)S(1)}, u32[]{:S(2)}, u32[]{:S(2)}) collective-permute-start(bf16[128,1024]{1,0:T(8,128)(2,1)S(1)} %collective-permute-done.4.rest_2_), channel_id=1, source_target_pairs={{0,1},{1,0},{2,3},{3,2},{4,5},{5,4},{6,7},{7,6},{8,9},{9,8},{10,11... | collective-permute-start | bytes 786440 | tf_op jit(solution)/shard_map/ppermute | solution.py:502
  55.2 4.2 %copy-start.18 = (bf16[128,1024]{1,0:T(8,128)(2,1)}, bf16[128,1024]{1,0:T(8,128)(2,1)S(1)}, u32[]{:S(2)}) copy-start(bf16[128,1024]{1,0:T(8,128)(2,1)S(1)} %collective-permute-done.5.rest_3_) | copy-start | bytes 786436
  55.2 1.7 %collective-permute-start.9 = (bf16[128,1024]{1,0:T(8,128)(2,1)S(1)}, bf16[128,1024]{1,0:T(8,128)(2,1)S(1)}, u32[]{:S(2)}, u32[]{:S(2)}) collective-permute-start(bf16[128,1024]{1,0:T(8,128)(2,1)S(1)} %collective-permute-done.5.rest_3_), channel_id=1, source_target_pairs={{0,1},{1,0},{2,3},{3,2},{4,5},{5,4},{6,7},{7,6},{8,9},{9,8},{10,11... | collective-permute-start | bytes 786440 | tf_op jit(solution)/shard_map/ppermute | solution.py:502
  55.2 4.2 %copy-start.19 = (bf16[128,1024]{1,0:T(8,128)(2,1)}, bf16[128,1024]{1,0:T(8,128)(2,1)S(1)}, u32[]{:S(2)}) copy-start(bf16[128,1024]{1,0:T(8,128)(2,1)S(1)} %collective-permute-done.6.rest_4_) | copy-start | bytes 786436
  56.1 3.3 %copy-start.20 = (bf16[128,1024]{1,0:T(8,128)(2,1)}, bf16[128,1024]{1,0:T(8,128)(2,1)S(1)}, u32[]{:S(2)}) copy-start(bf16[128,1024]{1,0:T(8,128)(2,1)S(1)} %collective-permute-done.7.rest_5_) | copy-start | bytes 786436
  56.5 3.0 %copy-start.21 = (bf16[128,1024]{1,0:T(8,128)(2,1)}, bf16[128,1024]{1,0:T(8,128)(2,1)S(1)}, u32[]{:S(2)}) copy-start(bf16[128,1024]{1,0:T(8,128)(2,1)S(1)} %collective-permute-done.8.rest_6_) | copy-start | bytes 786436
  56.8 2.6 %copy-start.22 = (bf16[128,1024]{1,0:T(8,128)(2,1)}, bf16[128,1024]{1,0:T(8,128)(2,1)S(1)}, u32[]{:S(2)}) copy-start(bf16[128,1024]{1,0:T(8,128)(2,1)S(1)} %collective-permute-done.9.rest_7_) | copy-start | bytes 786436
  59.4 1.1 copy-start.10
  68.4 5.0 %collective-permute-start.13 = (bf16[4,128,1024]{2,1,0:T(8,128)(2,1)}, bf16[4,128,1024]{2,1,0:T(8,128)(2,1)S(1)}, u32[]{:S(2)}, u32[]{:S(2)}) collective-permute-start(bf16[4,128,1024]{2,1,0:T(8,128)(2,1)} %get-tuple-element.46), channel_id=1, source_target_pairs={{0,1},{1,0},{2,3},{3,2},{4,5},{5,4},{6,7},{7,6},{8,9},{9,8},{10,11... | collective-permute-start | bytes 3145736 | tf_op jit(solution)/shard_map/ppermute | solution.py:502
  68.5 25.2 %all-to-all-start.2 = ((bf16[32,160,128]{2,1,0:T(8,128)(2,1)}), bf16[32,160,128]{2,1,0:T(8,128)(2,1)S(1)}, u32[]{:S(2)}, u32[]{:S(2)}) async-start(bf16[32,160,128]{2,1,0:T(8,128)(2,1)} %bitcast.40), calls=%async_computation.2 | async-start | bytes 2621440 | tf_op jit(solution)/shard_map/all_to_all | solution.py:511
  73.4 1.0 copy-start.7
  74.4 1.2 copy-start.6
  75.6 1.2 copy-start.8
  76.8 20.8 %copy-start = (bf16[128,1,4096]{2,0,1:T(8,128)(2,1)S(1)}, bf16[128,1,4096]{2,0,1:T(8,128)(2,1)}, u32[]{:S(2)}) copy-start(bf16[128,1,4096]{2,0,1:T(8,128)(2,1)} %param.13) | copy-start | bytes 3145732
  76.8 20.8 %copy-start.1 = (bf16[128,1,4096]{2,0,1:T(8,128)(2,1)S(1)}, bf16[128,1,4096]{2,0,1:T(8,128)(2,1)}, u32[]{:S(2)}) copy-start(bf16[128,1,4096]{2,0,1:T(8,128)(2,1)} %param.14) | copy-start | bytes 3145732
  77.8 0.7 copy-start.4
  78.5 18.2 %collective-permute-start.14 = (bf16[128,1024]{1,0:T(8,128)(2,1)}, bf16[128,1024]{1,0:T(8,128)(2,1)}, u32[]{:S(2)}, u32[]{:S(2)}) collective-permute-start(bf16[128,1024]{1,0:T(8,128)(2,1)} %get-tuple-element.48), channel_id=1, source_target_pairs={{0,6},{2,0},{4,2},{6,4},{1,7},{3,1},{5,3},{7,5},{8,14},{10,8},{12,... | collective-permute-start | bytes 786440 | tf_op jit(solution)/shard_map/ppermute | solution.py:506
  81.0 16.6 %collective-permute-start.15 = (bf16[128,1024]{1,0:T(8,128)(2,1)}, bf16[128,1024]{1,0:T(8,128)(2,1)}, u32[]{:S(2)}, u32[]{:S(2)}) collective-permute-start(bf16[128,1024]{1,0:T(8,128)(2,1)} %get-tuple-element.49), channel_id=1, source_target_pairs={{0,4},{2,6},{4,0},{6,2},{1,5},{3,7},{5,1},{7,3},{8,12},{10,14},{12... | collective-permute-start | bytes 786440 | tf_op jit(solution)/shard_map/ppermute | solution.py:506
  81.3 16.3 %collective-permute-start.16 = (bf16[128,1024]{1,0:T(8,128)(2,1)}, bf16[128,1024]{1,0:T(8,128)(2,1)}, u32[]{:S(2)}, u32[]{:S(2)}) collective-permute-start(bf16[128,1024]{1,0:T(8,128)(2,1)} %get-tuple-element.50), channel_id=1, source_target_pairs={{0,2},{2,4},{4,6},{6,0},{1,3},{3,5},{5,7},{7,1},{8,10},{10,12},{12... | collective-permute-start | bytes 786440 | tf_op jit(solution)/shard_map/ppermute | solution.py:506
  93.7 4.0 %copy-start.2 = (bf16[128,1,4096]{2,0,1:T(8,128)(2,1)S(1)}, bf16[128,1,4096]{2,0,1:T(8,128)(2,1)}, u32[]{:S(2)}) copy-start(bf16[128,1,4096]{2,0,1:T(8,128)(2,1)} %param.15) | copy-start | bytes 3145732
  93.7 4.0 %copy-start.5 = (bf16[128,1024]{1,0:T(8,128)(2,1)S(1)}, bf16[128,1024]{1,0:T(8,128)(2,1)}, u32[]{:S(2)}) copy-start(bf16[128,1024]{1,0:T(8,128)(2,1)} %copy-done.4) | copy-start | bytes 786436
  93.8 7.4 %collective-permute-start.10 = (bf16[2,40,128]{2,1,0:T(8,128)(2,1)S(1)}, bf16[2,40,128]{2,1,0:T(8,128)(2,1)S(1)}, u32[]{:S(2)}, u32[]{:S(2)}) collective-permute-start(bf16[2,40,128]{2,1,0:T(8,128)(2,1)S(1)} %get-tuple-element.41), channel_id=1, source_target_pairs={{0,6},{2,0},{4,2},{6,4},{1,7},{3,1},{5,3},{7,5},{8,14},{10,8},{12,... | collective-permute-start | bytes 61448 | tf_op jit(solution)/shard_map/ppermute | solution.py:506
  96.4 5.3 %collective-permute-start.11 = (bf16[2,40,128]{2,1,0:T(8,128)(2,1)S(1)}, bf16[2,40,128]{2,1,0:T(8,128)(2,1)S(1)}, u32[]{:S(2)}, u32[]{:S(2)}) collective-permute-start(bf16[2,40,128]{2,1,0:T(8,128)(2,1)S(1)} %get-tuple-element.42), channel_id=1, source_target_pairs={{0,4},{2,6},{4,0},{6,2},{1,5},{3,7},{5,1},{7,3},{8,12},{10,14},{12... | collective-permute-start | bytes 61448 | tf_op jit(solution)/shard_map/ppermute | solution.py:506
  96.7 5.2 %collective-permute-start.12 = (bf16[2,40,128]{2,1,0:T(8,128)(2,1)S(1)}, bf16[2,40,128]{2,1,0:T(8,128)(2,1)S(1)}, u32[]{:S(2)}, u32[]{:S(2)}) collective-permute-start(bf16[2,40,128]{2,1,0:T(8,128)(2,1)S(1)} %get-tuple-element.43), channel_id=1, source_target_pairs={{0,2},{2,4},{4,6},{6,0},{1,3},{3,5},{5,7},{7,1},{8,10},{10,12},{12... | collective-permute-start | bytes 61448 | tf_op jit(solution)/shard_map/ppermute | solution.py:506
  97.6 3.6 %copy-start.9 = (s32[2]{0:T(128)}, s32[2]{0:T(128)S(1)}, u32[]{:S(2)}) copy-start(s32[2]{0:T(128)S(1)} %pad_add_fusion.place_ref) | copy-start | bytes 28
  102.7 14.8 %all-to-all-start.3 = ((bf16[16,96,128]{2,1,0:T(8,128)(2,1)}), bf16[16,96,128]{2,1,0:T(8,128)(2,1)S(1)}, u32[]{:S(2)}, u32[]{:S(2)}) async-start(bf16[16,96,128]{2,1,0:T(8,128)(2,1)} %make_grad_pre.1), calls=%async_computation.3 | async-start | bytes 786432 | tf_op jit(solution)/shard_map/all_to_all | solution.py:511
  107.8 9.7 %copy-start.3 = (bf16[1,4096,128]{2,1,0:T(8,128)(2,1)S(1)}, bf16[1,4096,128]{2,1,0:T(8,128)(2,1)}, u32[]{:S(2)}) copy-start(bf16[1,4096,128]{2,1,0:T(8,128)(2,1)} %param.10) | copy-start | bytes 3145732

commit v6 on v5

--- a/solution.py
+++ b/solution.py
@@ -34,7 +34,8 @@
 def adam_step(weights, gradient, moment_one, moment_two):
     one_new = 0.9 * moment_one + 0.1 * gradient
     two_new = 0.999 * moment_two + 0.001 * gradient * gradient
-    stepped = weights - 0.05 * one_new / (jnp.sqrt(two_new) + 1e-08)
+    root = two_new * lax.rsqrt(two_new)
+    stepped = weights - 0.05 * one_new / (root + 1e-08)
     return (stepped, one_new, two_new)
 
 
@@ -449,7 +450,7 @@
         turned[:, half * HALF:(half + 1) * HALF] = grad_pre.T.astype(bf16)
     rms = jnp.sum(got[:, 2 * SHARD:], axis=0)
     row = jnp.sum(rms[:3], axis=0, keepdims=True) * (1.0 / LAYERS)
-    column = jnp.broadcast_to(row, (OWN, OWN)).T[:, :1]
+    column = 1.0 / jnp.broadcast_to(row, (OWN, OWN)).T[:, :1]
 
     @pl.loop(0, PARTS)
     def _(c):
@@ -463,7 +464,7 @@
         w_new[c] = (stepped * row).astype(bf16)
         m_new[c] = one.astype(bf16)
         v_new[c] = two.astype(bf16)
-        dec_new[c] = (dec[c] / column).astype(bf16)
+        dec_new[c] = (dec[c] * column).astype(bf16)
         for copy in stores(c):
             copy.start()
 

time: 127 us -> 127 us (level)
  no operation moved by 1% of the time
where the time goes in v6:
time: 127 us; the launch traced here: 126 us
  waiting for transfers between devices  46.7 us (37%)
  starting transfers between devices  38.3 us (30%)
  Pallas kernels  34.9 us (27%)
  local copies, waits for them, and re-layouts  5.21 us (4%)
    all_to_all x4, waiting for transfers between devices, exchange(): lax.all_to_all(flat, axes, split_axis=0, concat_axis=0, tiled=True)  28.7 us
    all_to_all x4, starting transfers between devices, exchange(): lax.all_to_all(flat, axes, split_axis=0, concat_axis=0, tiled=True)  22 us
    ppermute x12, waiting for transfers between devices, shift(): return lax.ppermute(array, 'x', [(i, (i + steps) % NX) for i in range(NX)])  16.4 us
    ppermute x12, starting transfers between devices, shift(): return lax.ppermute(array, 'x', [(i, (i + steps) % NX) for i in range(NX)])  15.8 us
    pallas_call x1, Pallas kernels, encoder_adam(): pl.pallas_call(encoder_kernel, in_specs=[held] * 4 + [anywhere] * 2, out_...  8.93 us
    pallas_call x1, Pallas kernels, residue_part(): pl.pallas_call(residue_kernel, in_specs=[anywhere] * (2 + 2 * NX), out_sp...  7.88 us
    pallas_call x1, Pallas kernels, preact_share(): pl.pallas_call(preact_kernel, in_specs=[anywhere] * 3, out_specs=[pl.Bloc...  6.99 us
    unnamed x46, local copies, waits for them, and re-layouts  5.2 us
  transfers between devices with their start and end apart: 21, of which 13 were waited for; matrix products, arithmetic and copies ran while one was open for 0% of the time, Pallas kernels for 7%

profile of v6, /device:TPU:0, one launch (start us, length us, event | category | flops | bytes accessed | tf_op | source)
XLA Modules:
  0.0 126.3 jit_solution(7882366334834105389)
XLA Ops:
  0.6 7.0 %preact_share.1 = (bf16[16,2,40,128]{3,2,1,0:T(8,128)(2,1)}, bf16[128,1024]{1,0:T(8,128)(2,1)}, bf16[128,1024]{1,0:T(8,128)(2,1)}, bf16[128,1024]{1,0:T(8,128)(2...) custom-call(bf16[1280,4096]{1,0:T(8,128)(2,1)} %bitcast.37, bf16[4096,128]{1,0:T(8,128)(2,1)} %bitcast.34, ...), custom_call_target="tpu_custom_call" | custom-call | flops 1342177280 | bytes 10485760 | tf_op jit(solution)/shard_map/preact_share/pallas_call | solution.py:113
  7.6 8.1 %all-to-all-start = ((bf16[16,80,128]{2,1,0:T(8,128)(2,1)}), bf16[16,80,128]{2,1,0:T(8,128)(2,1)S(1)}, u32[]{:S(2)}, u32[]{:S(2)}) async-start(bf16[16,80,128]{2,1,0:T(8,128)(2,1)} %bitcast.44), calls=%async_computation | async-start | bytes 655360 | tf_op jit(solution)/shard_map/all_to_all | solution.py:512
  15.9 9.2 %all-to-all-done = bf16[16,80,128]{2,1,0:T(8,128)(2,1)S(1)} async-done(((bf16[16,80,128]{2,1,0:T(8,128)(2,1)}), bf16[16,80,128]{2,1,0:T(8,128)(2,1)S(1)}, u32[]{:S(2)}, u32[]{:S(2)}) %all-to-all-start) | async-done | bytes 327712 | tf_op jit(solution)/shard_map/all_to_all | solution.py:512
  25.1 0.1 make_codes.1
  25.1 2.8 %collective-permute-start.2 = (bf16[2,40,128]{2,1,0:T(8,128)(2,1)S(1)}, bf16[2,40,128]{2,1,0:T(8,128)(2,1)S(1)}, u32[]{:S(2)}, u32[]{:S(2)}) collective-permute-start(bf16[2,40,128]{2,1,0:T(8,128)(2,1)S(1)} %get-tuple-element.33.refs_0_), channel_id=1, source_target_pairs={{0,6},{2,0},{4,2},{6,4},{1,7},{3,1},{5,3},{7,5},{8,14},{10,8},{12,... | collective-permute-start | bytes 61448 | tf_op jit(solution)/shard_map/ppermute | solution.py:507
  28.0 0.8 collective-permute-start.1
  28.8 0.9 collective-permute-start
  29.6 3.6 %collective-permute-done.1.refs_2_ = bf16[2,40,128]{2,1,0:T(8,128)(2,1)S(1)} collective-permute-done((bf16[2,40,128]{2,1,0:T(8,128)(2,1)S(1)}, bf16[2,40,128]{2,1,0:T(8,128)(2,1)S(1)}, u32[]{:S(2)}, u32[]{:S(2)}) %collective-permute-start.1) | collective-permute-done | bytes 20512 | tf_op jit(solution)/shard_map/ppermute | solution.py:507
  33.2 0.5 collective-permute-done.refs_1_
  33.7 1.3 %spread_codes.1 = bf16[2,16,160,128]{3,2,1,0:T(8,128)(2,1)} custom-call(bf16[2,40,128]{2,1,0:T(8,128)(2,1)S(1)} %get-tuple-element.33.refs_0_, bf16[2,40,128]{2,1,0:T(8,128)(2,1)S(1)} %collective-permute-done.refs_1_, bf16[2,40,128]{2,1,0:T(8,128)(2,1)S(1)} %collective-permute-done.1.refs_2_, bf16[2,40,128]{2,1,0:T(8,128)(2,1)S(1)} %collective-permute-done.2.refs_3_), custom_call_target="tpu_custom_call" | custom-call | flops 1000000 | bytes 2000000 | tf_op jit(solution)/shard_map/spread_codes/pallas_call | solution.py:167
  35.0 4.1 %all-to-all-start.1 = ((bf16[32,160,128]{2,1,0:T(8,128)(2,1)}), bf16[32,160,128]{2,1,0:T(8,128)(2,1)S(1)}, u32[]{:S(2)}, u32[]{:S(2)}) async-start(bf16[32,160,128]{2,1,0:T(8,128)(2,1)} %bitcast.7), calls=%async_computation.1 | async-start | bytes 2621440 | tf_op jit(solution)/shard_map/all_to_all | solution.py:512
  39.2 0.1 collective-permute-start.3
  39.3 1.8 %collective-permute-start.4 = (bf16[128,1024]{1,0:T(8,128)(2,1)S(1)}, bf16[128,1024]{1,0:T(8,128)(2,1)S(1)}, u32[]{:S(2)}, u32[]{:S(2)}) collective-permute-start(bf16[128,1024]{1,0:T(8,128)(2,1)S(1)} %copy-done.14), channel_id=1, source_target_pairs={{0,4},{2,6},{4,0},{6,2},{1,5},{3,7},{5,1},{7,3},{8,12},{10,14},{12... | collective-permute-start | bytes 786440 | tf_op jit(solution)/shard_map/ppermute | solution.py:507
  41.0 2.4 %collective-permute-start.5 = (bf16[128,1024]{1,0:T(8,128)(2,1)S(1)}, bf16[128,1024]{1,0:T(8,128)(2,1)S(1)}, u32[]{:S(2)}, u32[]{:S(2)}) collective-permute-start(bf16[128,1024]{1,0:T(8,128)(2,1)S(1)} %copy-done.13), channel_id=1, source_target_pairs={{0,6},{2,0},{4,2},{6,4},{1,7},{3,1},{5,3},{7,5},{8,14},{10,8},{12,... | collective-permute-start | bytes 786440 | tf_op jit(solution)/shard_map/ppermute | solution.py:507
  43.4 11.2 %collective-permute-done.3.rest_1_ = bf16[128,1024]{1,0:T(8,128)(2,1)S(1)} collective-permute-done((bf16[128,1024]{1,0:T(8,128)(2,1)S(1)}, bf16[128,1024]{1,0:T(8,128)(2,1)S(1)}, u32[]{:S(2)}, u32[]{:S(2)}) %collective-permute-start.3) | collective-permute-done | bytes 262176 | tf_op jit(solution)/shard_map/ppermute | solution.py:507
  54.6 0.0 copy-start.17
  54.6 0.5 collective-permute-start.8
  55.1 0.1 collective-permute-done.5.rest_3_
  55.2 0.9 collective-permute-done.7.rest_5_
  56.1 0.4 collective-permute-done.8.rest_6_
  56.5 0.4 collective-permute-done.9.rest_7_
  56.8 2.6 %all-to-all-done.1 = bf16[32,160,128]{2,1,0:T(8,128)(2,1)S(1)} async-done(((bf16[32,160,128]{2,1,0:T(8,128)(2,1)}), bf16[32,160,128]{2,1,0:T(8,128)(2,1)S(1)}, u32[]{:S(2)}, u32[]{:S(2)}) %all-to-all-start.1) | async-done | bytes 1310752 | tf_op jit(solution)/shard_map/all_to_all | solution.py:512
  59.5 1.0 copy-done.10
  60.5 7.9 %residue_part.1 = (bf16[2,16,160,128]{3,2,1,0:T(8,128)(2,1)}, bf16[4,128,1024]{2,1,0:T(8,128)(2,1)}, bf16[4,128,1024]{2,1,0:T(8,128)(2,1)}) custom-call(bf16[2,16,160,128]{3,2,1,0:T(8,128)(2,1)} %bitcast.39, bf16[640,1024]{1,0:T(8,128)(2,1)} %get-tuple-element.34.acts_ref, bf16[128,1024]{1,0:T(8,128)(2,1)} %get-tuple-element.35.rest_0_, ...), custom_call_target="tpu_custom_call" | custom-call | flops 4026531840 | bytes 10000000 | tf_op jit(solution)/shard_map/residue_part/pallas_call | solution.py:234
  68.4 0.1 collective-permute-start.13
  68.5 4.9 %all-to-all-start.2 = ((bf16[32,160,128]{2,1,0:T(8,128)(2,1)}), bf16[32,160,128]{2,1,0:T(8,128)(2,1)S(1)}, u32[]{:S(2)}, u32[]{:S(2)}) async-start(bf16[32,160,128]{2,1,0:T(8,128)(2,1)} %bitcast.40), calls=%async_computation.2 | async-start | bytes 2621440 | tf_op jit(solution)/shard_map/all_to_all | solution.py:512
  73.4 1.0 copy-done.7
  74.4 1.2 copy-done.6
  75.6 1.2 copy-done.8
  76.8 1.0 join_halves.1
  77.8 0.7 copy-done.4
  78.5 2.5 %collective-permute-start.14 = (bf16[128,1024]{1,0:T(8,128)(2,1)}, bf16[128,1024]{1,0:T(8,128)(2,1)}, u32[]{:S(2)}, u32[]{:S(2)}) collective-permute-start(bf16[128,1024]{1,0:T(8,128)(2,1)} %get-tuple-element.48), channel_id=1, source_target_pairs={{0,6},{2,0},{4,2},{6,4},{1,7},{3,1},{5,3},{7,5},{8,14},{10,8},{12,... | collective-permute-start | bytes 786440 | tf_op jit(solution)/shard_map/ppermute | solution.py:507
  81.0 0.3 collective-permute-start.15
  81.3 0.6 collective-permute-start.16
  81.9 11.8 %all-to-all-done.2 = bf16[32,160,128]{2,1,0:T(8,128)(2,1)S(1)} async-done(((bf16[32,160,128]{2,1,0:T(8,128)(2,1)}), bf16[32,160,128]{2,1,0:T(8,128)(2,1)S(1)}, u32[]{:S(2)}, u32[]{:S(2)}) %all-to-all-start.2) | async-done | bytes 1310752 | tf_op jit(solution)/shard_map/all_to_all | solution.py:512
  93.7 0.2 sum_layers.1
  93.8 2.6 %collective-permute-start.10 = (bf16[2,40,128]{2,1,0:T(8,128)(2,1)S(1)}, bf16[2,40,128]{2,1,0:T(8,128)(2,1)S(1)}, u32[]{:S(2)}, u32[]{:S(2)}) collective-permute-start(bf16[2,40,128]{2,1,0:T(8,128)(2,1)S(1)} %get-tuple-element.41), channel_id=1, source_target_pairs={{0,6},{2,0},{4,2},{6,4},{1,7},{3,1},{5,3},{7,5},{8,14},{10,8},{12,... | collective-permute-start | bytes 61448 | tf_op jit(solution)/shard_map/ppermute | solution.py:507
  96.4 0.3 collective-permute-start.11
  96.7 0.8 collective-permute-start.12
  97.5 0.1 pad_add_fusion.place_ref
  97.7 3.3 %decoder_size.1.rms_ref = f32[8,128]{1,0:T(8,128)S(1)} custom-call(s32[2]{0:T(128)S(1)} %pad_add_fusion.place_ref, bf16[128,1024]{1,0:T(8,128)(2,1)S(1)} %copy-done.5, bf16[128,1024]{1,0:T(8,128)(2,1)} %collective-permute-done.14.refs_1_, bf16[128,1024]{1,0:T(8,128)(2,1)} %collective-permute-done.15.refs_2_, ...), custom_call_target="tpu_custom_call" | custom-call | flops 10485760 | bytes 4000000 | tf_op jit(solution)/shard_map/decoder_size/pallas_call | solution.py:315
  101.0 0.8 collective-permute-done.11.two_ref
  101.7 0.2 collective-permute-done.12.three_ref
  101.9 0.8 make_grad_pre.1
  102.7 4.8 %all-to-all-start.3 = ((bf16[16,96,128]{2,1,0:T(8,128)(2,1)}), bf16[16,96,128]{2,1,0:T(8,128)(2,1)S(1)}, u32[]{:S(2)}, u32[]{:S(2)}) async-start(bf16[16,96,128]{2,1,0:T(8,128)(2,1)} %make_grad_pre.1), calls=%async_computation.3 | async-start | bytes 786432 | tf_op jit(solution)/shard_map/all_to_all | solution.py:512
  107.5 4.5 %decoder_adam.1 = (bf16[128,4096]{1,0:T(8,128)(2,1)}, bf16[128,4096]{1,0:T(8,128)(2,1)}, f32[128,4096]{1,0:T(8,128)}) custom-call(s32[2]{0:T(128)} %copy-done.9, bf16[128,1024]{1,0:T(8,128)(2,1)} %copy-done.4, bf16[128,1024]{1,0:T(8,128)(2,1)} %collective-permute-done.14.refs_1_, bf16[128,1024]{1,0:T(8,128)(2,1)} %collective-permute-done.15.refs_2_, ...), custom_call_target="tpu_custom_call" | custom-call | flops 10485760 | bytes 8000000 | tf_op jit(solution)/shard_map/decoder_adam/pallas_call | solution.py:347
  112.0 5.1 %all-to-all-done.3.got_ref = bf16[16,96,128]{2,1,0:T(8,128)(2,1)S(1)} async-done(((bf16[16,96,128]{2,1,0:T(8,128)(2,1)}), bf16[16,96,128]{2,1,0:T(8,128)(2,1)S(1)}, u32[]{:S(2)}, u32[]{:S(2)}) %all-to-all-start.3) | async-done | bytes 393248 | tf_op jit(solution)/shard_map/all_to_all | solution.py:512
  117.2 8.9 %encoder_adam.1 = (bf16[4096,128]{1,0:T(8,128)(2,1)}, bf16[4096,128]{1,0:T(8,128)(2,1)}, bf16[4096,128]{1,0:T(8,128)(2,1)}, bf16[128,4096]{1,0:T(8,128)(2,1)}) custom-call(bf16[16,96,128]{2,1,0:T(8,128)(2,1)S(1)} %all-to-all-done.3.got_ref, bf16[4096,128]{1,0:T(8,128)(2,1)S(1)} %bitcast.35, bf16[4096,128]{1,0:T(8,128)(2,1)} %bitcast.41, ...), custom_call_target="tpu_custom_call" | custom-call | flops 1342177280 | bytes 20000000 | tf_op jit(solution)/shard_map/encoder_adam/pallas_call | solution.py:480
  (53 shorter events, 0.2 us)
Async XLA Ops:
  0.6 15.2 %copy-start.11 = (s32[1280,128]{1,0:T(8,128)S(1)}, s32[1280,128]{1,0:T(8,128)}, u32[]{:S(2)}) copy-start(s32[1280,128]{1,0:T(8,128)} %param.9) | copy-start | bytes 1966084
  7.6 17.4 %all-to-all-start = ((bf16[16,80,128]{2,1,0:T(8,128)(2,1)}), bf16[16,80,128]{2,1,0:T(8,128)(2,1)S(1)}, u32[]{:S(2)}, u32[]{:S(2)}) async-start(bf16[16,80,128]{2,1,0:T(8,128)(2,1)} %bitcast.44), calls=%async_computation | async-start | bytes 655360 | tf_op jit(solution)/shard_map/all_to_all | solution.py:512
  25.1 4.5 %collective-permute-start.2 = (bf16[2,40,128]{2,1,0:T(8,128)(2,1)S(1)}, bf16[2,40,128]{2,1,0:T(8,128)(2,1)S(1)}, u32[]{:S(2)}, u32[]{:S(2)}) collective-permute-start(bf16[2,40,128]{2,1,0:T(8,128)(2,1)S(1)} %get-tuple-element.33.refs_0_), channel_id=1, source_target_pairs={{0,6},{2,0},{4,2},{6,4},{1,7},{3,1},{5,3},{7,5},{8,14},{10,8},{12,... | collective-permute-start | bytes 61448 | tf_op jit(solution)/shard_map/ppermute | solution.py:507
  28.0 5.3 %collective-permute-start.1 = (bf16[2,40,128]{2,1,0:T(8,128)(2,1)S(1)}, bf16[2,40,128]{2,1,0:T(8,128)(2,1)S(1)}, u32[]{:S(2)}, u32[]{:S(2)}) collective-permute-start(bf16[2,40,128]{2,1,0:T(8,128)(2,1)S(1)} %get-tuple-element.33.refs_0_), channel_id=1, source_target_pairs={{0,4},{2,6},{4,0},{6,2},{1,5},{3,7},{5,1},{7,3},{8,12},{10,14},{12... | collective-permute-start | bytes 61448 | tf_op jit(solution)/shard_map/ppermute | solution.py:507
  28.8 5.0 %collective-permute-start = (bf16[2,40,128]{2,1,0:T(8,128)(2,1)S(1)}, bf16[2,40,128]{2,1,0:T(8,128)(2,1)S(1)}, u32[]{:S(2)}, u32[]{:S(2)}) collective-permute-start(bf16[2,40,128]{2,1,0:T(8,128)(2,1)S(1)} %get-tuple-element.33.refs_0_), channel_id=1, source_target_pairs={{0,2},{2,4},{4,6},{6,0},{1,3},{3,5},{5,7},{7,1},{8,10},{10,12},{12... | collective-permute-start | bytes 61448 | tf_op jit(solution)/shard_map/ppermute | solution.py:507
  35.0 4.1 %copy-start.15 = (bf16[128,1024]{1,0:T(8,128)(2,1)S(1)}, bf16[128,1024]{1,0:T(8,128)(2,1)}, u32[]{:S(2)}) copy-start(bf16[128,1024]{1,0:T(8,128)(2,1)} %get-tuple-element.36) | copy-start | bytes 786436
  35.0 4.2 %copy-start.14 = (bf16[128,1024]{1,0:T(8,128)(2,1)S(1)}, bf16[128,1024]{1,0:T(8,128)(2,1)}, u32[]{:S(2)}) copy-start(bf16[128,1024]{1,0:T(8,128)(2,1)} %get-tuple-element.37) | copy-start | bytes 786436
  35.0 6.0 %copy-start.13 = (bf16[128,1024]{1,0:T(8,128)(2,1)S(1)}, bf16[128,1024]{1,0:T(8,128)(2,1)}, u32[]{:S(2)}) copy-start(bf16[128,1024]{1,0:T(8,128)(2,1)} %get-tuple-element.38) | copy-start | bytes 786436
  35.0 8.4 %copy-start.12 = (bf16[128,1024]{1,0:T(8,128)(2,1)S(1)}, bf16[128,1024]{1,0:T(8,128)(2,1)}, u32[]{:S(2)}) copy-start(bf16[128,1024]{1,0:T(8,128)(2,1)} %get-tuple-element.35.rest_0_) | copy-start | bytes 786436
  35.0 24.4 %all-to-all-start.1 = ((bf16[32,160,128]{2,1,0:T(8,128)(2,1)}), bf16[32,160,128]{2,1,0:T(8,128)(2,1)S(1)}, u32[]{:S(2)}, u32[]{:S(2)}) async-start(bf16[32,160,128]{2,1,0:T(8,128)(2,1)} %bitcast.7), calls=%async_computation.1 | async-start | bytes 2621440 | tf_op jit(solution)/shard_map/all_to_all | solution.py:512
  39.2 15.4 %collective-permute-start.3 = (bf16[128,1024]{1,0:T(8,128)(2,1)S(1)}, bf16[128,1024]{1,0:T(8,128)(2,1)S(1)}, u32[]{:S(2)}, u32[]{:S(2)}) collective-permute-start(bf16[128,1024]{1,0:T(8,128)(2,1)S(1)} %copy-done.15), channel_id=1, source_target_pairs={{0,2},{2,4},{4,6},{6,0},{1,3},{3,5},{5,7},{7,1},{8,10},{10,12},{12... | collective-permute-start | bytes 786440 | tf_op jit(solution)/shard_map/ppermute | solution.py:507
  39.3 15.3 %collective-permute-start.4 = (bf16[128,1024]{1,0:T(8,128)(2,1)S(1)}, bf16[128,1024]{1,0:T(8,128)(2,1)S(1)}, u32[]{:S(2)}, u32[]{:S(2)}) collective-permute-start(bf16[128,1024]{1,0:T(8,128)(2,1)S(1)} %copy-done.14), channel_id=1, source_target_pairs={{0,4},{2,6},{4,0},{6,2},{1,5},{3,7},{5,1},{7,3},{8,12},{10,14},{12... | collective-permute-start | bytes 786440 | tf_op jit(solution)/shard_map/ppermute | solution.py:507
  41.0 14.2 %collective-permute-start.5 = (bf16[128,1024]{1,0:T(8,128)(2,1)S(1)}, bf16[128,1024]{1,0:T(8,128)(2,1)S(1)}, u32[]{:S(2)}, u32[]{:S(2)}) collective-permute-start(bf16[128,1024]{1,0:T(8,128)(2,1)S(1)} %copy-done.13), channel_id=1, source_target_pairs={{0,6},{2,0},{4,2},{6,4},{1,7},{3,1},{5,3},{7,5},{8,14},{10,8},{12,... | collective-permute-start | bytes 786440 | tf_op jit(solution)/shard_map/ppermute | solution.py:507
  43.4 11.8 %collective-permute-start.6 = (bf16[128,1024]{1,0:T(8,128)(2,1)S(1)}, bf16[128,1024]{1,0:T(8,128)(2,1)S(1)}, u32[]{:S(2)}, u32[]{:S(2)}) collective-permute-start(bf16[128,1024]{1,0:T(8,128)(2,1)S(1)} %copy-done.12), channel_id=1, source_target_pairs={{0,1},{1,0},{2,3},{3,2},{4,5},{5,4},{6,7},{7,6},{8,9},{9,8},{10,11... | collective-permute-start | bytes 786440 | tf_op jit(solution)/shard_map/ppermute | solution.py:503
  54.6 4.9 %copy-start.16 = (bf16[128,1024]{1,0:T(8,128)(2,1)}, bf16[128,1024]{1,0:T(8,128)(2,1)S(1)}, u32[]{:S(2)}) copy-start(bf16[128,1024]{1,0:T(8,128)(2,1)S(1)} %collective-permute-done.3.rest_1_) | copy-start | bytes 786436
  54.6 1.5 %collective-permute-start.7 = (bf16[128,1024]{1,0:T(8,128)(2,1)S(1)}, bf16[128,1024]{1,0:T(8,128)(2,1)S(1)}, u32[]{:S(2)}, u32[]{:S(2)}) collective-permute-start(bf16[128,1024]{1,0:T(8,128)(2,1)S(1)} %collective-permute-done.3.rest_1_), channel_id=1, source_target_pairs={{0,1},{1,0},{2,3},{3,2},{4,5},{5,4},{6,7},{7,6},{8,9},{9,8},{10,11... | collective-permute-start | bytes 786440 | tf_op jit(solution)/shard_map/ppermute | solution.py:503
  54.6 4.9 %copy-start.17 = (bf16[128,1024]{1,0:T(8,128)(2,1)}, bf16[128,1024]{1,0:T(8,128)(2,1)S(1)}, u32[]{:S(2)}) copy-start(bf16[128,1024]{1,0:T(8,128)(2,1)S(1)} %collective-permute-done.4.rest_2_) | copy-start | bytes 786436
  54.6 1.9 %collective-permute-start.8 = (bf16[128,1024]{1,0:T(8,128)(2,1)S(1)}, bf16[128,1024]{1,0:T(8,128)(2,1)S(1)}, u32[]{:S(2)}, u32[]{:S(2)}) collective-permute-start(bf16[128,1024]{1,0:T(8,128)(2,1)S(1)} %collective-permute-done.4.rest_2_), channel_id=1, source_target_pairs={{0,1},{1,0},{2,3},{3,2},{4,5},{5,4},{6,7},{7,6},{8,9},{9,8},{10,11... | collective-permute-start | bytes 786440 | tf_op jit(solution)/shard_map/ppermute | solution.py:503
  55.2 4.2 %copy-start.18 = (bf16[128,1024]{1,0:T(8,128)(2,1)}, bf16[128,1024]{1,0:T(8,128)(2,1)S(1)}, u32[]{:S(2)}) copy-start(bf16[128,1024]{1,0:T(8,128)(2,1)S(1)} %collective-permute-done.5.rest_3_) | copy-start | bytes 786436
  55.2 1.7 %collective-permute-start.9 = (bf16[128,1024]{1,0:T(8,128)(2,1)S(1)}, bf16[128,1024]{1,0:T(8,128)(2,1)S(1)}, u32[]{:S(2)}, u32[]{:S(2)}) collective-permute-start(bf16[128,1024]{1,0:T(8,128)(2,1)S(1)} %collective-permute-done.5.rest_3_), channel_id=1, source_target_pairs={{0,1},{1,0},{2,3},{3,2},{4,5},{5,4},{6,7},{7,6},{8,9},{9,8},{10,11... | collective-permute-start | bytes 786440 | tf_op jit(solution)/shard_map/ppermute | solution.py:503
  55.2 4.2 %copy-start.19 = (bf16[128,1024]{1,0:T(8,128)(2,1)}, bf16[128,1024]{1,0:T(8,128)(2,1)S(1)}, u32[]{:S(2)}) copy-start(bf16[128,1024]{1,0:T(8,128)(2,1)S(1)} %collective-permute-done.6.rest_4_) | copy-start | bytes 786436
  56.1 3.3 %copy-start.20 = (bf16[128,1024]{1,0:T(8,128)(2,1)}, bf16[128,1024]{1,0:T(8,128)(2,1)S(1)}, u32[]{:S(2)}) copy-start(bf16[128,1024]{1,0:T(8,128)(2,1)S(1)} %collective-permute-done.7.rest_5_) | copy-start | bytes 786436
  56.5 3.0 %copy-start.21 = (bf16[128,1024]{1,0:T(8,128)(2,1)}, bf16[128,1024]{1,0:T(8,128)(2,1)S(1)}, u32[]{:S(2)}) copy-start(bf16[128,1024]{1,0:T(8,128)(2,1)S(1)} %collective-permute-done.8.rest_6_) | copy-start | bytes 786436
  56.8 2.6 %copy-start.22 = (bf16[128,1024]{1,0:T(8,128)(2,1)}, bf16[128,1024]{1,0:T(8,128)(2,1)S(1)}, u32[]{:S(2)}) copy-start(bf16[128,1024]{1,0:T(8,128)(2,1)S(1)} %collective-permute-done.9.rest_7_) | copy-start | bytes 786436
  59.4 1.1 copy-start.10
  68.4 5.0 %collective-permute-start.13 = (bf16[4,128,1024]{2,1,0:T(8,128)(2,1)}, bf16[4,128,1024]{2,1,0:T(8,128)(2,1)S(1)}, u32[]{:S(2)}, u32[]{:S(2)}) collective-permute-start(bf16[4,128,1024]{2,1,0:T(8,128)(2,1)} %get-tuple-element.46), channel_id=1, source_target_pairs={{0,1},{1,0},{2,3},{3,2},{4,5},{5,4},{6,7},{7,6},{8,9},{9,8},{10,11... | collective-permute-start | bytes 3145736 | tf_op jit(solution)/shard_map/ppermute | solution.py:503
  68.5 25.2 %all-to-all-start.2 = ((bf16[32,160,128]{2,1,0:T(8,128)(2,1)}), bf16[32,160,128]{2,1,0:T(8,128)(2,1)S(1)}, u32[]{:S(2)}, u32[]{:S(2)}) async-start(bf16[32,160,128]{2,1,0:T(8,128)(2,1)} %bitcast.40), calls=%async_computation.2 | async-start | bytes 2621440 | tf_op jit(solution)/shard_map/all_to_all | solution.py:512
  73.4 1.0 copy-start.7
  74.4 1.2 copy-start.6
  75.6 1.2 copy-start.8
  76.8 20.8 %copy-start = (bf16[128,1,4096]{2,0,1:T(8,128)(2,1)S(1)}, bf16[128,1,4096]{2,0,1:T(8,128)(2,1)}, u32[]{:S(2)}) copy-start(bf16[128,1,4096]{2,0,1:T(8,128)(2,1)} %param.13) | copy-start | bytes 3145732
  76.8 20.8 %copy-start.1 = (bf16[128,1,4096]{2,0,1:T(8,128)(2,1)S(1)}, bf16[128,1,4096]{2,0,1:T(8,128)(2,1)}, u32[]{:S(2)}) copy-start(bf16[128,1,4096]{2,0,1:T(8,128)(2,1)} %param.14) | copy-start | bytes 3145732
  77.8 0.7 copy-start.4
  78.5 18.2 %collective-permute-start.14 = (bf16[128,1024]{1,0:T(8,128)(2,1)}, bf16[128,1024]{1,0:T(8,128)(2,1)}, u32[]{:S(2)}, u32[]{:S(2)}) collective-permute-start(bf16[128,1024]{1,0:T(8,128)(2,1)} %get-tuple-element.48), channel_id=1, source_target_pairs={{0,6},{2,0},{4,2},{6,4},{1,7},{3,1},{5,3},{7,5},{8,14},{10,8},{12,... | collective-permute-start | bytes 786440 | tf_op jit(solution)/shard_map/ppermute | solution.py:507
  81.0 16.6 %collective-permute-start.15 = (bf16[128,1024]{1,0:T(8,128)(2,1)}, bf16[128,1024]{1,0:T(8,128)(2,1)}, u32[]{:S(2)}, u32[]{:S(2)}) collective-permute-start(bf16[128,1024]{1,0:T(8,128)(2,1)} %get-tuple-element.49), channel_id=1, source_target_pairs={{0,4},{2,6},{4,0},{6,2},{1,5},{3,7},{5,1},{7,3},{8,12},{10,14},{12... | collective-permute-start | bytes 786440 | tf_op jit(solution)/shard_map/ppermute | solution.py:507
  81.3 16.3 %collective-permute-start.16 = (bf16[128,1024]{1,0:T(8,128)(2,1)}, bf16[128,1024]{1,0:T(8,128)(2,1)}, u32[]{:S(2)}, u32[]{:S(2)}) collective-permute-start(bf16[128,1024]{1,0:T(8,128)(2,1)} %get-tuple-element.50), channel_id=1, source_target_pairs={{0,2},{2,4},{4,6},{6,0},{1,3},{3,5},{5,7},{7,1},{8,10},{10,12},{12... | collective-permute-start | bytes 786440 | tf_op jit(solution)/shard_map/ppermute | solution.py:507
  93.7 4.0 %copy-start.2 = (bf16[128,1,4096]{2,0,1:T(8,128)(2,1)S(1)}, bf16[128,1,4096]{2,0,1:T(8,128)(2,1)}, u32[]{:S(2)}) copy-start(bf16[128,1,4096]{2,0,1:T(8,128)(2,1)} %param.15) | copy-start | bytes 3145732
  93.7 4.0 %copy-start.5 = (bf16[128,1024]{1,0:T(8,128)(2,1)S(1)}, bf16[128,1024]{1,0:T(8,128)(2,1)}, u32[]{:S(2)}) copy-start(bf16[128,1024]{1,0:T(8,128)(2,1)} %copy-done.4) | copy-start | bytes 786436
  93.8 7.1 %collective-permute-start.10 = (bf16[2,40,128]{2,1,0:T(8,128)(2,1)S(1)}, bf16[2,40,128]{2,1,0:T(8,128)(2,1)S(1)}, u32[]{:S(2)}, u32[]{:S(2)}) collective-permute-start(bf16[2,40,128]{2,1,0:T(8,128)(2,1)S(1)} %get-tuple-element.41), channel_id=1, source_target_pairs={{0,6},{2,0},{4,2},{6,4},{1,7},{3,1},{5,3},{7,5},{8,14},{10,8},{12,... | collective-permute-start | bytes 61448 | tf_op jit(solution)/shard_map/ppermute | solution.py:507
  96.4 5.3 %collective-permute-start.11 = (bf16[2,40,128]{2,1,0:T(8,128)(2,1)S(1)}, bf16[2,40,128]{2,1,0:T(8,128)(2,1)S(1)}, u32[]{:S(2)}, u32[]{:S(2)}) collective-permute-start(bf16[2,40,128]{2,1,0:T(8,128)(2,1)S(1)} %get-tuple-element.42), channel_id=1, source_target_pairs={{0,4},{2,6},{4,0},{6,2},{1,5},{3,7},{5,1},{7,3},{8,12},{10,14},{12... | collective-permute-start | bytes 61448 | tf_op jit(solution)/shard_map/ppermute | solution.py:507
  96.7 5.2 %collective-permute-start.12 = (bf16[2,40,128]{2,1,0:T(8,128)(2,1)S(1)}, bf16[2,40,128]{2,1,0:T(8,128)(2,1)S(1)}, u32[]{:S(2)}, u32[]{:S(2)}) collective-permute-start(bf16[2,40,128]{2,1,0:T(8,128)(2,1)S(1)} %get-tuple-element.43), channel_id=1, source_target_pairs={{0,2},{2,4},{4,6},{6,0},{1,3},{3,5},{5,7},{7,1},{8,10},{10,12},{12... | collective-permute-start | bytes 61448 | tf_op jit(solution)/shard_map/ppermute | solution.py:507
  97.6 3.3 %copy-start.9 = (s32[2]{0:T(128)}, s32[2]{0:T(128)S(1)}, u32[]{:S(2)}) copy-start(s32[2]{0:T(128)S(1)} %pad_add_fusion.place_ref) | copy-start | bytes 28
  102.7 14.5 %all-to-all-start.3 = ((bf16[16,96,128]{2,1,0:T(8,128)(2,1)}), bf16[16,96,128]{2,1,0:T(8,128)(2,1)S(1)}, u32[]{:S(2)}, u32[]{:S(2)}) async-start(bf16[16,96,128]{2,1,0:T(8,128)(2,1)} %make_grad_pre.1), calls=%async_computation.3 | async-start | bytes 786432 | tf_op jit(solution)/shard_map/all_to_all | solution.py:512
  107.5 9.7 %copy-start.3 = (bf16[1,4096,128]{2,1,0:T(8,128)(2,1)S(1)}, bf16[1,4096,128]{2,1,0:T(8,128)(2,1)}, u32[]{:S(2)}) copy-start(bf16[1,4096,128]{2,1,0:T(8,128)(2,1)} %param.10) | copy-start | bytes 3145732
